TPU v7x, 256 devices: a whole 4x4x8 slice. The times are simulated.
256 devices in a mesh: aux: 32 (over z_hi, x, core), row: 8 (over z_lo, y).
Axes of the slice: x: 4, y: 4, z: 8 (z_hi: 4, z_lo: 2; z = z_hi * 2 + z_lo), core: 2. Of those that a mesh axis runs over, the one named last changes fastest.
Arguments:
- integrals: bfloat16 [128, 1024, 8000], P('aux', 'row'), may hold values from -0.71875 to 0.71875
- block_mask: int32 [32, 16, 16], P('aux', 'row'), may hold values 0 or 1
- coefficients: bfloat16 [8000, 256], P('aux'), may hold values from -0.0625 to 0.0625
- occ_index: int32 [64], replicated, may hold values from 0 to 255
Outputs:
- exchange: float32 [1024, 384], P(('row', 'aux'))
All inputs are finite; a program needn't handle non-finite values. No bound on the sum of `block_mask` on one device may be relied on, other than what follows from the above.
Results may differ from a plain program's by a relative error of at most 0.0011.
Values may be sent and summed in bfloat16 or wider, within the bound.
No kernel may reach another device: no remote copies, remote signals or barrier semaphores. Data moves between devices by JAX's collectives and lax.ppermute only.
A program may use at most 128 MiB of HBM per device.

v0:
```python
import jax
import jax.numpy as jnp
from jax import lax
from jax.sharding import PartitionSpec as P

COL_BLK = 500
BANDS = 3
ROW_BLK = 64


def from_behind(block, axis, distance):
    devices = range(lax.axis_size(axis))
    route = [((i - distance) % len(devices), i) for i in devices]
    return lax.ppermute(block, axis, route)


def per_device(integrals, block_mask, coefficients, occ_index):
    p_local, r_local, basis = integrals.shape
    occ_all = coefficients.shape[1]
    occ_batch = occ_index.shape[0]
    picker = (jnp.arange(occ_all, dtype=jnp.int32)[:, None] == occ_index[None, :]).astype(
        jnp.bfloat16
    )
    rows_mask = jnp.repeat(jnp.repeat(block_mask[0], ROW_BLK, axis=0), COL_BLK, axis=1).astype(
        jnp.bfloat16
    )
    screened = (integrals * rows_mask[None, :, :]).reshape(p_local * r_local, basis)
    picked = jnp.dot(
        lax.all_gather(coefficients, "aux", axis=0, tiled=True),
        picker,
        preferred_element_type=jnp.float32,
    ).astype(jnp.bfloat16)
    accum = jnp.dot(screened, picked, preferred_element_type=jnp.float32)
    half = accum.astype(jnp.bfloat16).reshape(p_local, r_local, occ_batch)
    previous = from_behind(half, "row", 1)
    farther = from_behind(previous, "row", 1)
    bands = []
    for other in (half, previous, farther):
        bands.append(jnp.einsum("pmi,pni->mn", half, other, preferred_element_type=jnp.float32))
    partial_sums = jnp.stack(bands, axis=1).reshape(r_local, BANDS * r_local)
    return lax.psum_scatter(partial_sums, "aux", scatter_dimension=0, tiled=True)


def solution(mesh):
    in_specs = (P("aux", "row", None), P("aux", "row", None), P("aux", None), P())
    out_specs = P(("row", "aux"), None)
    return jax.shard_map(
        per_device, mesh=mesh, in_specs=in_specs, out_specs=out_specs, check_vma=False
    )
```

profile of v0, /device:TPU:1, one launch (start us, length us, event | category | flops | bytes accessed | tf_op | source)
XLA Modules:
  0.0 376.3 jit_solution(15506394348860730612)
XLA Ops:
  6.5 0.7 all-gather.3.cloned.1.call-update
  7.3 0.0 all-reduce.3.cloned.1.call-start
  7.3 0.7 convert_bitcast_fusion
  8.0 0.1 copy.20
  8.1 0.1 broadcast_in_dim.4
  8.2 0.1 convert_element_type.28
  8.3 0.3 broadcast_in_dim.10
  8.5 1.5 convert_element_type.29
  10.1 7.9 %broadcast_multiply_fusion = bf16[4,128,8000]{1,2,0:T(8,128)(2,1)} fusion(bf16[4,128,8000]{1,2,0:T(8,128)(2,1)} %param.4, bf16[128,8000]{0,1:T(8,128)(2,1)} %convert_element_type.29), kind=kLoop, calls=%fused_computation.1 | loop fusion | flops 4096000 | bytes 18432000 | tf_op jit(solution)/shard_map/mul | solution.py:27
  17.9 11.3 %copy.21 = bf16[4,128,8000]{2,1,0:T(8,128)(2,1)} copy(bf16[4,128,8000]{1,2,0:T(8,128)(2,1)} %broadcast_multiply_fusion) | data formatting | bytes 16384000 | tf_op jit(solution)/shard_map/mul | solution.py:27
  29.3 45.3 %all-gather.3.cloned.1.call-done = bf16[32,250,256]{2,1,0:T(8,128)(2,1)} async-done(((bf16[1,250,256]{2,1,0:T(8,128)(2,1)}), bf16[32,250,256]{2,1,0:T(8,128)(2,1)}) %all-gather.3.cloned.1.call-update) | async-done | bytes 4096016 | tf_op jit(solution)/shard_map/all_gather | solution.py:29
  74.6 5.1 %reshape.24 = bf16[8000,256]{1,0:T(8,128)(2,1)} reshape(bf16[32,250,256]{2,1,0:T(8,128)(2,1)} %all-gather.3.cloned.1.call-done) | data formatting | bytes 8192000
  79.7 8.3 %fusion.2 = bf16[8,4,8,128]{3,2,1,0:T(8,128)(2,1)S(1)} fusion(bf16[512,8000]{1,0:T(8,128)(2,1)} %bitcast.31, bf16[8000,256]{1,0:T(8,128)(2,1)} %reshape.24, s32[64]{0:T(128)S(1)} %copy-done), kind=kOutput, calls=%fused_computation.4 | convolution fusion | flops 787009536 | bytes 12353792 | tf_op jit(solution)/shard_map/dot_general | solution.py:33
  88.0 1.2 collective-permute-start
  89.2 0.2 convolution_bitcast_fusion.2
  89.4 3.9 %collective-permute-done = bf16[4,128,64]{1,2,0:T(8,128)(2,1)S(1)} collective-permute-done((bf16[4,128,64]{1,2,0:T(8,128)(2,1)S(1)}, bf16[4,128,64]{1,2,0:T(8,128)(2,1)S(1)}, u32[]{:S(2)}, u32[]{:S(2)}) %collective-permute-start) | collective-permute-done | bytes 65568 | tf_op jit(solution)/shard_map/ppermute | solution.py:14
  93.3 0.2 convolution_bitcast_fusion.1
  93.5 5.0 %collective-permute-done.1 = bf16[4,128,64]{1,2,0:T(8,128)(2,1)S(1)} collective-permute-done((bf16[4,128,64]{1,2,0:T(8,128)(2,1)S(1)}, bf16[4,128,64]{1,2,0:T(8,128)(2,1)S(1)}, u32[]{:S(2)}, u32[]{:S(2)}) %collective-permute-start.1) | collective-permute-done | bytes 65568 | tf_op jit(solution)/shard_map/ppermute | solution.py:14
  98.5 0.2 convolution_bitcast_fusion
  98.8 0.8 copy.27
  99.6 0.0 all-reduce.3.cloned.1.call-update
  99.6 0.6 dynamic-slice
  100.9 267.2 %all-reduce.3.cloned.1.call-done = f32[128,384]{1,0:T(8,128)} async-done(((f32[128,384]{1,0:T(8,128)}), f32[128,384]{1,0:T(8,128)}) %all-reduce.3.cloned.1.call-update) | async-done | bytes 196624
  368.1 1.3 constant_dynamic-slice_fusion
  (8 shorter events, 0.0 us)
Async XLA Ops:
  6.5 68.1 %all-gather.3.cloned.1.call-start = ((), (), s32[]{:S(2)}) async-start(), calls=%async_computation | async-start | bytes 4325376 | tf_op jit(solution)/shard_map/all_gather | solution.py:29
  7.3 360.9 %all-reduce.3.cloned.1.call-start = ((), (), s32[]{:S(2)}) async-start(), calls=%async_computation.1 | async-start | bytes 393216
  29.3 50.4 %copy-start = (s32[64]{0:T(128)S(1)}, s32[64]{0:T(128)}, u32[]{:S(2)}) copy-start(s32[64]{0:T(128)} %param.7) | copy-start | bytes 772
  79.7 20.0 %copy-start.1 = (u32[256]{0:T(256)S(1)}, u32[256]{0:T(256)}, u32[]{:S(2)}) copy-start(u32[256]{0:T(256)} %constant.5) | copy-start | bytes 3076
  88.0 5.3 %collective-permute-start = (bf16[4,128,64]{1,2,0:T(8,128)(2,1)S(1)}, bf16[4,128,64]{1,2,0:T(8,128)(2,1)S(1)}, u32[]{:S(2)}, u32[]{:S(2)}) collective-permute-start(bf16[4,128,64]{1,2,0:T(8,128)(2,1)S(1)} %bitcast.34), channel_id=1, source_target_pairs={{7,0},{0,1},{1,2},{2,3},{3,4},{4,5},{5,6},{6,7},{15,8},{8,9},{9,10... | collective-permute-start | bytes 196616 | tf_op jit(solution)/shard_map/ppermute | solution.py:14
  93.3 5.2 %collective-permute-start.1 = (bf16[4,128,64]{1,2,0:T(8,128)(2,1)S(1)}, bf16[4,128,64]{1,2,0:T(8,128)(2,1)S(1)}, u32[]{:S(2)}, u32[]{:S(2)}) collective-permute-start(bf16[4,128,64]{1,2,0:T(8,128)(2,1)S(1)} %collective-permute-done), channel_id=1, source_target_pairs={{7,0},{0,1},{1,2},{2,3},{3,4},{4,5},{5,6},{6,7},{15,8},{8,9},{9,10... | collective-permute-start | bytes 196616 | tf_op jit(solution)/shard_map/ppermute | solution.py:14
Sparse Core Ops, SparseCore 0:
  9.9 64.6 all-gather.2
  99.7 268.3 all-reduce.2
where the time goes:
time: 377 us; the launch traced here: 376 us
  waiting for transfers between devices  322 us (85%)
  local copies, waits for them, and re-layouts  21.2 us (6%)
  between operations  14.1 us (4%)
  matrix products  8.97 us (2%)
  other arithmetic  8.59 us (2%)
    unnamed x3, waiting for transfers between devices  268 us
    all_gather x1, waiting for transfers between devices, per_device(): lax.all_gather(coefficients, 'aux', axis=0, tiled=True)  45.3 us
    mul x1, local copies, waits for them, and re-layouts, per_device(): integrals * rows_mask[None, :, :]  11.3 us
    ppermute x2, waiting for transfers between devices, from_behind(): return lax.ppermute(block, axis, route)  8.91 us
    dot_general x1, matrix products, per_device(): accum = jnp.dot(screened, picked, preferred_element_type=jnp.float32)  8.33 us
    mul x1, other arithmetic, per_device(): integrals * rows_mask[None, :, :]  7.89 us
  transfers between devices with their start and end apart: 4, of which 4 were waited for; matrix products, arithmetic and copies ran while one was open for 6% of the time, Pallas kernels for 0%

commit v1 on v0

v1 whole, which is shorter than its diff:
```python
import jax
import jax.numpy as jnp
from jax import lax
from jax.experimental import pallas as pl
from jax.experimental.pallas import tpu as pltpu
from jax.sharding import Mesh, PartitionSpec as P

BANDS = 3
COL_BLK = 500
HALF = 256
WIN = 2 * HALF
ALIGN = 16
ROW_BLK = 64

AUX = ("zh", "x", "core")
CHIPS = ("zh", "x")
ROW = ("zl", "y")


def window_offset(q):
    return (COL_BLK * q) % ALIGN


def pick_kernel(cols, occ_ref, coef_ref, out_ref):
    rows, occ_all = coef_ref.shape
    batch = occ_ref.shape[1]
    chip = lax.axis_index("zh") * lax.axis_size("x") + lax.axis_index("x")
    start = window_offset(chip) + cols * lax.axis_index("core")
    picker = lax.broadcasted_iota(jnp.int32, (occ_all, batch), 0) == occ_ref[...]
    picked = jnp.dot(
        coef_ref[...],
        picker.astype(jnp.float32).astype(jnp.bfloat16),
        preferred_element_type=jnp.float32,
    ).astype(jnp.bfloat16)
    source = lax.broadcasted_iota(jnp.int32, (rows, HALF), 0)
    place = lax.broadcasted_iota(jnp.int32, (rows, HALF), 1)
    shift = ((source + start) & (HALF - 1)) == place
    window = lax.dot_general(
        picked,
        shift.astype(jnp.float32).astype(jnp.bfloat16),
        (((0,), (0,)), ((), ())),
        preferred_element_type=jnp.float32,
    ).astype(jnp.bfloat16)
    for peer in range(out_ref.shape[0]):
        out_ref[peer] = window


def half_kernel(mask_ref, own_ref, other_ref, integrals_ref, out_ref, blocks, sems):
    chips, batch, _ = own_ref.shape
    p_local, basis, rows = integrals_ref.shape
    core = lax.axis_index("core")
    ends = [COL_BLK * q - window_offset(q) + WIN for q in range(chips)]
    copies = []
    begin = 0
    for q in range(chips):
        span = pl.ds(begin, ends[q] - begin)
        copies.append(
            pltpu.make_async_copy(
                integrals_ref.at[:, span, :], blocks.at[:, span, :], sems.at[q]
            )
        )
        copies[-1].start()
        begin = ends[q]
    lane = lax.broadcasted_iota(jnp.int32, (batch, HALF), 1)
    column = lax.broadcasted_iota(jnp.int32, (1, 2 * rows), 1) % rows
    zero = jnp.zeros((batch, HALF), jnp.bfloat16)
    totals = [jnp.zeros((batch, 2 * rows), jnp.float32) for _ in range(p_local // 2)]
    for q in range(chips):
        own, other = own_ref[q], other_ref[q]
        edge_own = window_offset(q) + (COL_BLK // 2) * core
        edge_other = window_offset(q) + (COL_BLK // 2) * (1 - core)
        low = jnp.where(lane >= edge_own, own, zero) + jnp.where(lane >= edge_other, other, zero)
        high = jnp.where(lane < edge_own, own, zero) + jnp.where(lane < edge_other, other, zero)
        window = jnp.concatenate([low, high], axis=1)
        keep = jnp.where(
            column < ROW_BLK, mask_ref[0, q], mask_ref[1, q]
        ).astype(jnp.float32)
        copies[q].wait()
        span = pl.ds(ends[q] - WIN, WIN)
        for pair in range(p_local // 2):
            block = jnp.concatenate(
                [blocks[2 * pair, span, :], blocks[2 * pair + 1, span, :]], axis=1
            )
            product = jnp.dot(window, block, preferred_element_type=jnp.float32)
            totals[pair] = totals[pair] + product * keep
    for p in range(p_local):
        part = totals[p // 2][:, (p % 2) * rows : (p % 2 + 1) * rows]
        out_ref[p * batch : (p + 1) * batch, :] = part.astype(jnp.bfloat16)


def band_kernel(rows_dev, half_ref, previous_ref, farther_ref, own_ref, send_ref):
    depth, rows = half_ref.shape
    core = lax.axis_index("core")
    out_row = lax.broadcasted_iota(jnp.int32, (rows, rows), 0)
    in_row = lax.broadcasted_iota(jnp.int32, (rows, rows), 1)
    mine = out_row < rows // 2
    local = jnp.where(mine, out_row, out_row - rows // 2)
    parity = jnp.where(mine, core, 1 - core)
    wanted = (local // rows_dev) * (2 * rows_dev) + parity * rows_dev + local % rows_dev
    order = (wanted == in_row).astype(jnp.float32).astype(jnp.bfloat16)
    left = lax.dot_general(
        order, half_ref[...], (((1,), (1,)), ((), ())), preferred_element_type=jnp.float32
    ).astype(jnp.bfloat16)
    for j, ref in enumerate((half_ref, previous_ref, farther_ref)):
        product = jnp.dot(left, ref[...], preferred_element_type=jnp.float32)
        own_ref[:, j * rows : (j + 1) * rows] = product[: rows // 2]
        send_ref[:, j * rows : (j + 1) * rows] = product[rows // 2 :]


def from_behind(block, axis, distance):
    devices = range(lax.axis_size(axis))
    route = [((i - distance) % len(devices), i) for i in devices]
    return lax.ppermute(block, axis, route)


def per_device(integrals, block_mask, coefficients, occ_index):
    p_local, r_local, basis = integrals.shape
    cols, _ = coefficients.shape
    batch = occ_index.shape[0]
    chips = lax.axis_size(CHIPS)
    cores = lax.axis_size("core")
    whole = pl.BlockSpec(memory_space=pltpu.VMEM)
    scalars = pl.BlockSpec(memory_space=pltpu.SMEM)

    windows = pl.pallas_call(
        lambda *refs: pick_kernel(cols, *refs),
        out_shape=jax.ShapeDtypeStruct((chips, batch, HALF), jnp.bfloat16),
        in_specs=[whole, whole],
        out_specs=whole,
        name="pick",
    )(occ_index.reshape(1, batch), coefficients)
    own = lax.all_to_all(windows, CHIPS, 0, 0)
    other = lax.ppermute(own, "core", [(0, 1), (1, 0)])

    half = pl.pallas_call(
        half_kernel,
        out_shape=jax.ShapeDtypeStruct((p_local * batch, r_local), jnp.bfloat16),
        in_specs=[scalars, whole, whole, pl.BlockSpec(memory_space=pl.ANY)],
        out_specs=whole,
        scratch_shapes=[
            pltpu.VMEM((p_local, basis, r_local), jnp.bfloat16),
            pltpu.SemaphoreType.DMA((chips,)),
        ],
        compiler_params=pltpu.CompilerParams(vmem_limit_bytes=24 * 1024 * 1024),
        name="half",
    )(block_mask[0], own, other, jnp.swapaxes(integrals, 1, 2))

    previous = from_behind(half, ROW, 1)
    farther = from_behind(half, ROW, 2)
    rows_dev = r_local // (chips * cores)
    part = jax.ShapeDtypeStruct((r_local // cores, BANDS * r_local), jnp.float32)
    kept, sent = pl.pallas_call(
        lambda *refs: band_kernel(rows_dev, *refs),
        out_shape=(part, part),
        in_specs=[whole] * 3,
        out_specs=(whole, whole),
        name="bands",
    )(half, previous, farther)
    chip_sum = kept + lax.ppermute(sent, "core", [(0, 1), (1, 0)])
    pieces = lax.all_to_all(
        chip_sum.reshape(chips, rows_dev, BANDS * r_local), CHIPS, 0, 0
    )
    return jnp.sum(pieces, axis=0)


def solution(mesh):
    fine = Mesh(mesh.devices.reshape(4, 4, 2, 2, 4), AUX + ROW)
    in_specs = (P(AUX, ROW, None), P(AUX, ROW, None), P(AUX, None), P())
    out_specs = P(ROW + AUX, None)
    return jax.shard_map(
        per_device, mesh=fine, in_specs=in_specs, out_specs=out_specs, check_vma=False
    )
```

time: 377 us -> 72.2 us (0.19)
  waiting for transfers between devices: 322 us -> 7.52 us
  blocking collectives: 0 us -> 39.9 us
  local copies, waits for them, and re-layouts: 21.2 us -> 4.66 us
  between operations: 14.1 us -> 0.04 us
  Pallas kernels: 0 us -> 9.5 us
  matrix products: 8.97 us -> 0 us
  starting transfers between devices: 1.22 us -> 8.7 us
  other arithmetic: 8.59 us -> 1.53 us
    unnamed x3 -> x0, waiting for transfers between devices: 268 us -> none
    all_gather x1 -> x0, waiting for transfers between devices: 45.3 us -> none  [per_device(): lax.all_gather(coefficients, 'aux', axis=0, tiled=True)]
    all_to_all x0 -> x2, blocking collectives: none -> 39.9 us  [the longest x1 26.4 us: per_device(): own = lax.all_to_all(windows, CHIPS, 0, 0)]
    mul x1 -> x0, local copies, waits for them, and re-layouts: 11.3 us -> none  [per_device(): integrals * rows_mask[None, :, :]]
    pallas_call x0 -> x3, Pallas kernels: none -> 9.5 us  [the longest x1 5.48 us: per_device(): pl.pallas_call(half_kernel, out_shape=jax.ShapeDtypeStruct((p_local * bat...]
    dot_general x4 -> x0, matrix products: 8.97 us -> none  [the longest x1 8.33 us: per_device(): accum = jnp.dot(screened, picked, preferred_element_type=jnp.float32)]
    mul x1 -> x0, other arithmetic: 7.89 us -> none  [per_device(): integrals * rows_mask[None, :, :]]
    ppermute x0 -> x2, starting transfers between devices: none -> 5.29 us  [the longest x1 3.49 us: per_device(): other = lax.ppermute(own, 'core', [(0, 1), (1, 0)])]
  transfers between devices with their start and end apart: 4 -> 4, of which waited for: 4 -> 4; matrix products, arithmetic and copies ran while one was open for 6% -> 0% of each run, Pallas kernels for 0% -> 0%
where the time goes in v1:
time: 72.2 us; the launch traced here: 71.9 us
  blocking collectives  39.9 us (55%)
  Pallas kernels  9.5 us (13%)
  starting transfers between devices  8.7 us (12%)
  waiting for transfers between devices  7.52 us (10%)
  local copies, waits for them, and re-layouts  4.66 us (6%)
  other arithmetic  1.53 us (2%)
    all_to_all x1, blocking collectives, per_device(): own = lax.all_to_all(windows, CHIPS, 0, 0)  26.4 us
    all_to_all x1, blocking collectives, per_device(): lax.all_to_all(chip_sum.reshape(chips, rows_dev, BANDS * r_local), CHIPS,...  13.6 us
    pallas_call x1, Pallas kernels, per_device(): pl.pallas_call(half_kernel, out_shape=jax.ShapeDtypeStruct((p_local * bat...  5.48 us
    ppermute x2, waiting for transfers between devices, from_behind(): return lax.ppermute(block, axis, route)  4.83 us
    unnamed x10, local copies, waits for them, and re-layouts  4.63 us
    ppermute x1, starting transfers between devices, per_device(): other = lax.ppermute(own, 'core', [(0, 1), (1, 0)])  3.49 us
    ppermute x2, starting transfers between devices, from_behind(): return lax.ppermute(block, axis, route)  3.41 us
    pallas_call x1, Pallas kernels, per_device(): pl.pallas_call(lambda *refs: pick_kernel(cols, *refs), out_shape=jax.Shap...  2.12 us
  transfers between devices with their start and end apart: 4, of which 4 were waited for; matrix products, arithmetic and copies ran while one was open for 0% of the time, Pallas kernels for 0%

profile of v1, /device:TPU:1, one launch (start us, length us, event | category | flops | bytes accessed | tf_op | source)
XLA Modules:
  0.0 71.9 jit_solution(13028151276452388076)
XLA Ops:
  0.0 2.1 %pick.1 = bf16[16,64,256]{2,1,0:T(8,128)(2,1)} custom-call(s32[1,64]{1,0:T(1,128)} %bitcast.5, bf16[250,256]{1,0:T(8,128)(2,1)} %refs_1_.1), custom_call_target="tpu_custom_call" | custom-call | tf_op jit(solution)/shard_map/pick/pallas_call | solution.py:125
  2.1 26.4 %all_to_all.10.own_ref = bf16[16,64,256]{2,1,0:T(8,128)(2,1)S(1)} all-to-all(bf16[16,64,256]{2,1,0:T(8,128)(2,1)} %pick.1), channel_id=1, replica_groups=mesh['zh'=4,'x'=4,'core'=2,'zl'=2,'y'=4] {'zh','x'}, dimensions={0} | all-to-all | bytes 1048576 | tf_op jit(solution)/shard_map/all_to_all | solution.py:132
  28.5 3.5 %collective-permute-start = (bf16[16,64,256]{2,1,0:T(8,128)(2,1)S(1)}, bf16[16,64,256]{2,1,0:T(8,128)(2,1)S(1)}, u32[]{:S(2)}, u32[]{:S(2)}) collective-permute-start(bf16[16,64,256]{2,1,0:T(8,128)(2,1)S(1)} %all_to_all.10.own_ref), channel_id=1, source_target_pairs={{0,8},{8,0},{1,9},{9,1},{2,10},{10,2},{3,11},{11,3},{4,12},{12,4},... | collective-permute-start | bytes 1572872 | tf_op jit(solution)/shard_map/ppermute | solution.py:133
  32.0 1.5 %collective-permute-done.other_ref = bf16[16,64,256]{2,1,0:T(8,128)(2,1)S(1)} collective-permute-done((bf16[16,64,256]{2,1,0:T(8,128)(2,1)S(1)}, bf16[16,64,256]{2,1,0:T(8,128)(2,1)S(1)}, u32[]{:S(2)}, u32[]{:S(2)}) %collective-permute-start) | collective-permute-done | bytes 524320 | tf_op jit(solution)/shard_map/ppermute | solution.py:133
  33.5 3.3 %copy-done = bf16[4,128,8000]{1,2,0:T(8,128)(2,1)S(1)} copy-done((bf16[4,128,8000]{1,2,0:T(8,128)(2,1)S(1)}, bf16[4,128,8000]{1,2,0:T(8,128)(2,1)}, u32[]{:S(2)}) %copy-start) | copy-done | bytes 8192024
  36.9 0.0 copy-start.2
  36.9 0.7 copy-done.2
  37.5 5.5 %half.1.refs_0_ = bf16[256,128]{1,0:T(8,128)(2,1)S(1)} custom-call(s32[2,16]{1,0:T(2,128)S(1)} %bitcast.4, bf16[16,64,256]{2,1,0:T(8,128)(2,1)S(1)} %all_to_all.10.own_ref, bf16[16,64,256]{2,1,0:T(8,128)(2,1)S(1)} %collective-permute-done.other_ref, bf16[4,8000,128]{2,1,0:T(8,128)(2,1)S(1)} %bitcast.3), custom_call_target="tpu_custom_call" | custom-call | tf_op jit(solution)/shard_map/half/pallas_call | solution.py:135
  43.0 0.0 copy-start.1
  43.0 3.0 %collective-permute-start.2 = (bf16[256,128]{1,0:T(8,128)(2,1)S(1)}, bf16[256,128]{1,0:T(8,128)(2,1)S(1)}, u32[]{:S(2)}, u32[]{:S(2)}) collective-permute-start(bf16[256,128]{1,0:T(8,128)(2,1)S(1)} %half.1.refs_0_), channel_id=1, source_target_pairs={{6,0},{7,1},{0,2},{1,3},{2,4},{3,5},{4,6},{5,7},{14,8},{15,9},{8,1... | collective-permute-start | bytes 196616 | tf_op jit(solution)/shard_map/ppermute | solution.py:113
  46.0 0.4 collective-permute-start.1
  46.4 2.2 %collective-permute-done.2.refs_2_ = bf16[256,128]{1,0:T(8,128)(2,1)S(1)} collective-permute-done((bf16[256,128]{1,0:T(8,128)(2,1)S(1)}, bf16[256,128]{1,0:T(8,128)(2,1)S(1)}, u32[]{:S(2)}, u32[]{:S(2)}) %collective-permute-start.2) | collective-permute-done | bytes 65568 | tf_op jit(solution)/shard_map/ppermute | solution.py:113
  48.6 0.0 copy-start.3
  48.6 2.6 %collective-permute-done.1.refs_1_ = bf16[256,128]{1,0:T(8,128)(2,1)S(1)} collective-permute-done((bf16[256,128]{1,0:T(8,128)(2,1)S(1)}, bf16[256,128]{1,0:T(8,128)(2,1)S(1)}, u32[]{:S(2)}, u32[]{:S(2)}) %collective-permute-start.1) | collective-permute-done | bytes 65568 | tf_op jit(solution)/shard_map/ppermute | solution.py:113
  51.3 0.0 copy-done.1
  51.3 0.0 copy-done.3
  51.3 0.0 copy-start.4
  51.3 0.6 copy-done.4
  51.9 1.9 %bands.1 = (f32[64,384]{1,0:T(8,128)}, f32[64,384]{1,0:T(8,128)}) custom-call(bf16[256,128]{1,0:T(8,128)(2,1)} %copy-done.1, bf16[256,128]{1,0:T(8,128)(2,1)} %copy-done.4, bf16[256,128]{1,0:T(8,128)(2,1)} %copy-done.3), custom_call_target="tpu_custom_call" | custom-call | tf_op jit(solution)/shard_map/bands/pallas_call | solution.py:152
  53.8 1.8 %collective-permute-start.3 = (f32[64,384]{1,0:T(8,128)}, f32[64,384]{1,0:T(8,128)S(1)}, u32[]{:S(2)}, u32[]{:S(2)}) collective-permute-start(f32[64,384]{1,0:T(8,128)} %get-tuple-element.8), channel_id=1, source_target_pairs={{0,8},{8,0},{1,9},{9,1},{2,10},{10,2},{3,11},{11,3},{4,12},{12,4},... | collective-permute-start | bytes 294920 | tf_op jit(solution)/shard_map/ppermute | solution.py:159
  55.6 1.2 %collective-permute-done.3 = f32[64,384]{1,0:T(8,128)S(1)} collective-permute-done((f32[64,384]{1,0:T(8,128)}, f32[64,384]{1,0:T(8,128)S(1)}, u32[]{:S(2)}, u32[]{:S(2)}) %collective-permute-start.3) | collective-permute-done | bytes 98336 | tf_op jit(solution)/shard_map/ppermute | solution.py:159
  56.8 0.9 %add.3 = f32[64,384]{1,0:T(8,128)S(1)} add(f32[64,384]{1,0:T(8,128)} %get-tuple-element.7, f32[64,384]{1,0:T(8,128)S(1)} %collective-permute-done.3) | non-fusion elementwise | flops 24576 | bytes 294912 | tf_op jit(solution)/shard_map/add | solution.py:159
  57.7 13.6 %all_to_all.11 = f32[16,4,384]{2,1,0:T(4,128)S(1)} all-to-all(f32[16,4,384]{2,1,0:T(4,128)S(1)} %reshape.7), channel_id=1, replica_groups=mesh['zh'=4,'x'=4,'core'=2,'zl'=2,'y'=4] {'zh','x'}, dimensions={0} | all-to-all | bytes 196608 | tf_op jit(solution)/shard_map/all_to_all | solution.py:160
  71.3 0.6 reduce_sum.9
  (2 shorter events, 0.0 us)
Async XLA Ops:
  28.5 5.0 %collective-permute-start = (bf16[16,64,256]{2,1,0:T(8,128)(2,1)S(1)}, bf16[16,64,256]{2,1,0:T(8,128)(2,1)S(1)}, u32[]{:S(2)}, u32[]{:S(2)}) collective-permute-start(bf16[16,64,256]{2,1,0:T(8,128)(2,1)S(1)} %all_to_all.10.own_ref), channel_id=1, source_target_pairs={{0,8},{8,0},{1,9},{9,1},{2,10},{10,2},{3,11},{11,3},{4,12},{12,4},... | collective-permute-start | bytes 1572872 | tf_op jit(solution)/shard_map/ppermute | solution.py:133
  33.5 3.3 %copy-start = (bf16[4,128,8000]{1,2,0:T(8,128)(2,1)S(1)}, bf16[4,128,8000]{1,2,0:T(8,128)(2,1)}, u32[]{:S(2)}) copy-start(bf16[4,128,8000]{1,2,0:T(8,128)(2,1)} %param.4) | copy-start | bytes 24576004
  36.9 0.7 copy-start.2
  43.0 8.3 %copy-start.1 = (bf16[256,128]{1,0:T(8,128)(2,1)}, bf16[256,128]{1,0:T(8,128)(2,1)S(1)}, u32[]{:S(2)}) copy-start(bf16[256,128]{1,0:T(8,128)(2,1)S(1)} %half.1.refs_0_) | copy-start | bytes 196612
  43.0 5.6 %collective-permute-start.2 = (bf16[256,128]{1,0:T(8,128)(2,1)S(1)}, bf16[256,128]{1,0:T(8,128)(2,1)S(1)}, u32[]{:S(2)}, u32[]{:S(2)}) collective-permute-start(bf16[256,128]{1,0:T(8,128)(2,1)S(1)} %half.1.refs_0_), channel_id=1, source_target_pairs={{6,0},{7,1},{0,2},{1,3},{2,4},{3,5},{4,6},{5,7},{14,8},{15,9},{8,1... | collective-permute-start | bytes 196616 | tf_op jit(solution)/shard_map/ppermute | solution.py:113
  46.0 5.2 %collective-permute-start.1 = (bf16[256,128]{1,0:T(8,128)(2,1)S(1)}, bf16[256,128]{1,0:T(8,128)(2,1)S(1)}, u32[]{:S(2)}, u32[]{:S(2)}) collective-permute-start(bf16[256,128]{1,0:T(8,128)(2,1)S(1)} %half.1.refs_0_), channel_id=1, source_target_pairs={{7,0},{0,1},{1,2},{2,3},{3,4},{4,5},{5,6},{6,7},{15,8},{8,9},{9,10... | collective-permute-start | bytes 196616 | tf_op jit(solution)/shard_map/ppermute | solution.py:113
  48.6 2.6 %copy-start.3 = (bf16[256,128]{1,0:T(8,128)(2,1)}, bf16[256,128]{1,0:T(8,128)(2,1)S(1)}, u32[]{:S(2)}) copy-start(bf16[256,128]{1,0:T(8,128)(2,1)S(1)} %collective-permute-done.2.refs_2_) | copy-start | bytes 196612
  51.3 0.6 copy-start.4
  53.8 3.0 %collective-permute-start.3 = (f32[64,384]{1,0:T(8,128)}, f32[64,384]{1,0:T(8,128)S(1)}, u32[]{:S(2)}, u32[]{:S(2)}) collective-permute-start(f32[64,384]{1,0:T(8,128)} %get-tuple-element.8), channel_id=1, source_target_pairs={{0,8},{8,0},{1,9},{9,1},{2,10},{10,2},{3,11},{11,3},{4,12},{12,4},... | collective-permute-start | bytes 294920 | tf_op jit(solution)/shard_map/ppermute | solution.py:159

commit v2 on v1

v2 whole, which is shorter than its diff:
```python
import jax
import jax.numpy as jnp
from jax import lax
from jax.experimental import pallas as pl
from jax.experimental.pallas import tpu as pltpu
from jax.sharding import Mesh, PartitionSpec as P

BANDS = 3
COL_BLK = 500
HALF = 256
WIN = 2 * HALF
ALIGN = 16
ROW_BLK = 64
MIB = 1024 * 1024

ZH, X, CORE, ZL, Y = "zh", "x", "core", "zl", "y"
AUX = (ZH, X, CORE)
ROW = (ZL, Y)


WHOLE = pl.BlockSpec(memory_space=pltpu.VMEM)
ANYWHERE = pl.BlockSpec(memory_space=pl.ANY)


def window_offset(q):
    return (COL_BLK * q) % ALIGN


def pick_kernel(occ_hbm, coef_hbm, mask_hbm, window_ref, keep_ref, occ_ref, coef_ref, mask_ref, sems):
    copies = [
        pltpu.make_async_copy(occ_hbm, occ_ref, sems.at[0]),
        pltpu.make_async_copy(coef_hbm, coef_ref, sems.at[1]),
        pltpu.make_async_copy(mask_hbm, mask_ref, sems.at[2]),
    ]
    for copy in copies:
        copy.start()
    cols, occ_all = coef_ref.shape
    batch = occ_ref.shape[1]
    chip = lax.axis_index(ZH) * lax.axis_size(X) + lax.axis_index(X)
    start = window_offset(chip) + cols * lax.axis_index(CORE)
    source = lax.broadcasted_iota(jnp.int32, (cols, HALF), 0)
    place = lax.broadcasted_iota(jnp.int32, (cols, HALF), 1)
    shift = ((source + start) & (HALF - 1)) == place
    copies[0].wait()
    picker = lax.broadcasted_iota(jnp.int32, (occ_all, batch), 0) == occ_ref[...]
    copies[2].wait()
    lane = lax.broadcasted_iota(jnp.int32, (1, keep_ref.shape[1]), 1)
    for q in range(keep_ref.shape[0]):
        keep = jnp.where(lane < ROW_BLK, mask_ref[0, q], mask_ref[1, q])
        keep_ref[q : q + 1, :] = keep.astype(jnp.float32)
    copies[1].wait()
    picked = jnp.dot(
        coef_ref[...],
        picker.astype(jnp.float32).astype(jnp.bfloat16),
        preferred_element_type=jnp.float32,
    ).astype(jnp.bfloat16)
    window_ref[0] = lax.dot_general(
        picked,
        shift.astype(jnp.float32).astype(jnp.bfloat16),
        (((0,), (0,)), ((), ())),
        preferred_element_type=jnp.float32,
    ).astype(jnp.bfloat16)


def stage_kernel(integrals_ref, total_ref):
    del integrals_ref
    total_ref[...] = jnp.zeros_like(total_ref)


def half_kernel(distance, last, keep_ref, own_ref, other_ref, integrals_ref, before_ref, out_ref):
    slots, batch, _ = own_ref.shape
    p_local, _, rows = integrals_ref.shape
    zh, zl, core = lax.axis_index(ZH), lax.axis_index(ZL), lax.axis_index(CORE)
    layers, width = lax.axis_size(ZH), lax.axis_size(X)
    x = lax.rem(lax.axis_index(X) + distance, width)
    near = jnp.where(zl == 0, layers - 1, 1)
    lane = lax.broadcasted_iota(jnp.int32, (batch, HALF), 1)
    zero = jnp.zeros((batch, HALF), jnp.bfloat16)
    pairs = p_local // 2
    totals = [before_ref[pair] for pair in range(pairs)]
    for slot, shift in enumerate((0, near, layers - near, 2)):
        q = lax.rem(zh + shift, layers) * width + x
        offset = lax.rem(COL_BLK * q, ALIGN)
        own, other = own_ref[slot], other_ref[slot]
        edge_own = offset + (COL_BLK // 2) * core
        edge_other = offset + (COL_BLK // 2) * (1 - core)
        low = jnp.where(lane >= edge_own, own, zero) + jnp.where(lane >= edge_other, other, zero)
        high = jnp.where(lane < edge_own, own, zero) + jnp.where(lane < edge_other, other, zero)
        window = jnp.concatenate([low, high], axis=1)
        keep = keep_ref[pl.ds(q, 1), :]
        keep = jnp.concatenate([keep, keep], axis=1)
        span = pl.ds(pl.multiple_of(COL_BLK * q - offset, ALIGN), WIN)
        for pair in range(pairs):
            block = jnp.concatenate(
                [integrals_ref[2 * pair, span, :], integrals_ref[2 * pair + 1, span, :]], axis=1
            )
            product = jnp.dot(window, block, preferred_element_type=jnp.float32)
            totals[pair] = totals[pair] + product * keep
    if last:
        for p in range(p_local):
            part = totals[p // 2][:, (p % 2) * rows : (p % 2 + 1) * rows]
            out_ref[p * batch : (p + 1) * batch, :] = part.astype(jnp.bfloat16)
    else:
        for pair in range(pairs):
            out_ref[pair] = totals[pair]


def band_kernel(rows_dev, half_ref, previous_ref, farther_ref, own_ref, send_ref):
    rows = half_ref.shape[1]
    core = lax.axis_index(CORE)
    out_row = lax.broadcasted_iota(jnp.int32, (rows, rows), 0)
    in_row = lax.broadcasted_iota(jnp.int32, (rows, rows), 1)
    mine = out_row < rows // 2
    local = jnp.where(mine, out_row, out_row - rows // 2)
    parity = jnp.where(mine, core, 1 - core)
    wanted = (local // rows_dev) * (2 * rows_dev) + parity * rows_dev + local % rows_dev
    order = (wanted == in_row).astype(jnp.float32).astype(jnp.bfloat16)
    left = lax.dot_general(
        order, half_ref[...], (((1,), (1,)), ((), ())), preferred_element_type=jnp.float32
    ).astype(jnp.bfloat16)
    for j, ref in enumerate((half_ref, previous_ref, farther_ref)):
        product = jnp.dot(left, ref[...], preferred_element_type=jnp.float32)
        own_ref[:, j * rows : (j + 1) * rows] = product[: rows // 2]
        send_ref[:, j * rows : (j + 1) * rows] = product[rows // 2 :]


def from_behind(block, axis, distance):
    devices = range(lax.axis_size(axis))
    route = [((i - distance) % len(devices), i) for i in devices]
    return lax.ppermute(block, axis, route)


def along_z(block, even, odd):
    height = lax.axis_size((ZH, ZL))
    route = [((z + (odd if z % 2 else even)) % height, z) for z in range(height)]
    return lax.ppermute(block, (ZH, ZL), route)


def other_core(block):
    return lax.ppermute(block, CORE, [(0, 1), (1, 0)])


def params(mib):
    return pltpu.CompilerParams(vmem_limit_bytes=mib * MIB)


def per_device(integrals, block_mask, coefficients, occ_index):
    p_local, r_local, basis = integrals.shape
    cols, occ_all = coefficients.shape
    batch = occ_index.shape[0]
    chips = lax.axis_size((ZH, X))
    mask = block_mask[0]

    window, keep = pl.pallas_call(
        pick_kernel,
        out_shape=(
            jax.ShapeDtypeStruct((1, batch, HALF), jnp.bfloat16),
            jax.ShapeDtypeStruct((chips, r_local), jnp.float32),
        ),
        in_specs=[ANYWHERE] * 3,
        out_specs=(WHOLE, WHOLE),
        scratch_shapes=[
            pltpu.VMEM((1, batch), jnp.int32),
            pltpu.VMEM((cols, occ_all), jnp.bfloat16),
            pltpu.SMEM(mask.shape, jnp.int32),
            pltpu.SemaphoreType.DMA((3,)),
        ],
        name="pick",
    )(occ_index.reshape(1, batch), coefficients, mask)

    by_column, window = lax.optimization_barrier((jnp.swapaxes(integrals, 1, 2), window))
    layers = [window, along_z(window, -1, 1), along_z(window, 2, -2), along_z(window, -3, 3)]
    running = jax.ShapeDtypeStruct((p_local // 2, batch, 2 * r_local), jnp.float32)
    total = pl.pallas_call(
        stage_kernel,
        out_shape=running,
        in_specs=[WHOLE],
        out_specs=WHOLE,
        compiler_params=params(12),
        name="stage",
    )(by_column)
    layers, by_column, total = lax.optimization_barrier((layers, by_column, total))
    stack = jnp.concatenate(layers, axis=0)

    for distance in (0, 1, 3, 2):
        own = stack if distance == 0 else from_behind(stack, X, -distance)
        last = distance == 2
        out = jax.ShapeDtypeStruct((p_local * batch, r_local), jnp.bfloat16) if last else running
        total = pl.pallas_call(
            lambda *refs, distance=distance, last=last: half_kernel(distance, last, *refs),
            out_shape=out,
            in_specs=[WHOLE] * 5,
            out_specs=WHOLE,
            compiler_params=params(12),
            cost_estimate=pl.CostEstimate(
                flops=2 * batch * WIN * 4 * p_local * r_local,
                bytes_accessed=by_column.size // 2,
                transcendentals=0,
            ),
            name="half",
        )(keep, own, other_core(own), by_column, total)
    half = total

    previous = from_behind(half, ROW, 1)
    farther = from_behind(half, ROW, 2)
    rows_dev = r_local // (chips * lax.axis_size(CORE))
    part = jax.ShapeDtypeStruct((chips * rows_dev, BANDS * r_local), jnp.float32)
    kept, sent = pl.pallas_call(
        lambda *refs: band_kernel(rows_dev, *refs),
        out_shape=(part, part),
        in_specs=[WHOLE] * 3,
        out_specs=(WHOLE, WHOLE),
        compiler_params=params(4),
        name="bands",
    )(half, previous, farther)
    chip_sum = kept + other_core(sent)
    pieces = lax.all_to_all(
        chip_sum.reshape(chips, rows_dev, BANDS * r_local), (ZH, X), 0, 0
    )
    return jnp.sum(pieces, axis=0)


def solution(mesh):
    fine = Mesh(mesh.devices.reshape(4, 4, 2, 2, 4), AUX + ROW)
    in_specs = (P(AUX, ROW, None), P(AUX, ROW, None), P(AUX, None), P())
    out_specs = P(ROW + AUX, None)
    return jax.shard_map(
        per_device, mesh=fine, in_specs=in_specs, out_specs=out_specs, check_vma=False
    )
```

time: 72.2 us -> 56.6 us (0.78)
  blocking collectives: 39.9 us -> 13.1 us
  starting transfers between devices: 8.7 us -> 26.9 us
  Pallas kernels: 9.5 us -> 4.29 us
  other arithmetic: 1.53 us -> 0.64 us
    all_to_all x2 -> x1, blocking collectives: 39.9 us -> 13.1 us  [per_device(): lax.all_to_all(chip_sum.reshape(chips, rows_dev, BANDS * r_local), (ZH, X...]
    ppermute x2 -> x8, starting transfers between devices: 5.29 us -> 19.3 us  [the longest x3 10.5 us: along_z(): return lax.ppermute(block, (ZH, ZL), route)]
    ppermute x2 -> x5, starting transfers between devices: 3.41 us -> 7.68 us  [from_behind(): return lax.ppermute(block, axis, route)]
    pallas_call x2 -> x6, Pallas kernels: 7.59 us -> 3.95 us  [the longest x4 2.02 us: per_device(): pl.pallas_call(lambda *refs, distance=distance, last=last: half_kernel(di...]
    ppermute x2 -> x8, waiting for transfers between devices: 2.69 us -> 0.96 us  [the longest x5 0.95 us: other_core(): return lax.ppermute(block, CORE, [(0, 1), (1, 0)])]
    pallas_call x1, Pallas kernels: 1.9 us -> 0.35 us  [per_device(): pl.pallas_call(lambda *refs: band_kernel(rows_dev, *refs), out_shape=(par...]
    ppermute x2 -> x5, waiting for transfers between devices: 4.83 us -> 6.28 us  [from_behind(): return lax.ppermute(block, axis, route)]
    add x1, other arithmetic: 0.9 us -> 0.01 us  [per_device(): chip_sum = kept + other_core(sent)]
  transfers between devices with their start and end apart: 4 -> 13, of which waited for: 4 -> 4; matrix products, arithmetic and copies ran while one was open for 0% -> 0% of each run, Pallas kernels for 0% -> 3%
where the time goes in v2:
time: 56.6 us; the launch traced here: 56.5 us
  starting transfers between devices  26.9 us (48%)
  blocking collectives  13.1 us (23%)
  waiting for transfers between devices  7.24 us (13%)
  Pallas kernels  4.29 us (8%)
  local copies, waits for them, and re-layouts  4.09 us (7%)
  other arithmetic  0.64 us (1%)
    all_to_all x1, blocking collectives, per_device(): lax.all_to_all(chip_sum.reshape(chips, rows_dev, BANDS * r_local), (ZH, X...  13.1 us
    ppermute x3, starting transfers between devices, along_z(): return lax.ppermute(block, (ZH, ZL), route)  10.5 us
    ppermute x5, starting transfers between devices, other_core(): return lax.ppermute(block, CORE, [(0, 1), (1, 0)])  8.76 us
    ppermute x5, starting transfers between devices, from_behind(): return lax.ppermute(block, axis, route)  7.68 us
    ppermute x5, waiting for transfers between devices, from_behind(): return lax.ppermute(block, axis, route)  6.28 us
    unnamed x11, local copies, waits for them, and re-layouts  4.05 us
    pallas_call x4, Pallas kernels, per_device(): pl.pallas_call(lambda *refs, distance=distance, last=last: half_kernel(di...  2.02 us
    pallas_call x1, Pallas kernels, per_device(): pl.pallas_call(pick_kernel, out_shape=(jax.ShapeDtypeStruct((1, batch, HA...  1.91 us
  transfers between devices with their start and end apart: 13, of which 4 were waited for; matrix products, arithmetic and copies ran while one was open for 0% of the time, Pallas kernels for 3%

profile of v2, /device:TPU:1, one launch (start us, length us, event | category | flops | bytes accessed | tf_op | source)
XLA Modules:
  0.0 56.5 jit_solution(3055348297228784390)
XLA Ops:
  0.0 1.9 %pick.1 = (bf16[1,64,256]{2,1,0:T(8,128)(2,1)}, f32[16,128]{1,0:T(8,128)}) custom-call(s32[1,64]{1,0:T(1,128)} %bitcast.9, bf16[250,256]{1,0:T(8,128)(2,1)} %coef_hbm.1, s32[2,16]{1,0:T(2,128)} %bitcast.8), custom_call_target="tpu_custom_call" | custom-call | tf_op jit(solution)/shard_map/pick/pallas_call | solution.py:154
  1.9 7.4 %collective-permute-start.2 = (bf16[1,64,256]{2,1,0:T(8,128)(2,1)}, bf16[1,64,256]{2,1,0:T(8,128)(2,1)S(1)}, u32[]{:S(2)}, u32[]{:S(2)}) collective-permute-start(bf16[1,64,256]{2,1,0:T(8,128)(2,1)} %get-tuple-element.21), channel_id=1, source_target_pairs={{132,0},{128,4},{196,64},{192,68},{4,128},{0,132},{68,192},{64,196... | collective-permute-start | bytes 98312 | tf_op jit(solution)/shard_map/ppermute | solution.py:136
  9.6 2.8 %collective-permute-start = (bf16[1,64,256]{2,1,0:T(8,128)(2,1)}, bf16[1,64,256]{2,1,0:T(8,128)(2,1)S(1)}, u32[]{:S(2)}, u32[]{:S(2)}) collective-permute-start(bf16[1,64,256]{2,1,0:T(8,128)(2,1)} %get-tuple-element.21), channel_id=1, source_target_pairs={{196,0},{64,4},{4,64},{128,68},{68,128},{192,132},{132,192},{0,196... | collective-permute-start | bytes 98312 | tf_op jit(solution)/shard_map/ppermute | solution.py:136
  12.4 3.3 %copy-done = bf16[4,128,8000]{1,2,0:T(8,128)(2,1)S(1)} copy-done((bf16[4,128,8000]{1,2,0:T(8,128)(2,1)S(1)}, bf16[4,128,8000]{1,2,0:T(8,128)(2,1)}, u32[]{:S(2)}) %copy-start) | copy-done | bytes 8192024
  15.8 0.7 %copy-done.3 = bf16[1,64,256]{2,1,0:T(8,128)(2,1)S(1)} copy-done((bf16[1,64,256]{2,1,0:T(8,128)(2,1)S(1)}, bf16[1,64,256]{2,1,0:T(8,128)(2,1)}, u32[]{:S(2)}) %copy-start.3) | copy-done | bytes 32792
  16.5 2.6 %collective-permute-start.7 = (bf16[4,64,256]{2,1,0:T(8,128)(2,1)S(1)}, bf16[4,64,256]{2,1,0:T(8,128)(2,1)S(1)}, u32[]{:S(2)}, u32[]{:S(2)}) collective-permute-start(bf16[4,64,256]{2,1,0:T(8,128)(2,1)S(1)} %constant_dynamic-update-slice_fusion.refs_1_), channel_id=1, source_target_pairs={{16,0},{32,16},{48,32},{0,48},{17,1},{33,17},{49,33},{1,49},{18,2}... | collective-permute-start | bytes 393224 | tf_op jit(solution)/shard_map/ppermute | solution.py:130
  19.1 1.7 %collective-permute-start.3 = (bf16[4,64,256]{2,1,0:T(8,128)(2,1)S(1)}, bf16[4,64,256]{2,1,0:T(8,128)(2,1)S(1)}, u32[]{:S(2)}, u32[]{:S(2)}) collective-permute-start(bf16[4,64,256]{2,1,0:T(8,128)(2,1)S(1)} %constant_dynamic-update-slice_fusion.refs_1_), channel_id=1, source_target_pairs={{32,0},{48,16},{0,32},{16,48},{33,1},{49,17},{1,33},{17,49},{34,2}... | collective-permute-start | bytes 393224 | tf_op jit(solution)/shard_map/ppermute | solution.py:130
  20.8 2.4 %collective-permute-start.9 = (bf16[4,64,256]{2,1,0:T(8,128)(2,1)S(1)}, bf16[4,64,256]{2,1,0:T(8,128)(2,1)S(1)}, u32[]{:S(2)}, u32[]{:S(2)}) collective-permute-start(bf16[4,64,256]{2,1,0:T(8,128)(2,1)S(1)} %constant_dynamic-update-slice_fusion.refs_1_), channel_id=1, source_target_pairs={{0,8},{8,0},{1,9},{9,1},{2,10},{10,2},{3,11},{11,3},{4,12},{12,4},... | collective-permute-start | bytes 393224 | tf_op jit(solution)/shard_map/ppermute | solution.py:140
  23.2 1.6 %collective-permute-start.8 = (bf16[4,64,256]{2,1,0:T(8,128)(2,1)S(1)}, bf16[4,64,256]{2,1,0:T(8,128)(2,1)S(1)}, u32[]{:S(2)}, u32[]{:S(2)}) collective-permute-start(bf16[4,64,256]{2,1,0:T(8,128)(2,1)S(1)} %collective-permute-done.7.refs_1_), channel_id=1, source_target_pairs={{0,8},{8,0},{1,9},{9,1},{2,10},{10,2},{3,11},{11,3},{4,12},{12,4},... | collective-permute-start | bytes 393224 | tf_op jit(solution)/shard_map/ppermute | solution.py:140
  24.8 1.4 %collective-permute-done.5.refs_1_ = bf16[4,64,256]{2,1,0:T(8,128)(2,1)S(1)} collective-permute-done((bf16[4,64,256]{2,1,0:T(8,128)(2,1)S(1)}, bf16[4,64,256]{2,1,0:T(8,128)(2,1)S(1)}, u32[]{:S(2)}, u32[]{:S(2)}) %collective-permute-start.5) | collective-permute-done | bytes 131104 | tf_op jit(solution)/shard_map/ppermute | solution.py:130
  26.3 2.8 %collective-permute-start.6 = (bf16[4,64,256]{2,1,0:T(8,128)(2,1)S(1)}, bf16[4,64,256]{2,1,0:T(8,128)(2,1)S(1)}, u32[]{:S(2)}, u32[]{:S(2)}) collective-permute-start(bf16[4,64,256]{2,1,0:T(8,128)(2,1)S(1)} %collective-permute-done.5.refs_1_), channel_id=1, source_target_pairs={{0,8},{8,0},{1,9},{9,1},{2,10},{10,2},{3,11},{11,3},{4,12},{12,4},... | collective-permute-start | bytes 393224 | tf_op jit(solution)/shard_map/ppermute | solution.py:140
  29.1 0.5 half.4.refs_4_
  29.6 0.5 half.5.refs_4_
  30.1 0.5 half.6.refs_4_
  30.6 0.5 half.7.refs_0_
  31.1 3.0 %collective-permute-start.11 = (bf16[256,128]{1,0:T(8,128)(2,1)S(1)}, bf16[256,128]{1,0:T(8,128)(2,1)S(1)}, u32[]{:S(2)}, u32[]{:S(2)}) collective-permute-start(bf16[256,128]{1,0:T(8,128)(2,1)S(1)} %half.7.refs_0_), channel_id=1, source_target_pairs={{6,0},{7,1},{0,2},{1,3},{2,4},{3,5},{4,6},{5,7},{14,8},{15,9},{8,1... | collective-permute-start | bytes 196616 | tf_op jit(solution)/shard_map/ppermute | solution.py:130
  34.1 0.4 collective-permute-start.10
  34.5 2.2 %collective-permute-done.11.refs_2_ = bf16[256,128]{1,0:T(8,128)(2,1)S(1)} collective-permute-done((bf16[256,128]{1,0:T(8,128)(2,1)S(1)}, bf16[256,128]{1,0:T(8,128)(2,1)S(1)}, u32[]{:S(2)}, u32[]{:S(2)}) %collective-permute-start.11) | collective-permute-done | bytes 65568 | tf_op jit(solution)/shard_map/ppermute | solution.py:130
  36.8 2.6 %collective-permute-done.10.refs_1_ = bf16[256,128]{1,0:T(8,128)(2,1)S(1)} collective-permute-done((bf16[256,128]{1,0:T(8,128)(2,1)S(1)}, bf16[256,128]{1,0:T(8,128)(2,1)S(1)}, u32[]{:S(2)}, u32[]{:S(2)}) %collective-permute-start.10) | collective-permute-done | bytes 65568 | tf_op jit(solution)/shard_map/ppermute | solution.py:130
  39.4 0.3 bands.1
  39.7 2.0 %collective-permute-start.12 = (f32[64,384]{1,0:T(8,128)S(1)}, f32[64,384]{1,0:T(8,128)S(1)}, u32[]{:S(2)}, u32[]{:S(2)}) collective-permute-start(f32[64,384]{1,0:T(8,128)S(1)} %get-tuple-element.28), channel_id=1, source_target_pairs={{0,8},{8,0},{1,9},{9,1},{2,10},{10,2},{3,11},{11,3},{4,12},{12,4},... | collective-permute-start | bytes 294920 | tf_op jit(solution)/shard_map/ppermute | solution.py:140
  41.7 0.9 %collective-permute-done.12 = f32[64,384]{1,0:T(8,128)S(1)} collective-permute-done((f32[64,384]{1,0:T(8,128)S(1)}, f32[64,384]{1,0:T(8,128)S(1)}, u32[]{:S(2)}, u32[]{:S(2)}) %collective-permute-start.12) | collective-permute-done | bytes 98336 | tf_op jit(solution)/shard_map/ppermute | solution.py:140
  42.7 13.1 %all_to_all.5 = f32[16,4,384]{2,1,0:T(4,128)S(1)} all-to-all(f32[16,4,384]{2,1,0:T(4,128)S(1)} %reshape.7), channel_id=1, replica_groups=mesh['zh'=4,'x'=4,'core'=2,'zl'=2,'y'=4] {'zh','x'}, dimensions={0} | all-to-all | bytes 196608 | tf_op jit(solution)/shard_map/all_to_all | solution.py:217
  55.8 0.6 %reduce_sum.9 = f32[4,384]{1,0:T(4,128)} reduce(f32[16,4,384]{2,1,0:T(4,128)S(1)} %all_to_all.5, f32[]{:T(128)} %constant.0.clone.1), dimensions={0}, to_apply=%region_0.0 | reduce | flops 23040 | bytes 104452 | tf_op jit(solution)/shard_map/reduce_sum | solution.py:220
  (25 shorter events, 0.4 us)
Async XLA Ops:
  1.9 13.8 %collective-permute-start.2 = (bf16[1,64,256]{2,1,0:T(8,128)(2,1)}, bf16[1,64,256]{2,1,0:T(8,128)(2,1)S(1)}, u32[]{:S(2)}, u32[]{:S(2)}) collective-permute-start(bf16[1,64,256]{2,1,0:T(8,128)(2,1)} %get-tuple-element.21), channel_id=1, source_target_pairs={{132,0},{128,4},{196,64},{192,68},{4,128},{0,132},{68,192},{64,196... | collective-permute-start | bytes 98312 | tf_op jit(solution)/shard_map/ppermute | solution.py:136
  9.3 6.5 %collective-permute-start.1 = (bf16[1,64,256]{2,1,0:T(8,128)(2,1)}, bf16[1,64,256]{2,1,0:T(8,128)(2,1)S(1)}, u32[]{:S(2)}, u32[]{:S(2)}) collective-permute-start(bf16[1,64,256]{2,1,0:T(8,128)(2,1)} %get-tuple-element.21), channel_id=1, source_target_pairs={{64,0},{196,4},{128,64},{4,68},{192,128},{68,132},{0,192},{132,196... | collective-permute-start | bytes 98312 | tf_op jit(solution)/shard_map/ppermute | solution.py:136
  9.6 6.2 %collective-permute-start = (bf16[1,64,256]{2,1,0:T(8,128)(2,1)}, bf16[1,64,256]{2,1,0:T(8,128)(2,1)S(1)}, u32[]{:S(2)}, u32[]{:S(2)}) collective-permute-start(bf16[1,64,256]{2,1,0:T(8,128)(2,1)} %get-tuple-element.21), channel_id=1, source_target_pairs={{196,0},{64,4},{4,64},{128,68},{68,128},{192,132},{132,192},{0,196... | collective-permute-start | bytes 98312 | tf_op jit(solution)/shard_map/ppermute | solution.py:136
  12.4 3.3 %copy-start = (bf16[4,128,8000]{1,2,0:T(8,128)(2,1)S(1)}, bf16[4,128,8000]{1,2,0:T(8,128)(2,1)}, u32[]{:S(2)}) copy-start(bf16[4,128,8000]{1,2,0:T(8,128)(2,1)} %param.4) | copy-start | bytes 24576004
  15.8 0.8 %copy-start.3 = (bf16[1,64,256]{2,1,0:T(8,128)(2,1)S(1)}, bf16[1,64,256]{2,1,0:T(8,128)(2,1)}, u32[]{:S(2)}) copy-start(bf16[1,64,256]{2,1,0:T(8,128)(2,1)} %get-tuple-element.21) | copy-start | bytes 98308
  15.8 13.3 %copy-start.1 = (bf16[4,128,8000]{1,2,0:T(8,128)(2,1)S(1)}, bf16[4,128,8000]{1,2,0:T(8,128)(2,1)}, u32[]{:S(2)}) copy-start(bf16[4,128,8000]{1,2,0:T(8,128)(2,1)} %param.4) | copy-start | bytes 24576004
  15.8 13.3 %copy-start.2 = (f32[16,128]{1,0:T(8,128)S(1)}, f32[16,128]{1,0:T(8,128)}, u32[]{:S(2)}) copy-start(f32[16,128]{1,0:T(8,128)} %get-tuple-element.17.refs_0_) | copy-start | bytes 24580
  16.5 6.6 %collective-permute-start.7 = (bf16[4,64,256]{2,1,0:T(8,128)(2,1)S(1)}, bf16[4,64,256]{2,1,0:T(8,128)(2,1)S(1)}, u32[]{:S(2)}, u32[]{:S(2)}) collective-permute-start(bf16[4,64,256]{2,1,0:T(8,128)(2,1)S(1)} %constant_dynamic-update-slice_fusion.refs_1_), channel_id=1, source_target_pairs={{16,0},{32,16},{48,32},{0,48},{17,1},{33,17},{49,33},{1,49},{18,2}... | collective-permute-start | bytes 393224 | tf_op jit(solution)/shard_map/ppermute | solution.py:130
  19.1 7.2 %collective-permute-start.5 = (bf16[4,64,256]{2,1,0:T(8,128)(2,1)S(1)}, bf16[4,64,256]{2,1,0:T(8,128)(2,1)S(1)}, u32[]{:S(2)}, u32[]{:S(2)}) collective-permute-start(bf16[4,64,256]{2,1,0:T(8,128)(2,1)S(1)} %constant_dynamic-update-slice_fusion.refs_1_), channel_id=1, source_target_pairs={{48,0},{0,16},{16,32},{32,48},{49,1},{1,17},{17,33},{33,49},{50,2}... | collective-permute-start | bytes 393224 | tf_op jit(solution)/shard_map/ppermute | solution.py:130
  19.1 9.9 %collective-permute-start.3 = (bf16[4,64,256]{2,1,0:T(8,128)(2,1)S(1)}, bf16[4,64,256]{2,1,0:T(8,128)(2,1)S(1)}, u32[]{:S(2)}, u32[]{:S(2)}) collective-permute-start(bf16[4,64,256]{2,1,0:T(8,128)(2,1)S(1)} %constant_dynamic-update-slice_fusion.refs_1_), channel_id=1, source_target_pairs={{32,0},{48,16},{0,32},{16,48},{33,1},{49,17},{1,33},{17,49},{34,2}... | collective-permute-start | bytes 393224 | tf_op jit(solution)/shard_map/ppermute | solution.py:130
  20.8 8.2 %collective-permute-start.9 = (bf16[4,64,256]{2,1,0:T(8,128)(2,1)S(1)}, bf16[4,64,256]{2,1,0:T(8,128)(2,1)S(1)}, u32[]{:S(2)}, u32[]{:S(2)}) collective-permute-start(bf16[4,64,256]{2,1,0:T(8,128)(2,1)S(1)} %constant_dynamic-update-slice_fusion.refs_1_), channel_id=1, source_target_pairs={{0,8},{8,0},{1,9},{9,1},{2,10},{10,2},{3,11},{11,3},{4,12},{12,4},... | collective-permute-start | bytes 393224 | tf_op jit(solution)/shard_map/ppermute | solution.py:140
  23.2 6.4 %collective-permute-start.8 = (bf16[4,64,256]{2,1,0:T(8,128)(2,1)S(1)}, bf16[4,64,256]{2,1,0:T(8,128)(2,1)S(1)}, u32[]{:S(2)}, u32[]{:S(2)}) collective-permute-start(bf16[4,64,256]{2,1,0:T(8,128)(2,1)S(1)} %collective-permute-done.7.refs_1_), channel_id=1, source_target_pairs={{0,8},{8,0},{1,9},{9,1},{2,10},{10,2},{3,11},{11,3},{4,12},{12,4},... | collective-permute-start | bytes 393224 | tf_op jit(solution)/shard_map/ppermute | solution.py:140
  26.3 3.8 %collective-permute-start.6 = (bf16[4,64,256]{2,1,0:T(8,128)(2,1)S(1)}, bf16[4,64,256]{2,1,0:T(8,128)(2,1)S(1)}, u32[]{:S(2)}, u32[]{:S(2)}) collective-permute-start(bf16[4,64,256]{2,1,0:T(8,128)(2,1)S(1)} %collective-permute-done.5.refs_1_), channel_id=1, source_target_pairs={{0,8},{8,0},{1,9},{9,1},{2,10},{10,2},{3,11},{11,3},{4,12},{12,4},... | collective-permute-start | bytes 393224 | tf_op jit(solution)/shard_map/ppermute | solution.py:140
  29.0 1.6 %collective-permute-start.4 = (bf16[4,64,256]{2,1,0:T(8,128)(2,1)S(1)}, bf16[4,64,256]{2,1,0:T(8,128)(2,1)S(1)}, u32[]{:S(2)}, u32[]{:S(2)}) collective-permute-start(bf16[4,64,256]{2,1,0:T(8,128)(2,1)S(1)} %collective-permute-done.3.refs_1_), channel_id=1, source_target_pairs={{0,8},{8,0},{1,9},{9,1},{2,10},{10,2},{3,11},{11,3},{4,12},{12,4},... | collective-permute-start | bytes 393224 | tf_op jit(solution)/shard_map/ppermute | solution.py:140
  31.1 5.6 %collective-permute-start.11 = (bf16[256,128]{1,0:T(8,128)(2,1)S(1)}, bf16[256,128]{1,0:T(8,128)(2,1)S(1)}, u32[]{:S(2)}, u32[]{:S(2)}) collective-permute-start(bf16[256,128]{1,0:T(8,128)(2,1)S(1)} %half.7.refs_0_), channel_id=1, source_target_pairs={{6,0},{7,1},{0,2},{1,3},{2,4},{3,5},{4,6},{5,7},{14,8},{15,9},{8,1... | collective-permute-start | bytes 196616 | tf_op jit(solution)/shard_map/ppermute | solution.py:130
  34.1 5.2 %collective-permute-start.10 = (bf16[256,128]{1,0:T(8,128)(2,1)S(1)}, bf16[256,128]{1,0:T(8,128)(2,1)S(1)}, u32[]{:S(2)}, u32[]{:S(2)}) collective-permute-start(bf16[256,128]{1,0:T(8,128)(2,1)S(1)} %half.7.refs_0_), channel_id=1, source_target_pairs={{7,0},{0,1},{1,2},{2,3},{3,4},{4,5},{5,6},{6,7},{15,8},{8,9},{9,10... | collective-permute-start | bytes 196616 | tf_op jit(solution)/shard_map/ppermute | solution.py:130
  39.7 3.0 %collective-permute-start.12 = (f32[64,384]{1,0:T(8,128)S(1)}, f32[64,384]{1,0:T(8,128)S(1)}, u32[]{:S(2)}, u32[]{:S(2)}) collective-permute-start(f32[64,384]{1,0:T(8,128)S(1)} %get-tuple-element.28), channel_id=1, source_target_pairs={{0,8},{8,0},{1,9},{9,1},{2,10},{10,2},{3,11},{11,3},{4,12},{12,4},... | collective-permute-start | bytes 294920 | tf_op jit(solution)/shard_map/ppermute | solution.py:140

commit v3 on v2

v3 whole, which is shorter than its diff:
```python
import jax
import jax.numpy as jnp
from jax import lax
from jax.experimental import pallas as pl
from jax.experimental.pallas import tpu as pltpu
from jax.sharding import Mesh, PartitionSpec as P

BANDS = 3
COL_BLK = 500
WIN = 512
ALIGN = 16
ROW_BLK = 64
MIB = 1024 * 1024

ZH, X, CORE, ZL, Y = "zh", "x", "core", "zl", "y"
AUX = (ZH, X, CORE)
ROW = (ZL, Y)


WHOLE = pl.BlockSpec(memory_space=pltpu.VMEM)


def window_offset(q):
    return (COL_BLK * q) % ALIGN


def pick_kernel(cols, small_ref, own_ref, other_ref, window_ref):
    batch = small_ref.shape[1]
    chip = lax.axis_index(ZH) * lax.axis_size(X) + lax.axis_index(X)
    core = lax.axis_index(CORE)
    offset = window_offset(chip)
    picker = lax.broadcasted_iota(jnp.int32, (own_ref.shape[1], batch), 0) == small_ref[0:1, :]
    picker = picker.astype(jnp.float32).astype(jnp.bfloat16)
    window = jnp.zeros((batch, WIN), jnp.float32)
    for ref, start in ((own_ref, offset + cols * core), (other_ref, offset + cols * (1 - core))):
        picked = jnp.dot(ref[...], picker, preferred_element_type=jnp.float32)
        source = lax.broadcasted_iota(jnp.int32, (ref.shape[0], WIN), 0)
        place = lax.broadcasted_iota(jnp.int32, (ref.shape[0], WIN), 1)
        shift = (source + start == place).astype(jnp.float32).astype(jnp.bfloat16)
        window = window + lax.dot_general(
            picked.astype(jnp.bfloat16),
            shift,
            (((0,), (0,)), ((), ())),
            preferred_element_type=jnp.float32,
        )
    window_ref[...] = window.astype(jnp.bfloat16)


def stack_kernel(window_ref, first_ref, second_ref, out_ref):
    core = lax.axis_index(CORE)

    @pl.when(core == 0)
    def _():
        out_ref[0] = window_ref[...]

    @pl.when(core != 0)
    def _():
        out_ref[0] = second_ref[...]

    out_ref[1] = first_ref[...]


def stage_kernel(integrals_ref, total_ref):
    del integrals_ref
    total_ref[...] = jnp.zeros_like(total_ref)


def half_kernel(distance, last, small_ref, own_ref, other_ref, integrals_ref, before_ref, out_ref):
    slots, batch, _ = own_ref.shape
    p_local, _, rows = integrals_ref.shape
    zh, zl, core = lax.axis_index(ZH), lax.axis_index(ZL), lax.axis_index(CORE)
    layers, width = lax.axis_size(ZH), lax.axis_size(X)
    x = lax.axis_index(X) ^ distance
    near = jnp.where(zl == 0, layers - 1, 1)
    pairs = p_local // 2
    totals = [before_ref[pair] for pair in range(pairs)]
    masks = small_ref[...].astype(jnp.float32)
    entry = lax.broadcasted_iota(jnp.int32, masks.shape, 1)
    column = lax.broadcasted_iota(jnp.int32, (1, 2 * rows), 1) % rows
    for ref, holder in ((own_ref, core), (other_ref, 1 - core)):
        for slot in range(slots):
            even = 0 if slot == 0 else 2
            odd = layers - near if slot == 0 else near
            q = lax.rem(zh + jnp.where(holder == 0, even, odd), layers) * width + x
            offset = lax.rem(COL_BLK * q, ALIGN)
            chosen = jnp.sum(jnp.where(entry == q, masks, 0.0), axis=1, keepdims=True)
            keep = jnp.where(column < ROW_BLK, chosen[1:2, :], chosen[2:3, :])
            span = pl.ds(pl.multiple_of(COL_BLK * q - offset, ALIGN), WIN)
            for pair in range(pairs):
                block = jnp.concatenate(
                    [integrals_ref[2 * pair, span, :], integrals_ref[2 * pair + 1, span, :]],
                    axis=1,
                )
                product = jnp.dot(ref[slot], block, preferred_element_type=jnp.float32)
                totals[pair] = totals[pair] + product * keep
    if last:
        for p in range(p_local):
            part = totals[p // 2][:, (p % 2) * rows : (p % 2 + 1) * rows]
            out_ref[p * batch : (p + 1) * batch, :] = part.astype(jnp.bfloat16)
    else:
        for pair in range(pairs):
            out_ref[pair] = totals[pair]


def near_kernel(rows_dev, half_ref, previous_ref, left_ref, near_ref):
    rows = half_ref.shape[1]
    core = lax.axis_index(CORE)
    out_row = lax.broadcasted_iota(jnp.int32, (rows, rows), 0)
    in_row = lax.broadcasted_iota(jnp.int32, (rows, rows), 1)
    mine = out_row < rows // 2
    local = jnp.where(mine, out_row, out_row - rows // 2)
    parity = jnp.where(mine, core, 1 - core)
    wanted = (local // rows_dev) * (2 * rows_dev) + parity * rows_dev + local % rows_dev
    order = (wanted == in_row).astype(jnp.float32).astype(jnp.bfloat16)
    left = lax.dot_general(
        order, half_ref[...], (((1,), (1,)), ((), ())), preferred_element_type=jnp.float32
    ).astype(jnp.bfloat16)
    left_ref[...] = left
    for j, ref in enumerate((half_ref, previous_ref)):
        near_ref[:, j * rows : (j + 1) * rows] = jnp.dot(
            left, ref[...], preferred_element_type=jnp.float32
        )


def band_kernel(left_ref, near_ref, farther_ref, own_ref, send_ref):
    rows = left_ref.shape[0]
    done = near_ref.shape[1]
    own_ref[:, :done] = near_ref[: rows // 2, :]
    send_ref[:, :done] = near_ref[rows // 2 :, :]
    product = jnp.dot(left_ref[...], farther_ref[...], preferred_element_type=jnp.float32)
    own_ref[:, done:] = product[: rows // 2]
    send_ref[:, done:] = product[rows // 2 :]


def from_behind(block, axis, distance):
    devices = range(lax.axis_size(axis))
    route = [((i - distance) % len(devices), i) for i in devices]
    return lax.ppermute(block, axis, route)


def along_z(block, steps):
    height, halves, cores = (lax.axis_size(a) for a in ((ZH, ZL), ZL, CORE))

    def place(z, core):
        return (z // halves * cores + core) * halves + z % halves

    route = [
        (place((z + steps[core, z % halves]) % height, core), place(z, core))
        for z in range(height)
        for core in range(cores)
        if (core, z % halves) in steps
    ]
    return lax.ppermute(block, (ZH, CORE, ZL), route)


def across_x(block, distance):
    return lax.ppermute(block, X, [(i ^ distance, i) for i in range(lax.axis_size(X))])


def other_core(block):
    return lax.ppermute(block, CORE, [(0, 1), (1, 0)])


def params(mib):
    return pltpu.CompilerParams(vmem_limit_bytes=mib * MIB)


def per_device(integrals, block_mask, coefficients, occ_index):
    p_local, r_local, basis = integrals.shape
    cols = coefficients.shape[0]
    batch = occ_index.shape[0]
    chips = lax.axis_size((ZH, X))
    mask = block_mask[0]

    other_coefficients = other_core(coefficients)
    small = jnp.concatenate(
        [occ_index[None, :], jnp.pad(mask, ((0, 0), (0, batch - mask.shape[1])))], axis=0
    )
    padded = jnp.pad(coefficients, ((0, -cols % ALIGN), (0, 0)))
    window = pl.pallas_call(
        lambda *refs: pick_kernel(cols, *refs),
        out_shape=jax.ShapeDtypeStruct((batch, WIN), jnp.bfloat16),
        in_specs=[WHOLE] * 3,
        out_specs=WHOLE,
        compiler_params=params(4),
        name="pick",
    )(small, padded, other_coefficients)

    by_column, window = lax.optimization_barrier((jnp.swapaxes(integrals, 1, 2), window))
    second = along_z(window, {(1, 0): 2, (1, 1): -2})
    first = along_z(window, {(0, 0): -3, (0, 1): 3, (1, 0): -1, (1, 1): 1})
    running = jax.ShapeDtypeStruct((p_local // 2, batch, 2 * r_local), jnp.float32)
    total = pl.pallas_call(
        stage_kernel,
        out_shape=running,
        in_specs=[WHOLE],
        out_specs=WHOLE,
        compiler_params=params(12),
        name="stage",
    )(by_column)
    first, by_column, total = lax.optimization_barrier((first, by_column, total))
    stack = pl.pallas_call(
        stack_kernel,
        out_shape=jax.ShapeDtypeStruct((2, batch, WIN), jnp.bfloat16),
        in_specs=[WHOLE] * 3,
        out_specs=WHOLE,
        compiler_params=params(4),
        name="stack",
    )(window, first, second)

    for distance in (0, 2, 1, 3):
        own = stack if distance == 0 else across_x(stack, distance)
        if distance == 2:
            own, total = lax.optimization_barrier((own, total))
        last = distance == 3
        out = jax.ShapeDtypeStruct((p_local * batch, r_local), jnp.bfloat16) if last else running
        total = pl.pallas_call(
            lambda *refs, distance=distance, last=last: half_kernel(distance, last, *refs),
            out_shape=out,
            in_specs=[WHOLE] * 5,
            out_specs=WHOLE,
            compiler_params=params(12),
            cost_estimate=pl.CostEstimate(flops=1, bytes_accessed=4096, transcendentals=0)
            if distance == 0
            else pl.CostEstimate(
                flops=2 * batch * WIN * 4 * p_local * r_local,
                bytes_accessed=by_column.size // 2,
                transcendentals=0,
            ),
            name="half",
        )(small, own, other_core(own), by_column, total)
    half = total

    previous = from_behind(half, ROW, 1)
    farther = from_behind(half, ROW, 2)
    rows_dev = r_local // (chips * lax.axis_size(CORE))
    left, near = pl.pallas_call(
        lambda *refs: near_kernel(rows_dev, *refs),
        out_shape=(
            jax.ShapeDtypeStruct(half.shape[::-1], jnp.bfloat16),
            jax.ShapeDtypeStruct((r_local, (BANDS - 1) * r_local), jnp.float32),
        ),
        in_specs=[WHOLE] * 2,
        out_specs=(WHOLE, WHOLE),
        compiler_params=params(4),
        cost_estimate=pl.CostEstimate(flops=1, bytes_accessed=4096, transcendentals=0),
        name="near",
    )(half, previous)
    part = jax.ShapeDtypeStruct((chips * rows_dev, BANDS * r_local), jnp.float32)
    kept, sent = pl.pallas_call(
        band_kernel,
        out_shape=(part, part),
        in_specs=[WHOLE] * 3,
        out_specs=(WHOLE, WHOLE),
        compiler_params=params(4),
        name="bands",
    )(left, near, farther)
    chip_sum = kept + other_core(sent)
    pieces = lax.all_to_all(
        chip_sum.reshape(chips, rows_dev, BANDS * r_local), (ZH, X), 0, 0
    )
    return jnp.sum(pieces, axis=0)


def solution(mesh):
    fine = Mesh(mesh.devices.reshape(4, 4, 2, 2, 4), AUX + ROW)
    in_specs = (P(AUX, ROW, None), P(AUX, ROW, None), P(AUX, None), P())
    out_specs = P(ROW + AUX, None)
    return jax.shard_map(
        per_device, mesh=fine, in_specs=in_specs, out_specs=out_specs, check_vma=False
    )
```

time: 56.6 us -> 53.6 us (0.947)
  starting transfers between devices: 26.9 us -> 23.4 us
  Pallas kernels: 4.29 us -> 2.9 us
  blocking collectives: 13.1 us -> 14.3 us
  other arithmetic: 0.64 us -> 1.33 us
    ppermute x5 -> x2, starting transfers between devices: 7.68 us -> 4 us  [from_behind(): return lax.ppermute(block, axis, route)]
    ppermute x5 -> x2, waiting for transfers between devices: 6.28 us -> 2.67 us  [from_behind(): return lax.ppermute(block, axis, route)]
    ppermute x3 -> x5, waiting for transfers between devices: 0.01 us -> 2.89 us  [the longest x3 2.88 us: across_x(): lax.ppermute(block, X, [(i ^ distance, i) for i in range(lax.axis_size(X))])]
    pallas_call x2 -> x4, Pallas kernels: 2.26 us -> 0.93 us  [the longest x1 0.44 us: per_device(): pl.pallas_call(lambda *refs: pick_kernel(cols, *refs), out_shape=jax.Shap...]
    all_to_all x1, blocking collectives: 13.1 us -> 14.3 us  [per_device(): lax.all_to_all(chip_sum.reshape(chips, rows_dev, BANDS * r_local), (ZH, X...]
    pad x0 -> x1, local copies, waits for them, and re-layouts: none -> 0.91 us  [per_device(): padded = jnp.pad(coefficients, ((0, -cols % ALIGN), (0, 0)))]
    unnamed x11 -> x4, local copies, waits for them, and re-layouts: 4.05 us -> 3.32 us
    concatenate x0 -> x1, other arithmetic: none -> 0.69 us  [per_device(): jnp.concatenate([occ_index[None, :], jnp.pad(mask, ((0, 0), (0, batch - m...]
  transfers between devices with their start and end apart: 13 -> 13, of which waited for: 4 -> 6; matrix products, arithmetic and copies ran while one was open for 0% -> 3% of each run, Pallas kernels for 3% -> 3%
where the time goes in v3:
time: 53.6 us; the launch traced here: 53.1 us
  starting transfers between devices  23.4 us (44%)
  blocking collectives  14.3 us (27%)
  waiting for transfers between devices  6.69 us (12%)
  local copies, waits for them, and re-layouts  4.27 us (8%)
  Pallas kernels  2.9 us (5%)
  other arithmetic  1.33 us (2%)
    all_to_all x1, blocking collectives, per_device(): lax.all_to_all(chip_sum.reshape(chips, rows_dev, BANDS * r_local), (ZH, X...  14.3 us
    ppermute x6, starting transfers between devices, other_core(): return lax.ppermute(block, CORE, [(0, 1), (1, 0)])  8.75 us
    ppermute x2, starting transfers between devices, along_z(): return lax.ppermute(block, (ZH, CORE, ZL), route)  7 us
    ppermute x2, starting transfers between devices, from_behind(): return lax.ppermute(block, axis, route)  4 us
    ppermute x3, starting transfers between devices, across_x(): lax.ppermute(block, X, [(i ^ distance, i) for i in range(lax.axis_size(X))])  3.68 us
    unnamed x4, local copies, waits for them, and re-layouts  3.32 us
    ppermute x3, waiting for transfers between devices, across_x(): lax.ppermute(block, X, [(i ^ distance, i) for i in range(lax.axis_size(X))])  2.88 us
    ppermute x2, waiting for transfers between devices, from_behind(): return lax.ppermute(block, axis, route)  2.67 us
  transfers between devices with their start and end apart: 13, of which 6 were waited for; matrix products, arithmetic and copies ran while one was open for 3% of the time, Pallas kernels for 3%

profile of v3, /device:TPU:1, one launch (start us, length us, event | category | flops | bytes accessed | tf_op | source)
XLA Modules:
  0.0 53.1 jit_solution(17462714570356331393)
XLA Ops:
  0.0 3.2 %collective-permute-start = (bf16[250,256]{1,0:T(8,128)(2,1)}, bf16[250,256]{1,0:T(8,128)(2,1)S(1)}, u32[]{:S(2)}, u32[]{:S(2)}) collective-permute-start(bf16[250,256]{1,0:T(8,128)(2,1)} %param.6), channel_id=1, source_target_pairs={{0,8},{8,0},{1,9},{9,1},{2,10},{10,2},{3,11},{11,3},{4,12},{12,4},... | collective-permute-start | bytes 384008 | tf_op jit(solution)/shard_map/ppermute | solution.py:161
  3.2 0.9 %pad.9.refs_1_ = bf16[256,256]{1,0:T(8,128)(2,1)S(1)} pad(bf16[250,256]{1,0:T(8,128)(2,1)} %param.6, bf16[]{:T(256)} %constant.4.clone.1), padding=0_6x0_0 | pad | bytes 259074 | tf_op jit(solution)/shard_map/jit(_pad)/pad | solution.py:179
  4.2 0.7 %pad_add_fusion.refs_0_ = s32[3,64]{1,0:T(4,128)S(1)} fusion(s32[2,16]{1,0:T(2,128)} %bitcast.8, s32[1,64]{1,0:T(1,128)} %bitcast.9), kind=kLoop, calls=%fused_computation | loop fusion | flops 192 | bytes 1152 | tf_op jit(solution)/shard_map/concatenate | solution.py:176
  5.3 3.9 %collective-permute-start.1 = (bf16[64,512]{1,0:T(8,128)(2,1)S(1)}, bf16[64,512]{1,0:T(8,128)(2,1)S(1)}, u32[]{:S(2)}, u32[]{:S(2)}) collective-permute-start(bf16[64,512]{1,0:T(8,128)(2,1)S(1)} %pick.1.window_ref), channel_id=1, source_target_pairs={{132,0},{204,8},{128,4},{72,12},{196,64},{12,72},{192,68},{136,76}... | collective-permute-start | bytes 196616 | tf_op jit(solution)/shard_map/ppermute | solution.py:153
  9.2 3.1 %collective-permute-start.2 = (bf16[64,512]{1,0:T(8,128)(2,1)S(1)}, bf16[64,512]{1,0:T(8,128)(2,1)S(1)}, u32[]{:S(2)}, u32[]{:S(2)}) collective-permute-start(bf16[64,512]{1,0:T(8,128)(2,1)S(1)} %pick.1.window_ref), channel_id=1, source_target_pairs={{72,8},{204,12},{136,72},{12,76},{200,136},{76,140},{8,200},{140,2... | collective-permute-start | bytes 196616 | tf_op jit(solution)/shard_map/ppermute | solution.py:153
  12.3 3.3 %copy-done = bf16[4,128,8000]{1,2,0:T(8,128)(2,1)S(1)} copy-done((bf16[4,128,8000]{1,2,0:T(8,128)(2,1)S(1)}, bf16[4,128,8000]{1,2,0:T(8,128)(2,1)}, u32[]{:S(2)}) %copy-start) | copy-done | bytes 8192024
  15.8 2.8 %collective-permute-start.7 = (bf16[2,64,512]{2,1,0:T(8,128)(2,1)S(1)}, bf16[2,64,512]{2,1,0:T(8,128)(2,1)S(1)}, u32[]{:S(2)}, u32[]{:S(2)}) collective-permute-start(bf16[2,64,512]{2,1,0:T(8,128)(2,1)S(1)} %stack.1.refs_1_), channel_id=1, source_target_pairs={{32,0},{48,16},{0,32},{16,48},{33,1},{49,17},{1,33},{17,49},{34,2}... | collective-permute-start | bytes 393224 | tf_op jit(solution)/shard_map/ppermute | solution.py:157
  18.9 0.5 %collective-permute-start.3 = (bf16[2,64,512]{2,1,0:T(8,128)(2,1)S(1)}, bf16[2,64,512]{2,1,0:T(8,128)(2,1)S(1)}, u32[]{:S(2)}, u32[]{:S(2)}) collective-permute-start(bf16[2,64,512]{2,1,0:T(8,128)(2,1)S(1)} %stack.1.refs_1_), channel_id=1, source_target_pairs={{48,0},{32,16},{16,32},{0,48},{49,1},{33,17},{17,33},{1,49},{50,2}... | collective-permute-start | bytes 393224 | tf_op jit(solution)/shard_map/ppermute | solution.py:157
  19.5 0.5 half.4.refs_4_
  20.0 2.1 %collective-permute-done.7.refs_1_ = bf16[2,64,512]{2,1,0:T(8,128)(2,1)S(1)} collective-permute-done((bf16[2,64,512]{2,1,0:T(8,128)(2,1)S(1)}, bf16[2,64,512]{2,1,0:T(8,128)(2,1)S(1)}, u32[]{:S(2)}, u32[]{:S(2)}) %collective-permute-start.7) | collective-permute-done | bytes 131104 | tf_op jit(solution)/shard_map/ppermute | solution.py:157
  22.1 2.1 %collective-permute-start.9 = (bf16[2,64,512]{2,1,0:T(8,128)(2,1)S(1)}, bf16[2,64,512]{2,1,0:T(8,128)(2,1)S(1)}, u32[]{:S(2)}, u32[]{:S(2)}) collective-permute-start(bf16[2,64,512]{2,1,0:T(8,128)(2,1)S(1)} %collective-permute-done.7.refs_1_), channel_id=1, source_target_pairs={{0,8},{8,0},{1,9},{9,1},{2,10},{10,2},{3,11},{11,3},{4,12},{12,4},... | collective-permute-start | bytes 393224 | tf_op jit(solution)/shard_map/ppermute | solution.py:161
  24.2 0.8 %collective-permute-done.5.refs_1_ = bf16[2,64,512]{2,1,0:T(8,128)(2,1)S(1)} collective-permute-done((bf16[2,64,512]{2,1,0:T(8,128)(2,1)S(1)}, bf16[2,64,512]{2,1,0:T(8,128)(2,1)S(1)}, u32[]{:S(2)}, u32[]{:S(2)}) %collective-permute-start.5) | collective-permute-done | bytes 131104 | tf_op jit(solution)/shard_map/ppermute | solution.py:157
  25.0 1.2 %collective-permute-start.6 = (bf16[2,64,512]{2,1,0:T(8,128)(2,1)S(1)}, bf16[2,64,512]{2,1,0:T(8,128)(2,1)S(1)}, u32[]{:S(2)}, u32[]{:S(2)}) collective-permute-start(bf16[2,64,512]{2,1,0:T(8,128)(2,1)S(1)} %collective-permute-done.5.refs_1_), channel_id=1, source_target_pairs={{0,8},{8,0},{1,9},{9,1},{2,10},{10,2},{3,11},{11,3},{4,12},{12,4},... | collective-permute-start | bytes 393224 | tf_op jit(solution)/shard_map/ppermute | solution.py:161
  26.5 0.5 half.5.refs_4_
  27.2 0.5 half.6.refs_4_
  27.7 0.5 half.7.refs_0_
  28.2 1.4 %collective-permute-start.10 = (bf16[256,128]{1,0:T(8,128)(2,1)S(1)}, bf16[256,128]{1,0:T(8,128)(2,1)S(1)}, u32[]{:S(2)}, u32[]{:S(2)}) collective-permute-start(bf16[256,128]{1,0:T(8,128)(2,1)S(1)} %half.7.refs_0_), channel_id=1, source_target_pairs={{7,0},{0,1},{1,2},{2,3},{3,4},{4,5},{5,6},{6,7},{15,8},{8,9},{9,10... | collective-permute-start | bytes 196616 | tf_op jit(solution)/shard_map/ppermute | solution.py:138
  29.6 2.6 %collective-permute-start.11 = (bf16[256,128]{1,0:T(8,128)(2,1)S(1)}, bf16[256,128]{1,0:T(8,128)(2,1)S(1)}, u32[]{:S(2)}, u32[]{:S(2)}) collective-permute-start(bf16[256,128]{1,0:T(8,128)(2,1)S(1)} %half.7.refs_0_), channel_id=1, source_target_pairs={{6,0},{7,1},{0,2},{1,3},{2,4},{3,5},{4,6},{5,7},{14,8},{15,9},{8,1... | collective-permute-start | bytes 196616 | tf_op jit(solution)/shard_map/ppermute | solution.py:138
  32.2 1.3 %collective-permute-done.10.refs_1_ = bf16[256,128]{1,0:T(8,128)(2,1)S(1)} collective-permute-done((bf16[256,128]{1,0:T(8,128)(2,1)S(1)}, bf16[256,128]{1,0:T(8,128)(2,1)S(1)}, u32[]{:S(2)}, u32[]{:S(2)}) %collective-permute-start.10) | collective-permute-done | bytes 65568 | tf_op jit(solution)/shard_map/ppermute | solution.py:138
  33.8 1.4 %collective-permute-done.11.farther_ref = bf16[256,128]{1,0:T(8,128)(2,1)S(1)} collective-permute-done((bf16[256,128]{1,0:T(8,128)(2,1)S(1)}, bf16[256,128]{1,0:T(8,128)(2,1)S(1)}, u32[]{:S(2)}, u32[]{:S(2)}) %collective-permute-start.11) | collective-permute-done | bytes 65568 | tf_op jit(solution)/shard_map/ppermute | solution.py:138
  35.4 1.8 %collective-permute-start.12 = (f32[64,384]{1,0:T(8,128)S(1)}, f32[64,384]{1,0:T(8,128)S(1)}, u32[]{:S(2)}, u32[]{:S(2)}) collective-permute-start(f32[64,384]{1,0:T(8,128)S(1)} %get-tuple-element.26), channel_id=1, source_target_pairs={{0,8},{8,0},{1,9},{9,1},{2,10},{10,2},{3,11},{11,3},{4,12},{12,4},... | collective-permute-start | bytes 294920 | tf_op jit(solution)/shard_map/ppermute | solution.py:161
  37.1 0.9 %collective-permute-done.12 = f32[64,384]{1,0:T(8,128)S(1)} collective-permute-done((f32[64,384]{1,0:T(8,128)S(1)}, f32[64,384]{1,0:T(8,128)S(1)}, u32[]{:S(2)}, u32[]{:S(2)}) %collective-permute-start.12) | collective-permute-done | bytes 98336 | tf_op jit(solution)/shard_map/ppermute | solution.py:161
  38.1 14.3 %all_to_all.5 = f32[16,4,384]{2,1,0:T(4,128)S(1)} all-to-all(f32[16,4,384]{2,1,0:T(4,128)S(1)} %reshape.3), channel_id=1, replica_groups=mesh['zh'=4,'x'=4,'core'=2,'zl'=2,'y'=4] {'zh','x'}, dimensions={0} | all-to-all | bytes 196608 | tf_op jit(solution)/shard_map/all_to_all | solution.py:259
  52.5 0.6 %reduce_sum.9 = f32[4,384]{1,0:T(4,128)} reduce(f32[16,4,384]{2,1,0:T(4,128)S(1)} %all_to_all.5, f32[]{:T(128)} %constant.5.clone.1), dimensions={0}, to_apply=%region_0.1 | reduce | flops 23040 | bytes 104452 | tf_op jit(solution)/shard_map/reduce_sum | solution.py:262
  (21 shorter events, 1.9 us)
Async XLA Ops:
  0.0 4.9 %collective-permute-start = (bf16[250,256]{1,0:T(8,128)(2,1)}, bf16[250,256]{1,0:T(8,128)(2,1)S(1)}, u32[]{:S(2)}, u32[]{:S(2)}) collective-permute-start(bf16[250,256]{1,0:T(8,128)(2,1)} %param.6), channel_id=1, source_target_pairs={{0,8},{8,0},{1,9},{9,1},{2,10},{10,2},{3,11},{11,3},{4,12},{12,4},... | collective-permute-start | bytes 384008 | tf_op jit(solution)/shard_map/ppermute | solution.py:161
  5.3 10.4 %collective-permute-start.1 = (bf16[64,512]{1,0:T(8,128)(2,1)S(1)}, bf16[64,512]{1,0:T(8,128)(2,1)S(1)}, u32[]{:S(2)}, u32[]{:S(2)}) collective-permute-start(bf16[64,512]{1,0:T(8,128)(2,1)S(1)} %pick.1.window_ref), channel_id=1, source_target_pairs={{132,0},{204,8},{128,4},{72,12},{196,64},{12,72},{192,68},{136,76}... | collective-permute-start | bytes 196616 | tf_op jit(solution)/shard_map/ppermute | solution.py:153
  9.2 6.4 %collective-permute-start.2 = (bf16[64,512]{1,0:T(8,128)(2,1)S(1)}, bf16[64,512]{1,0:T(8,128)(2,1)S(1)}, u32[]{:S(2)}, u32[]{:S(2)}) collective-permute-start(bf16[64,512]{1,0:T(8,128)(2,1)S(1)} %pick.1.window_ref), channel_id=1, source_target_pairs={{72,8},{204,12},{136,72},{12,76},{200,136},{76,140},{8,200},{140,2... | collective-permute-start | bytes 196616 | tf_op jit(solution)/shard_map/ppermute | solution.py:153
  12.3 3.3 %copy-start = (bf16[4,128,8000]{1,2,0:T(8,128)(2,1)S(1)}, bf16[4,128,8000]{1,2,0:T(8,128)(2,1)}, u32[]{:S(2)}) copy-start(bf16[4,128,8000]{1,2,0:T(8,128)(2,1)} %param.4) | copy-start | bytes 24576004
  15.6 3.9 %copy-start.1 = (bf16[4,128,8000]{1,2,0:T(8,128)(2,1)S(1)}, bf16[4,128,8000]{1,2,0:T(8,128)(2,1)}, u32[]{:S(2)}) copy-start(bf16[4,128,8000]{1,2,0:T(8,128)(2,1)} %param.4) | copy-start | bytes 24576004
  15.7 3.8 %collective-permute-start.8 = (bf16[2,64,512]{2,1,0:T(8,128)(2,1)S(1)}, bf16[2,64,512]{2,1,0:T(8,128)(2,1)S(1)}, u32[]{:S(2)}, u32[]{:S(2)}) collective-permute-start(bf16[2,64,512]{2,1,0:T(8,128)(2,1)S(1)} %stack.1.refs_1_), channel_id=1, source_target_pairs={{0,8},{8,0},{1,9},{9,1},{2,10},{10,2},{3,11},{11,3},{4,12},{12,4},... | collective-permute-start | bytes 393224 | tf_op jit(solution)/shard_map/ppermute | solution.py:161
  15.8 6.3 %collective-permute-start.7 = (bf16[2,64,512]{2,1,0:T(8,128)(2,1)S(1)}, bf16[2,64,512]{2,1,0:T(8,128)(2,1)S(1)}, u32[]{:S(2)}, u32[]{:S(2)}) collective-permute-start(bf16[2,64,512]{2,1,0:T(8,128)(2,1)S(1)} %stack.1.refs_1_), channel_id=1, source_target_pairs={{32,0},{48,16},{0,32},{16,48},{33,1},{49,17},{1,33},{17,49},{34,2}... | collective-permute-start | bytes 393224 | tf_op jit(solution)/shard_map/ppermute | solution.py:157
  18.6 6.3 %collective-permute-start.5 = (bf16[2,64,512]{2,1,0:T(8,128)(2,1)S(1)}, bf16[2,64,512]{2,1,0:T(8,128)(2,1)S(1)}, u32[]{:S(2)}, u32[]{:S(2)}) collective-permute-start(bf16[2,64,512]{2,1,0:T(8,128)(2,1)S(1)} %stack.1.refs_1_), channel_id=1, source_target_pairs={{16,0},{0,16},{48,32},{32,48},{17,1},{1,17},{49,33},{33,49},{18,2}... | collective-permute-start | bytes 393224 | tf_op jit(solution)/shard_map/ppermute | solution.py:157
  18.9 7.3 %collective-permute-start.3 = (bf16[2,64,512]{2,1,0:T(8,128)(2,1)S(1)}, bf16[2,64,512]{2,1,0:T(8,128)(2,1)S(1)}, u32[]{:S(2)}, u32[]{:S(2)}) collective-permute-start(bf16[2,64,512]{2,1,0:T(8,128)(2,1)S(1)} %stack.1.refs_1_), channel_id=1, source_target_pairs={{48,0},{32,16},{16,32},{0,48},{49,1},{33,17},{17,33},{1,49},{50,2}... | collective-permute-start | bytes 393224 | tf_op jit(solution)/shard_map/ppermute | solution.py:157
  22.1 4.5 %collective-permute-start.9 = (bf16[2,64,512]{2,1,0:T(8,128)(2,1)S(1)}, bf16[2,64,512]{2,1,0:T(8,128)(2,1)S(1)}, u32[]{:S(2)}, u32[]{:S(2)}) collective-permute-start(bf16[2,64,512]{2,1,0:T(8,128)(2,1)S(1)} %collective-permute-done.7.refs_1_), channel_id=1, source_target_pairs={{0,8},{8,0},{1,9},{9,1},{2,10},{10,2},{3,11},{11,3},{4,12},{12,4},... | collective-permute-start | bytes 393224 | tf_op jit(solution)/shard_map/ppermute | solution.py:161
  25.0 2.2 %collective-permute-start.6 = (bf16[2,64,512]{2,1,0:T(8,128)(2,1)S(1)}, bf16[2,64,512]{2,1,0:T(8,128)(2,1)S(1)}, u32[]{:S(2)}, u32[]{:S(2)}) collective-permute-start(bf16[2,64,512]{2,1,0:T(8,128)(2,1)S(1)} %collective-permute-done.5.refs_1_), channel_id=1, source_target_pairs={{0,8},{8,0},{1,9},{9,1},{2,10},{10,2},{3,11},{11,3},{4,12},{12,4},... | collective-permute-start | bytes 393224 | tf_op jit(solution)/shard_map/ppermute | solution.py:161
  26.2 1.5 %collective-permute-start.4 = (bf16[2,64,512]{2,1,0:T(8,128)(2,1)S(1)}, bf16[2,64,512]{2,1,0:T(8,128)(2,1)S(1)}, u32[]{:S(2)}, u32[]{:S(2)}) collective-permute-start(bf16[2,64,512]{2,1,0:T(8,128)(2,1)S(1)} %collective-permute-done.3.refs_1_), channel_id=1, source_target_pairs={{0,8},{8,0},{1,9},{9,1},{2,10},{10,2},{3,11},{11,3},{4,12},{12,4},... | collective-permute-start | bytes 393224 | tf_op jit(solution)/shard_map/ppermute | solution.py:161
  28.2 5.3 %collective-permute-start.10 = (bf16[256,128]{1,0:T(8,128)(2,1)S(1)}, bf16[256,128]{1,0:T(8,128)(2,1)S(1)}, u32[]{:S(2)}, u32[]{:S(2)}) collective-permute-start(bf16[256,128]{1,0:T(8,128)(2,1)S(1)} %half.7.refs_0_), channel_id=1, source_target_pairs={{7,0},{0,1},{1,2},{2,3},{3,4},{4,5},{5,6},{6,7},{15,8},{8,9},{9,10... | collective-permute-start | bytes 196616 | tf_op jit(solution)/shard_map/ppermute | solution.py:138
  29.6 5.6 %collective-permute-start.11 = (bf16[256,128]{1,0:T(8,128)(2,1)S(1)}, bf16[256,128]{1,0:T(8,128)(2,1)S(1)}, u32[]{:S(2)}, u32[]{:S(2)}) collective-permute-start(bf16[256,128]{1,0:T(8,128)(2,1)S(1)} %half.7.refs_0_), channel_id=1, source_target_pairs={{6,0},{7,1},{0,2},{1,3},{2,4},{3,5},{4,6},{5,7},{14,8},{15,9},{8,1... | collective-permute-start | bytes 196616 | tf_op jit(solution)/shard_map/ppermute | solution.py:138
  35.4 2.7 %collective-permute-start.12 = (f32[64,384]{1,0:T(8,128)S(1)}, f32[64,384]{1,0:T(8,128)S(1)}, u32[]{:S(2)}, u32[]{:S(2)}) collective-permute-start(f32[64,384]{1,0:T(8,128)S(1)} %get-tuple-element.26), channel_id=1, source_target_pairs={{0,8},{8,0},{1,9},{9,1},{2,10},{10,2},{3,11},{11,3},{4,12},{12,4},... | collective-permute-start | bytes 294920 | tf_op jit(solution)/shard_map/ppermute | solution.py:161

commit v4 on v3

--- a/solution.py
+++ b/solution.py
@@ -65,19 +65,21 @@
     total_ref[...] = jnp.zeros_like(total_ref)
 
 
-def half_kernel(distance, last, small_ref, own_ref, other_ref, integrals_ref, before_ref, out_ref):
-    slots, batch, _ = own_ref.shape
+def half_kernel(parts, last, small_ref, integrals_ref, before_ref, *refs):
+    *stack_refs, out_ref = refs
+    slots, batch, _ = stack_refs[0].shape
     p_local, _, rows = integrals_ref.shape
     zh, zl, core = lax.axis_index(ZH), lax.axis_index(ZL), lax.axis_index(CORE)
     layers, width = lax.axis_size(ZH), lax.axis_size(X)
-    x = lax.axis_index(X) ^ distance
     near = jnp.where(zl == 0, layers - 1, 1)
     pairs = p_local // 2
     totals = [before_ref[pair] for pair in range(pairs)]
     masks = small_ref[...].astype(jnp.float32)
     entry = lax.broadcasted_iota(jnp.int32, masks.shape, 1)
     column = lax.broadcasted_iota(jnp.int32, (1, 2 * rows), 1) % rows
-    for ref, holder in ((own_ref, core), (other_ref, 1 - core)):
+    for ref, (distance, mine) in zip(stack_refs, parts):
+        x = lax.rem(lax.axis_index(X) + distance, width)
+        holder = core if mine else 1 - core
         for slot in range(slots):
             even = 0 if slot == 0 else 2
             odd = layers - near if slot == 0 else near
@@ -102,6 +104,10 @@
             out_ref[pair] = totals[pair]
 
 
+def turned(index, size):
+    return (index + size // 2) % size
+
+
 def near_kernel(rows_dev, half_ref, previous_ref, left_ref, near_ref):
     rows = half_ref.shape[1]
     core = lax.axis_index(CORE)
@@ -110,7 +116,10 @@
     mine = out_row < rows // 2
     local = jnp.where(mine, out_row, out_row - rows // 2)
     parity = jnp.where(mine, core, 1 - core)
-    wanted = (local // rows_dev) * (2 * rows_dev) + parity * rows_dev + local % rows_dev
+    place = local // rows_dev
+    width = lax.axis_size(X)
+    chip = turned(place // width, lax.axis_size(ZH)) * width + turned(place % width, width)
+    wanted = chip * (2 * rows_dev) + parity * rows_dev + local % rows_dev
     order = (wanted == in_row).astype(jnp.float32).astype(jnp.bfloat16)
     left = lax.dot_general(
         order, half_ref[...], (((1,), (1,)), ((), ())), preferred_element_type=jnp.float32
@@ -151,10 +160,6 @@
         if (core, z % halves) in steps
     ]
     return lax.ppermute(block, (ZH, CORE, ZL), route)
-
-
-def across_x(block, distance):
-    return lax.ppermute(block, X, [(i ^ distance, i) for i in range(lax.axis_size(X))])
 
 
 def other_core(block):
@@ -208,27 +213,34 @@
         name="stack",
     )(window, first, second)
 
-    for distance in (0, 2, 1, 3):
-        own = stack if distance == 0 else across_x(stack, distance)
-        if distance == 2:
-            own, total = lax.optimization_barrier((own, total))
-        last = distance == 3
+    def add_products(total, parts, stacks, last=False, cost=None):
         out = jax.ShapeDtypeStruct((p_local * batch, r_local), jnp.bfloat16) if last else running
-        total = pl.pallas_call(
-            lambda *refs, distance=distance, last=last: half_kernel(distance, last, *refs),
+        return pl.pallas_call(
+            lambda *refs: half_kernel(parts, last, *refs),
             out_shape=out,
-            in_specs=[WHOLE] * 5,
+            in_specs=[WHOLE] * (3 + len(stacks)),
             out_specs=WHOLE,
             compiler_params=params(12),
-            cost_estimate=pl.CostEstimate(flops=1, bytes_accessed=4096, transcendentals=0)
-            if distance == 0
-            else pl.CostEstimate(
-                flops=2 * batch * WIN * 4 * p_local * r_local,
-                bytes_accessed=by_column.size // 2,
+            cost_estimate=cost
+            or pl.CostEstimate(
+                flops=2 * batch * WIN * 2 * len(stacks) * p_local * r_local,
+                bytes_accessed=by_column.size * len(stacks) // 4,
                 transcendentals=0,
             ),
             name="half",
-        )(small, own, other_core(own), by_column, total)
+        )(small, by_column, total, *stacks)
+
+    brief = pl.CostEstimate(flops=1, bytes_accessed=4096, transcendentals=0)
+    total = add_products(total, [(0, True)], [stack], cost=brief)
+    parts, stacks = [(0, False)], [other_core(stack)]
+    for distance in (2, 1, 3):
+        own = from_behind(stack, X, -distance)
+        if distance == 2:
+            own, total = lax.optimization_barrier((own, total))
+        parts += [(distance, True), (distance, False)]
+        stacks += [own, other_core(own)]
+        total = add_products(total, parts, stacks, last=distance == 3)
+        parts, stacks = [], []
     half = total
 
     previous = from_behind(half, ROW, 1)
@@ -256,8 +268,16 @@
         name="bands",
     )(left, near, farther)
     chip_sum = kept + other_core(sent)
+    layers, width = lax.axis_size(ZH), lax.axis_size(X)
+    order = [
+        turned(zh, layers) * width + turned(x, width) for zh in range(layers) for x in range(width)
+    ]
     pieces = lax.all_to_all(
-        chip_sum.reshape(chips, rows_dev, BANDS * r_local), (ZH, X), 0, 0
+        chip_sum.reshape(chips, rows_dev, BANDS * r_local),
+        (ZH, X),
+        0,
+        0,
+        axis_index_groups=[order],
     )
     return jnp.sum(pieces, axis=0)
 

time: 53.6 us -> 50.4 us (0.940)
  starting transfers between devices: 23.4 us -> 20.4 us
  blocking collectives: 14.3 us -> 11.8 us
  waiting for transfers between devices: 6.69 us -> 8.99 us
    ppermute x2 -> x5, waiting for transfers between devices: 2.67 us -> 8.03 us  [from_behind(): return lax.ppermute(block, axis, route)]
    ppermute x2 -> x5, starting transfers between devices: 4 us -> 8.27 us  [from_behind(): return lax.ppermute(block, axis, route)]
    ppermute x3 -> x0, starting transfers between devices: 3.68 us -> none  [across_x(): lax.ppermute(block, X, [(i ^ distance, i) for i in range(lax.axis_size(X))])]
    ppermute x6, starting transfers between devices: 8.75 us -> 5.17 us  [other_core(): return lax.ppermute(block, CORE, [(0, 1), (1, 0)])]
    ppermute x3 -> x0, waiting for transfers between devices: 2.88 us -> none  [across_x(): lax.ppermute(block, X, [(i ^ distance, i) for i in range(lax.axis_size(X))])]
    all_to_all x1, blocking collectives: 14.3 us -> 11.8 us  [per_device(): lax.all_to_all(chip_sum.reshape(chips, rows_dev, BANDS * r_local), (ZH, X...]
    unnamed x4 -> x2, local copies, waits for them, and re-layouts: 3.32 us -> 3.32 us
  transfers between devices with their start and end apart: 13 -> 13, of which waited for: 6 -> 6; matrix products, arithmetic and copies ran while one was open for 3% -> 3% of each run, Pallas kernels for 3% -> 4%
where the time goes in v4:
time: 50.4 us; the launch traced here: 49.9 us
  starting transfers between devices  20.4 us (40%)
  blocking collectives  11.8 us (23%)
  waiting for transfers between devices  8.99 us (18%)
  local copies, waits for them, and re-layouts  4.26 us (8%)
  Pallas kernels  2.95 us (6%)
  other arithmetic  1.33 us (3%)
    all_to_all x1, blocking collectives, per_device(): lax.all_to_all(chip_sum.reshape(chips, rows_dev, BANDS * r_local), (ZH, X...  11.8 us
    ppermute x5, starting transfers between devices, from_behind(): return lax.ppermute(block, axis, route)  8.27 us
    ppermute x5, waiting for transfers between devices, from_behind(): return lax.ppermute(block, axis, route)  8.03 us
    ppermute x2, starting transfers between devices, along_z(): return lax.ppermute(block, (ZH, CORE, ZL), route)  7 us
    ppermute x6, starting transfers between devices, other_core(): return lax.ppermute(block, CORE, [(0, 1), (1, 0)])  5.17 us
    unnamed x2, local copies, waits for them, and re-layouts  3.32 us
    pallas_call x4, Pallas kernels, add_products(): pl.pallas_call(lambda *refs: half_kernel(parts, last, *refs), out_shape=o...  1.99 us
  transfers between devices with their start and end apart: 13, of which 6 were waited for; matrix products, arithmetic and copies ran while one was open for 3% of the time, Pallas kernels for 4%

profile of v4, /device:TPU:1, one launch (start us, length us, event | category | flops | bytes accessed | tf_op | source)
XLA Modules:
  0.0 49.9 jit_solution(6068775574410779524)
XLA Ops:
  0.0 3.2 %collective-permute-start = (bf16[250,256]{1,0:T(8,128)(2,1)}, bf16[250,256]{1,0:T(8,128)(2,1)S(1)}, u32[]{:S(2)}, u32[]{:S(2)}) collective-permute-start(bf16[250,256]{1,0:T(8,128)(2,1)} %param.6), channel_id=1, source_target_pairs={{0,8},{8,0},{1,9},{9,1},{2,10},{10,2},{3,11},{11,3},{4,12},{12,4},... | collective-permute-start | bytes 384008 | tf_op jit(solution)/shard_map/ppermute | solution.py:166
  3.2 0.9 %pad.9.refs_1_ = bf16[256,256]{1,0:T(8,128)(2,1)S(1)} pad(bf16[250,256]{1,0:T(8,128)(2,1)} %param.6, bf16[]{:T(256)} %constant.4.clone.1), padding=0_6x0_0 | pad | bytes 259074 | tf_op jit(solution)/shard_map/jit(_pad)/pad | solution.py:184
  4.2 0.7 %pad_add_fusion.refs_0_ = s32[3,64]{1,0:T(4,128)S(1)} fusion(s32[2,16]{1,0:T(2,128)} %bitcast.8, s32[1,64]{1,0:T(1,128)} %bitcast.9), kind=kLoop, calls=%fused_computation | loop fusion | flops 192 | bytes 1152 | tf_op jit(solution)/shard_map/concatenate | solution.py:181
  4.9 0.4 pick.1.window_ref
  5.3 3.9 %collective-permute-start.1 = (bf16[64,512]{1,0:T(8,128)(2,1)S(1)}, bf16[64,512]{1,0:T(8,128)(2,1)S(1)}, u32[]{:S(2)}, u32[]{:S(2)}) collective-permute-start(bf16[64,512]{1,0:T(8,128)(2,1)S(1)} %pick.1.window_ref), channel_id=1, source_target_pairs={{132,0},{204,8},{128,4},{72,12},{196,64},{12,72},{192,68},{136,76}... | collective-permute-start | bytes 196616 | tf_op jit(solution)/shard_map/ppermute | solution.py:162
  9.2 3.1 %collective-permute-start.2 = (bf16[64,512]{1,0:T(8,128)(2,1)S(1)}, bf16[64,512]{1,0:T(8,128)(2,1)S(1)}, u32[]{:S(2)}, u32[]{:S(2)}) collective-permute-start(bf16[64,512]{1,0:T(8,128)(2,1)S(1)} %pick.1.window_ref), channel_id=1, source_target_pairs={{72,8},{204,12},{136,72},{12,76},{200,136},{76,140},{8,200},{140,2... | collective-permute-start | bytes 196616 | tf_op jit(solution)/shard_map/ppermute | solution.py:162
  12.3 3.3 %copy-done = bf16[4,128,8000]{1,2,0:T(8,128)(2,1)S(1)} copy-done((bf16[4,128,8000]{1,2,0:T(8,128)(2,1)S(1)}, bf16[4,128,8000]{1,2,0:T(8,128)(2,1)}, u32[]{:S(2)}) %copy-start) | copy-done | bytes 8192024
  15.7 2.8 %collective-permute-start.3 = (bf16[2,64,512]{2,1,0:T(8,128)(2,1)S(1)}, bf16[2,64,512]{2,1,0:T(8,128)(2,1)S(1)}, u32[]{:S(2)}, u32[]{:S(2)}) collective-permute-start(bf16[2,64,512]{2,1,0:T(8,128)(2,1)S(1)} %stack.1.refs_3_), channel_id=1, source_target_pairs={{32,0},{48,16},{0,32},{16,48},{33,1},{49,17},{1,33},{17,49},{34,2}... | collective-permute-start | bytes 393224 | tf_op jit(solution)/shard_map/ppermute | solution.py:147
  18.5 0.9 %collective-permute-start.6 = (bf16[2,64,512]{2,1,0:T(8,128)(2,1)S(1)}, bf16[2,64,512]{2,1,0:T(8,128)(2,1)S(1)}, u32[]{:S(2)}, u32[]{:S(2)}) collective-permute-start(bf16[2,64,512]{2,1,0:T(8,128)(2,1)S(1)} %stack.1.refs_3_), channel_id=1, source_target_pairs={{16,0},{32,16},{48,32},{0,48},{17,1},{33,17},{49,33},{1,49},{18,2}... | collective-permute-start | bytes 393224 | tf_op jit(solution)/shard_map/ppermute | solution.py:147
  19.4 0.6 %collective-permute-start.8 = (bf16[2,64,512]{2,1,0:T(8,128)(2,1)S(1)}, bf16[2,64,512]{2,1,0:T(8,128)(2,1)S(1)}, u32[]{:S(2)}, u32[]{:S(2)}) collective-permute-start(bf16[2,64,512]{2,1,0:T(8,128)(2,1)S(1)} %stack.1.refs_3_), channel_id=1, source_target_pairs={{48,0},{0,16},{16,32},{32,48},{49,1},{1,17},{17,33},{33,49},{50,2}... | collective-permute-start | bytes 393224 | tf_op jit(solution)/shard_map/ppermute | solution.py:147
  20.3 2.0 %collective-permute-done.3.refs_4_ = bf16[2,64,512]{2,1,0:T(8,128)(2,1)S(1)} collective-permute-done((bf16[2,64,512]{2,1,0:T(8,128)(2,1)S(1)}, bf16[2,64,512]{2,1,0:T(8,128)(2,1)S(1)}, u32[]{:S(2)}, u32[]{:S(2)}) %collective-permute-start.3) | collective-permute-done | bytes 131104 | tf_op jit(solution)/shard_map/ppermute | solution.py:147
  22.3 2.6 %collective-permute-done.6.refs_3_ = bf16[2,64,512]{2,1,0:T(8,128)(2,1)S(1)} collective-permute-done((bf16[2,64,512]{2,1,0:T(8,128)(2,1)S(1)}, bf16[2,64,512]{2,1,0:T(8,128)(2,1)S(1)}, u32[]{:S(2)}, u32[]{:S(2)}) %collective-permute-start.6) | collective-permute-done | bytes 131104 | tf_op jit(solution)/shard_map/ppermute | solution.py:147
  24.9 0.8 %collective-permute-done.8.refs_3_ = bf16[2,64,512]{2,1,0:T(8,128)(2,1)S(1)} collective-permute-done((bf16[2,64,512]{2,1,0:T(8,128)(2,1)S(1)}, bf16[2,64,512]{2,1,0:T(8,128)(2,1)S(1)}, u32[]{:S(2)}, u32[]{:S(2)}) %collective-permute-start.8) | collective-permute-done | bytes 131104 | tf_op jit(solution)/shard_map/ppermute | solution.py:147
  26.1 0.7 %half.5.refs_2_ = f32[2,64,256]{2,1,0:T(8,128)S(1)} custom-call(s32[3,64]{1,0:T(4,128)S(1)} %pad_add_fusion.refs_0_, bf16[4,8000,128]{2,1,0:T(8,128)(2,1)S(1)} %bitcast.5, f32[2,64,256]{2,1,0:T(8,128)S(1)} %half.4.refs_2_, bf16[2,64,512]{2,1,0:T(8,128)(2,1)S(1)} %collective-permute-done.4.refs_3_, bf16[2,64,512]{2,1,0:T(8,128)(2,1)S(1)} %collective-permute-done.3.refs_4_, ...), custom_call_target="tpu_custom_call" | custom-call | flops 201326592 | bytes 3072000 | tf_op jit(solution)/shard_map/half/pallas_call | solution.py:218
  26.8 0.5 %half.6.refs_2_ = f32[2,64,256]{2,1,0:T(8,128)S(1)} custom-call(s32[3,64]{1,0:T(4,128)S(1)} %pad_add_fusion.refs_0_, bf16[4,8000,128]{2,1,0:T(8,128)(2,1)S(1)} %bitcast.6, f32[2,64,256]{2,1,0:T(8,128)S(1)} %half.5.refs_2_, bf16[2,64,512]{2,1,0:T(8,128)(2,1)S(1)} %collective-permute-done.6.refs_3_, bf16[2,64,512]{2,1,0:T(8,128)(2,1)S(1)} %collective-permute-done.7.refs_4_), custom_call_target="tpu_custom_call" | custom-call | flops 134217728 | bytes 2048000 | tf_op jit(solution)/shard_map/half/pallas_call | solution.py:218
  27.3 0.5 %half.7.refs_0_ = bf16[256,128]{1,0:T(8,128)(2,1)S(1)} custom-call(s32[3,64]{1,0:T(4,128)S(1)} %pad_add_fusion.refs_0_, bf16[4,8000,128]{2,1,0:T(8,128)(2,1)S(1)} %bitcast.7, f32[2,64,256]{2,1,0:T(8,128)S(1)} %half.6.refs_2_, bf16[2,64,512]{2,1,0:T(8,128)(2,1)S(1)} %collective-permute-done.8.refs_3_, bf16[2,64,512]{2,1,0:T(8,128)(2,1)S(1)} %collective-permute-done.9.refs_4_), custom_call_target="tpu_custom_call" | custom-call | flops 134217728 | bytes 2048000 | tf_op jit(solution)/shard_map/half/pallas_call | solution.py:218
  27.8 1.4 %collective-permute-start.10 = (bf16[256,128]{1,0:T(8,128)(2,1)S(1)}, bf16[256,128]{1,0:T(8,128)(2,1)S(1)}, u32[]{:S(2)}, u32[]{:S(2)}) collective-permute-start(bf16[256,128]{1,0:T(8,128)(2,1)S(1)} %half.7.refs_0_), channel_id=1, source_target_pairs={{7,0},{0,1},{1,2},{2,3},{3,4},{4,5},{5,6},{6,7},{15,8},{8,9},{9,10... | collective-permute-start | bytes 196616 | tf_op jit(solution)/shard_map/ppermute | solution.py:147
  29.2 2.6 %collective-permute-start.11 = (bf16[256,128]{1,0:T(8,128)(2,1)S(1)}, bf16[256,128]{1,0:T(8,128)(2,1)S(1)}, u32[]{:S(2)}, u32[]{:S(2)}) collective-permute-start(bf16[256,128]{1,0:T(8,128)(2,1)S(1)} %half.7.refs_0_), channel_id=1, source_target_pairs={{6,0},{7,1},{0,2},{1,3},{2,4},{3,5},{4,6},{5,7},{14,8},{15,9},{8,1... | collective-permute-start | bytes 196616 | tf_op jit(solution)/shard_map/ppermute | solution.py:147
  31.8 1.9 %collective-permute-done.10.refs_1_ = bf16[256,128]{1,0:T(8,128)(2,1)S(1)} collective-permute-done((bf16[256,128]{1,0:T(8,128)(2,1)S(1)}, bf16[256,128]{1,0:T(8,128)(2,1)S(1)}, u32[]{:S(2)}, u32[]{:S(2)}) %collective-permute-start.10) | collective-permute-done | bytes 65568 | tf_op jit(solution)/shard_map/ppermute | solution.py:147
  34.0 0.8 %collective-permute-done.11.farther_ref = bf16[256,128]{1,0:T(8,128)(2,1)S(1)} collective-permute-done((bf16[256,128]{1,0:T(8,128)(2,1)S(1)}, bf16[256,128]{1,0:T(8,128)(2,1)S(1)}, u32[]{:S(2)}, u32[]{:S(2)}) %collective-permute-start.11) | collective-permute-done | bytes 65568 | tf_op jit(solution)/shard_map/ppermute | solution.py:147
  35.0 1.5 %collective-permute-start.12 = (f32[64,384]{1,0:T(8,128)S(1)}, f32[64,384]{1,0:T(8,128)S(1)}, u32[]{:S(2)}, u32[]{:S(2)}) collective-permute-start(f32[64,384]{1,0:T(8,128)S(1)} %get-tuple-element.26), channel_id=1, source_target_pairs={{0,8},{8,0},{1,9},{9,1},{2,10},{10,2},{3,11},{11,3},{4,12},{12,4},... | collective-permute-start | bytes 294920 | tf_op jit(solution)/shard_map/ppermute | solution.py:166
  36.5 0.9 %collective-permute-done.12 = f32[64,384]{1,0:T(8,128)S(1)} collective-permute-done((f32[64,384]{1,0:T(8,128)S(1)}, f32[64,384]{1,0:T(8,128)S(1)}, u32[]{:S(2)}, u32[]{:S(2)}) %collective-permute-start.12) | collective-permute-done | bytes 98336 | tf_op jit(solution)/shard_map/ppermute | solution.py:166
  37.5 11.8 %all_to_all.5 = f32[16,4,384]{2,1,0:T(4,128)S(1)} all-to-all(f32[16,4,384]{2,1,0:T(4,128)S(1)} %reshape.3), channel_id=1, replica_groups={{160,176,128,144,224,240,192,208,32,48,0,16,96,112,64,80},{161,177,129,..., dimensions={0} | all-to-all | bytes 196608 | tf_op jit(solution)/shard_map/all_to_all | solution.py:275
  49.3 0.6 %reduce_sum.9 = f32[4,384]{1,0:T(4,128)} reduce(f32[16,4,384]{2,1,0:T(4,128)S(1)} %all_to_all.5, f32[]{:T(128)} %constant.5.clone.1), dimensions={0}, to_apply=%region_0.1 | reduce | flops 23040 | bytes 104452 | tf_op jit(solution)/shard_map/reduce_sum | solution.py:282
  (19 shorter events, 1.3 us)
Async XLA Ops:
  0.0 4.9 %collective-permute-start = (bf16[250,256]{1,0:T(8,128)(2,1)}, bf16[250,256]{1,0:T(8,128)(2,1)S(1)}, u32[]{:S(2)}, u32[]{:S(2)}) collective-permute-start(bf16[250,256]{1,0:T(8,128)(2,1)} %param.6), channel_id=1, source_target_pairs={{0,8},{8,0},{1,9},{9,1},{2,10},{10,2},{3,11},{11,3},{4,12},{12,4},... | collective-permute-start | bytes 384008 | tf_op jit(solution)/shard_map/ppermute | solution.py:166
  5.3 10.3 %collective-permute-start.1 = (bf16[64,512]{1,0:T(8,128)(2,1)S(1)}, bf16[64,512]{1,0:T(8,128)(2,1)S(1)}, u32[]{:S(2)}, u32[]{:S(2)}) collective-permute-start(bf16[64,512]{1,0:T(8,128)(2,1)S(1)} %pick.1.window_ref), channel_id=1, source_target_pairs={{132,0},{204,8},{128,4},{72,12},{196,64},{12,72},{192,68},{136,76}... | collective-permute-start | bytes 196616 | tf_op jit(solution)/shard_map/ppermute | solution.py:162
  9.2 6.4 %collective-permute-start.2 = (bf16[64,512]{1,0:T(8,128)(2,1)S(1)}, bf16[64,512]{1,0:T(8,128)(2,1)S(1)}, u32[]{:S(2)}, u32[]{:S(2)}) collective-permute-start(bf16[64,512]{1,0:T(8,128)(2,1)S(1)} %pick.1.window_ref), channel_id=1, source_target_pairs={{72,8},{204,12},{136,72},{12,76},{200,136},{76,140},{8,200},{140,2... | collective-permute-start | bytes 196616 | tf_op jit(solution)/shard_map/ppermute | solution.py:162
  12.3 3.3 %copy-start = (bf16[4,128,8000]{1,2,0:T(8,128)(2,1)S(1)}, bf16[4,128,8000]{1,2,0:T(8,128)(2,1)}, u32[]{:S(2)}) copy-start(bf16[4,128,8000]{1,2,0:T(8,128)(2,1)} %param.4) | copy-start | bytes 24576004
  15.7 6.6 %collective-permute-start.3 = (bf16[2,64,512]{2,1,0:T(8,128)(2,1)S(1)}, bf16[2,64,512]{2,1,0:T(8,128)(2,1)S(1)}, u32[]{:S(2)}, u32[]{:S(2)}) collective-permute-start(bf16[2,64,512]{2,1,0:T(8,128)(2,1)S(1)} %stack.1.refs_3_), channel_id=1, source_target_pairs={{32,0},{48,16},{0,32},{16,48},{33,1},{49,17},{1,33},{17,49},{34,2}... | collective-permute-start | bytes 393224 | tf_op jit(solution)/shard_map/ppermute | solution.py:147
  18.5 6.4 %collective-permute-start.6 = (bf16[2,64,512]{2,1,0:T(8,128)(2,1)S(1)}, bf16[2,64,512]{2,1,0:T(8,128)(2,1)S(1)}, u32[]{:S(2)}, u32[]{:S(2)}) collective-permute-start(bf16[2,64,512]{2,1,0:T(8,128)(2,1)S(1)} %stack.1.refs_3_), channel_id=1, source_target_pairs={{16,0},{32,16},{48,32},{0,48},{17,1},{33,17},{49,33},{1,49},{18,2}... | collective-permute-start | bytes 393224 | tf_op jit(solution)/shard_map/ppermute | solution.py:147
  19.4 6.3 %collective-permute-start.8 = (bf16[2,64,512]{2,1,0:T(8,128)(2,1)S(1)}, bf16[2,64,512]{2,1,0:T(8,128)(2,1)S(1)}, u32[]{:S(2)}, u32[]{:S(2)}) collective-permute-start(bf16[2,64,512]{2,1,0:T(8,128)(2,1)S(1)} %stack.1.refs_3_), channel_id=1, source_target_pairs={{48,0},{0,16},{16,32},{32,48},{49,1},{1,17},{17,33},{33,49},{50,2}... | collective-permute-start | bytes 393224 | tf_op jit(solution)/shard_map/ppermute | solution.py:147
  20.0 6.1 %collective-permute-start.4 = (bf16[2,64,512]{2,1,0:T(8,128)(2,1)S(1)}, bf16[2,64,512]{2,1,0:T(8,128)(2,1)S(1)}, u32[]{:S(2)}, u32[]{:S(2)}) collective-permute-start(bf16[2,64,512]{2,1,0:T(8,128)(2,1)S(1)} %stack.1.refs_3_), channel_id=1, source_target_pairs={{0,8},{8,0},{1,9},{9,1},{2,10},{10,2},{3,11},{11,3},{4,12},{12,4},... | collective-permute-start | bytes 393224 | tf_op jit(solution)/shard_map/ppermute | solution.py:166
  22.3 3.8 %collective-permute-start.5 = (bf16[2,64,512]{2,1,0:T(8,128)(2,1)S(1)}, bf16[2,64,512]{2,1,0:T(8,128)(2,1)S(1)}, u32[]{:S(2)}, u32[]{:S(2)}) collective-permute-start(bf16[2,64,512]{2,1,0:T(8,128)(2,1)S(1)} %collective-permute-done.3.refs_4_), channel_id=1, source_target_pairs={{0,8},{8,0},{1,9},{9,1},{2,10},{10,2},{3,11},{11,3},{4,12},{12,4},... | collective-permute-start | bytes 393224 | tf_op jit(solution)/shard_map/ppermute | solution.py:166
  24.9 1.9 %collective-permute-start.7 = (bf16[2,64,512]{2,1,0:T(8,128)(2,1)S(1)}, bf16[2,64,512]{2,1,0:T(8,128)(2,1)S(1)}, u32[]{:S(2)}, u32[]{:S(2)}) collective-permute-start(bf16[2,64,512]{2,1,0:T(8,128)(2,1)S(1)} %collective-permute-done.6.refs_3_), channel_id=1, source_target_pairs={{0,8},{8,0},{1,9},{9,1},{2,10},{10,2},{3,11},{11,3},{4,12},{12,4},... | collective-permute-start | bytes 393224 | tf_op jit(solution)/shard_map/ppermute | solution.py:166
  25.7 1.6 %collective-permute-start.9 = (bf16[2,64,512]{2,1,0:T(8,128)(2,1)S(1)}, bf16[2,64,512]{2,1,0:T(8,128)(2,1)S(1)}, u32[]{:S(2)}, u32[]{:S(2)}) collective-permute-start(bf16[2,64,512]{2,1,0:T(8,128)(2,1)S(1)} %collective-permute-done.8.refs_3_), channel_id=1, source_target_pairs={{0,8},{8,0},{1,9},{9,1},{2,10},{10,2},{3,11},{11,3},{4,12},{12,4},... | collective-permute-start | bytes 393224 | tf_op jit(solution)/shard_map/ppermute | solution.py:166
  27.8 5.9 %collective-permute-start.10 = (bf16[256,128]{1,0:T(8,128)(2,1)S(1)}, bf16[256,128]{1,0:T(8,128)(2,1)S(1)}, u32[]{:S(2)}, u32[]{:S(2)}) collective-permute-start(bf16[256,128]{1,0:T(8,128)(2,1)S(1)} %half.7.refs_0_), channel_id=1, source_target_pairs={{7,0},{0,1},{1,2},{2,3},{3,4},{4,5},{5,6},{6,7},{15,8},{8,9},{9,10... | collective-permute-start | bytes 196616 | tf_op jit(solution)/shard_map/ppermute | solution.py:147
  29.2 5.6 %collective-permute-start.11 = (bf16[256,128]{1,0:T(8,128)(2,1)S(1)}, bf16[256,128]{1,0:T(8,128)(2,1)S(1)}, u32[]{:S(2)}, u32[]{:S(2)}) collective-permute-start(bf16[256,128]{1,0:T(8,128)(2,1)S(1)} %half.7.refs_0_), channel_id=1, source_target_pairs={{6,0},{7,1},{0,2},{1,3},{2,4},{3,5},{4,6},{5,7},{14,8},{15,9},{8,1... | collective-permute-start | bytes 196616 | tf_op jit(solution)/shard_map/ppermute | solution.py:147
  35.0 2.5 %collective-permute-start.12 = (f32[64,384]{1,0:T(8,128)S(1)}, f32[64,384]{1,0:T(8,128)S(1)}, u32[]{:S(2)}, u32[]{:S(2)}) collective-permute-start(f32[64,384]{1,0:T(8,128)S(1)} %get-tuple-element.26), channel_id=1, source_target_pairs={{0,8},{8,0},{1,9},{9,1},{2,10},{10,2},{3,11},{11,3},{4,12},{12,4},... | collective-permute-start | bytes 294920 | tf_op jit(solution)/shard_map/ppermute | solution.py:166

commit v5 on v4

--- a/solution.py
+++ b/solution.py
@@ -191,19 +191,20 @@
         name="pick",
     )(small, padded, other_coefficients)
 
-    by_column, window = lax.optimization_barrier((jnp.swapaxes(integrals, 1, 2), window))
-    second = along_z(window, {(1, 0): 2, (1, 1): -2})
-    first = along_z(window, {(0, 0): -3, (0, 1): 3, (1, 0): -1, (1, 1): 1})
+    by_column = jnp.swapaxes(integrals, 1, 2)
     running = jax.ShapeDtypeStruct((p_local // 2, batch, 2 * r_local), jnp.float32)
     total = pl.pallas_call(
         stage_kernel,
         out_shape=running,
-        in_specs=[WHOLE],
+        in_specs=[pl.BlockSpec(memory_space=pl.ANY)],
         out_specs=WHOLE,
-        compiler_params=params(12),
+        compiler_params=params(52),
         name="stage",
     )(by_column)
-    first, by_column, total = lax.optimization_barrier((first, by_column, total))
+    window, total = lax.optimization_barrier((window, total))
+    second = along_z(window, {(1, 0): 2, (1, 1): -2})
+    first = along_z(window, {(0, 0): -3, (0, 1): 3, (1, 0): -1, (1, 1): 1})
+    first, window = lax.optimization_barrier((first, window))
     stack = pl.pallas_call(
         stack_kernel,
         out_shape=jax.ShapeDtypeStruct((2, batch, WIN), jnp.bfloat16),

time: 50.4 us -> 49.2 us (0.976)
  local copies, waits for them, and re-layouts: 4.26 us -> 0.95 us
  waiting for transfers between devices: 8.99 us -> 11.6 us
  other arithmetic: 1.33 us -> 0.65 us
    unnamed x2 -> x6, local copies, waits for them, and re-layouts: 3.32 us -> 0.01 us
    ppermute x2, waiting for transfers between devices: 0.01 us -> 2.81 us  [along_z(): return lax.ppermute(block, (ZH, CORE, ZL), route)]
    concatenate x1, other arithmetic: 0.69 us -> 0.01 us  [per_device(): jnp.concatenate([occ_index[None, :], jnp.pad(mask, ((0, 0), (0, batch - m...]
  transfers between devices with their start and end apart: 13 -> 13, of which waited for: 6 -> 8; matrix products, arithmetic and copies ran while one was open for 3% -> 2% of each run, Pallas kernels for 4% -> 4%
where the time goes in v5:
time: 49.2 us; the launch traced here: 49 us
  starting transfers between devices  20.5 us (42%)
  blocking collectives  12.2 us (25%)
  waiting for transfers between devices  11.6 us (24%)
  Pallas kernels  2.94 us (6%)
  local copies, waits for them, and re-layouts  0.95 us (2%)
  other arithmetic  0.65 us (1%)
    all_to_all x1, blocking collectives, per_device(): lax.all_to_all(chip_sum.reshape(chips, rows_dev, BANDS * r_local), (ZH, X...  12.2 us
    ppermute x5, starting transfers between devices, from_behind(): return lax.ppermute(block, axis, route)  8.3 us
    ppermute x5, waiting for transfers between devices, from_behind(): return lax.ppermute(block, axis, route)  7.6 us
    ppermute x2, starting transfers between devices, along_z(): return lax.ppermute(block, (ZH, CORE, ZL), route)  7.09 us
    ppermute x6, starting transfers between devices, other_core(): return lax.ppermute(block, CORE, [(0, 1), (1, 0)])  5.13 us
    ppermute x2, waiting for transfers between devices, along_z(): return lax.ppermute(block, (ZH, CORE, ZL), route)  2.81 us
    pallas_call x4, Pallas kernels, add_products(): pl.pallas_call(lambda *refs: half_kernel(parts, last, *refs), out_shape=o...  2 us
    ppermute x6, waiting for transfers between devices, other_core(): return lax.ppermute(block, CORE, [(0, 1), (1, 0)])  1.18 us
  transfers between devices with their start and end apart: 13, of which 8 were waited for; matrix products, arithmetic and copies ran while one was open for 2% of the time, Pallas kernels for 4%

profile of v5, /device:TPU:1, one launch (start us, length us, event | category | flops | bytes accessed | tf_op | source)
XLA Modules:
  0.0 49.0 jit_solution(7009167696849759284)
XLA Ops:
  0.0 3.2 %collective-permute-start = (bf16[250,256]{1,0:T(8,128)(2,1)}, bf16[250,256]{1,0:T(8,128)(2,1)S(1)}, u32[]{:S(2)}, u32[]{:S(2)}) collective-permute-start(bf16[250,256]{1,0:T(8,128)(2,1)} %param.6), channel_id=1, source_target_pairs={{0,8},{8,0},{1,9},{9,1},{2,10},{10,2},{3,11},{11,3},{4,12},{12,4},... | collective-permute-start | bytes 384008 | tf_op jit(solution)/shard_map/ppermute | solution.py:166
  3.2 0.9 %pad.9.refs_1_ = bf16[256,256]{1,0:T(8,128)(2,1)S(1)} pad(bf16[250,256]{1,0:T(8,128)(2,1)} %param.6, bf16[]{:T(256)} %constant.4.clone.1), padding=0_6x0_0 | pad | bytes 259074 | tf_op jit(solution)/shard_map/jit(_pad)/pad | solution.py:184
  4.4 0.4 pick.1.window_ref
  4.9 4.0 %collective-permute-start.1 = (bf16[64,512]{1,0:T(8,128)(2,1)S(1)}, bf16[64,512]{1,0:T(8,128)(2,1)S(1)}, u32[]{:S(2)}, u32[]{:S(2)}) collective-permute-start(bf16[64,512]{1,0:T(8,128)(2,1)S(1)} %pick.1.window_ref), channel_id=1, source_target_pairs={{132,0},{204,8},{128,4},{72,12},{196,64},{12,72},{192,68},{136,76}... | collective-permute-start | bytes 196616 | tf_op jit(solution)/shard_map/ppermute | solution.py:162
  8.9 3.1 %collective-permute-start.2 = (bf16[64,512]{1,0:T(8,128)(2,1)S(1)}, bf16[64,512]{1,0:T(8,128)(2,1)S(1)}, u32[]{:S(2)}, u32[]{:S(2)}) collective-permute-start(bf16[64,512]{1,0:T(8,128)(2,1)S(1)} %pick.1.window_ref), channel_id=1, source_target_pairs={{72,8},{204,12},{136,72},{12,76},{200,136},{76,140},{8,200},{140,2... | collective-permute-start | bytes 196616 | tf_op jit(solution)/shard_map/ppermute | solution.py:162
  12.0 2.8 %collective-permute-done.2.second_ref = bf16[64,512]{1,0:T(8,128)(2,1)S(1)} collective-permute-done((bf16[64,512]{1,0:T(8,128)(2,1)S(1)}, bf16[64,512]{1,0:T(8,128)(2,1)S(1)}, u32[]{:S(2)}, u32[]{:S(2)}) %collective-permute-start.2) | collective-permute-done | bytes 65568 | tf_op jit(solution)/shard_map/ppermute | solution.py:162
  14.8 2.8 %collective-permute-start.3 = (bf16[2,64,512]{2,1,0:T(8,128)(2,1)S(1)}, bf16[2,64,512]{2,1,0:T(8,128)(2,1)S(1)}, u32[]{:S(2)}, u32[]{:S(2)}) collective-permute-start(bf16[2,64,512]{2,1,0:T(8,128)(2,1)S(1)} %stack.1.refs_3_), channel_id=1, source_target_pairs={{32,0},{48,16},{0,32},{16,48},{33,1},{49,17},{1,33},{17,49},{34,2}... | collective-permute-start | bytes 393224 | tf_op jit(solution)/shard_map/ppermute | solution.py:147
  17.6 0.9 %collective-permute-start.6 = (bf16[2,64,512]{2,1,0:T(8,128)(2,1)S(1)}, bf16[2,64,512]{2,1,0:T(8,128)(2,1)S(1)}, u32[]{:S(2)}, u32[]{:S(2)}) collective-permute-start(bf16[2,64,512]{2,1,0:T(8,128)(2,1)S(1)} %stack.1.refs_3_), channel_id=1, source_target_pairs={{16,0},{32,16},{48,32},{0,48},{17,1},{33,17},{49,33},{1,49},{18,2}... | collective-permute-start | bytes 393224 | tf_op jit(solution)/shard_map/ppermute | solution.py:147
  18.5 0.6 %collective-permute-start.8 = (bf16[2,64,512]{2,1,0:T(8,128)(2,1)S(1)}, bf16[2,64,512]{2,1,0:T(8,128)(2,1)S(1)}, u32[]{:S(2)}, u32[]{:S(2)}) collective-permute-start(bf16[2,64,512]{2,1,0:T(8,128)(2,1)S(1)} %stack.1.refs_3_), channel_id=1, source_target_pairs={{48,0},{0,16},{16,32},{32,48},{49,1},{1,17},{17,33},{33,49},{50,2}... | collective-permute-start | bytes 393224 | tf_op jit(solution)/shard_map/ppermute | solution.py:147
  19.4 1.8 %collective-permute-done.3.refs_4_ = bf16[2,64,512]{2,1,0:T(8,128)(2,1)S(1)} collective-permute-done((bf16[2,64,512]{2,1,0:T(8,128)(2,1)S(1)}, bf16[2,64,512]{2,1,0:T(8,128)(2,1)S(1)}, u32[]{:S(2)}, u32[]{:S(2)}) %collective-permute-start.3) | collective-permute-done | bytes 131104 | tf_op jit(solution)/shard_map/ppermute | solution.py:147
  21.2 2.5 %collective-permute-done.6.refs_3_ = bf16[2,64,512]{2,1,0:T(8,128)(2,1)S(1)} collective-permute-done((bf16[2,64,512]{2,1,0:T(8,128)(2,1)S(1)}, bf16[2,64,512]{2,1,0:T(8,128)(2,1)S(1)}, u32[]{:S(2)}, u32[]{:S(2)}) %collective-permute-start.6) | collective-permute-done | bytes 131104 | tf_op jit(solution)/shard_map/ppermute | solution.py:147
  23.7 0.7 %collective-permute-done.8.refs_3_ = bf16[2,64,512]{2,1,0:T(8,128)(2,1)S(1)} collective-permute-done((bf16[2,64,512]{2,1,0:T(8,128)(2,1)S(1)}, bf16[2,64,512]{2,1,0:T(8,128)(2,1)S(1)}, u32[]{:S(2)}, u32[]{:S(2)}) %collective-permute-start.8) | collective-permute-done | bytes 131104 | tf_op jit(solution)/shard_map/ppermute | solution.py:147
  24.6 0.7 %half.5.refs_2_ = f32[2,64,256]{2,1,0:T(8,128)S(1)} custom-call(s32[3,64]{1,0:T(4,128)S(1)} %pad_add_fusion.refs_0_, bf16[4,8000,128]{2,1,0:T(8,128)(2,1)S(1)} %bitcast.5, f32[2,64,256]{2,1,0:T(8,128)S(1)} %half.4.refs_2_, bf16[2,64,512]{2,1,0:T(8,128)(2,1)S(1)} %collective-permute-done.4.refs_3_, bf16[2,64,512]{2,1,0:T(8,128)(2,1)S(1)} %collective-permute-done.3.refs_4_, ...), custom_call_target="tpu_custom_call" | custom-call | flops 201326592 | bytes 3072000 | tf_op jit(solution)/shard_map/half/pallas_call | solution.py:219
  25.2 0.5 %half.6.refs_2_ = f32[2,64,256]{2,1,0:T(8,128)S(1)} custom-call(s32[3,64]{1,0:T(4,128)S(1)} %pad_add_fusion.refs_0_, bf16[4,8000,128]{2,1,0:T(8,128)(2,1)S(1)} %bitcast.6, f32[2,64,256]{2,1,0:T(8,128)S(1)} %half.5.refs_2_, bf16[2,64,512]{2,1,0:T(8,128)(2,1)S(1)} %collective-permute-done.6.refs_3_, bf16[2,64,512]{2,1,0:T(8,128)(2,1)S(1)} %collective-permute-done.7.refs_4_), custom_call_target="tpu_custom_call" | custom-call | flops 134217728 | bytes 2048000 | tf_op jit(solution)/shard_map/half/pallas_call | solution.py:219
  25.8 0.5 %half.7.refs_0_ = bf16[256,128]{1,0:T(8,128)(2,1)S(1)} custom-call(s32[3,64]{1,0:T(4,128)S(1)} %pad_add_fusion.refs_0_, bf16[4,8000,128]{2,1,0:T(8,128)(2,1)S(1)} %bitcast.7, f32[2,64,256]{2,1,0:T(8,128)S(1)} %half.6.refs_2_, bf16[2,64,512]{2,1,0:T(8,128)(2,1)S(1)} %collective-permute-done.8.refs_3_, bf16[2,64,512]{2,1,0:T(8,128)(2,1)S(1)} %collective-permute-done.9.refs_4_), custom_call_target="tpu_custom_call" | custom-call | flops 134217728 | bytes 2048000 | tf_op jit(solution)/shard_map/half/pallas_call | solution.py:219
  26.3 1.4 %collective-permute-start.10 = (bf16[256,128]{1,0:T(8,128)(2,1)S(1)}, bf16[256,128]{1,0:T(8,128)(2,1)S(1)}, u32[]{:S(2)}, u32[]{:S(2)}) collective-permute-start(bf16[256,128]{1,0:T(8,128)(2,1)S(1)} %half.7.refs_0_), channel_id=1, source_target_pairs={{7,0},{0,1},{1,2},{2,3},{3,4},{4,5},{5,6},{6,7},{15,8},{8,9},{9,10... | collective-permute-start | bytes 196616 | tf_op jit(solution)/shard_map/ppermute | solution.py:147
  27.7 2.6 %collective-permute-start.11 = (bf16[256,128]{1,0:T(8,128)(2,1)S(1)}, bf16[256,128]{1,0:T(8,128)(2,1)S(1)}, u32[]{:S(2)}, u32[]{:S(2)}) collective-permute-start(bf16[256,128]{1,0:T(8,128)(2,1)S(1)} %half.7.refs_0_), channel_id=1, source_target_pairs={{6,0},{7,1},{0,2},{1,3},{2,4},{3,5},{4,6},{5,7},{14,8},{15,9},{8,1... | collective-permute-start | bytes 196616 | tf_op jit(solution)/shard_map/ppermute | solution.py:147
  30.3 1.3 %collective-permute-done.10.refs_1_ = bf16[256,128]{1,0:T(8,128)(2,1)S(1)} collective-permute-done((bf16[256,128]{1,0:T(8,128)(2,1)S(1)}, bf16[256,128]{1,0:T(8,128)(2,1)S(1)}, u32[]{:S(2)}, u32[]{:S(2)}) %collective-permute-start.10) | collective-permute-done | bytes 65568 | tf_op jit(solution)/shard_map/ppermute | solution.py:147
  31.6 0.3 near.1
  32.0 1.4 %collective-permute-done.11.farther_ref = bf16[256,128]{1,0:T(8,128)(2,1)S(1)} collective-permute-done((bf16[256,128]{1,0:T(8,128)(2,1)S(1)}, bf16[256,128]{1,0:T(8,128)(2,1)S(1)}, u32[]{:S(2)}, u32[]{:S(2)}) %collective-permute-start.11) | collective-permute-done | bytes 65568 | tf_op jit(solution)/shard_map/ppermute | solution.py:147
  33.5 1.7 %collective-permute-start.12 = (f32[64,384]{1,0:T(8,128)S(1)}, f32[64,384]{1,0:T(8,128)S(1)}, u32[]{:S(2)}, u32[]{:S(2)}) collective-permute-start(f32[64,384]{1,0:T(8,128)S(1)} %get-tuple-element.24), channel_id=1, source_target_pairs={{0,8},{8,0},{1,9},{9,1},{2,10},{10,2},{3,11},{11,3},{4,12},{12,4},... | collective-permute-start | bytes 294920 | tf_op jit(solution)/shard_map/ppermute | solution.py:166
  35.2 0.9 %collective-permute-done.12 = f32[64,384]{1,0:T(8,128)S(1)} collective-permute-done((f32[64,384]{1,0:T(8,128)S(1)}, f32[64,384]{1,0:T(8,128)S(1)}, u32[]{:S(2)}, u32[]{:S(2)}) %collective-permute-start.12) | collective-permute-done | bytes 98336 | tf_op jit(solution)/shard_map/ppermute | solution.py:166
  36.2 12.2 %all_to_all.5 = f32[16,4,384]{2,1,0:T(4,128)S(1)} all-to-all(f32[16,4,384]{2,1,0:T(4,128)S(1)} %reshape.3), channel_id=1, replica_groups={{160,176,128,144,224,240,192,208,32,48,0,16,96,112,64,80},{161,177,129,..., dimensions={0} | all-to-all | bytes 196608 | tf_op jit(solution)/shard_map/all_to_all | solution.py:276
  48.4 0.6 %reduce_sum.9 = f32[4,384]{1,0:T(4,128)} reduce(f32[16,4,384]{2,1,0:T(4,128)S(1)} %all_to_all.5, f32[]{:T(128)} %constant.5.clone.1), dimensions={0}, to_apply=%region_0.1 | reduce | flops 23040 | bytes 104452 | tf_op jit(solution)/shard_map/reduce_sum | solution.py:283
  (23 shorter events, 0.9 us)
Async XLA Ops:
  0.0 19.1 %copy-start = (bf16[4,128,8000]{1,2,0:T(8,128)(2,1)S(1)}, bf16[4,128,8000]{1,2,0:T(8,128)(2,1)}, u32[]{:S(2)}) copy-start(bf16[4,128,8000]{1,2,0:T(8,128)(2,1)} %param.4) | copy-start | bytes 24576004
  0.0 4.2 %copy-start.2 = (s32[64]{0:T(128)S(1)}, s32[64]{0:T(128)}, u32[]{:S(2)}) copy-start(s32[64]{0:T(128)} %param.7) | copy-start | bytes 772
  0.0 4.2 %copy-start.1 = (s32[1,2,16]{2,1,0:T(2,128)S(1)}, s32[1,2,16]{2,1,0:T(2,128)}, u32[]{:S(2)}) copy-start(s32[1,2,16]{2,1,0:T(2,128)} %param.5) | copy-start | bytes 388
  0.0 4.4 %collective-permute-start = (bf16[250,256]{1,0:T(8,128)(2,1)}, bf16[250,256]{1,0:T(8,128)(2,1)S(1)}, u32[]{:S(2)}, u32[]{:S(2)}) collective-permute-start(bf16[250,256]{1,0:T(8,128)(2,1)} %param.6), channel_id=1, source_target_pairs={{0,8},{8,0},{1,9},{9,1},{2,10},{10,2},{3,11},{11,3},{4,12},{12,4},... | collective-permute-start | bytes 384008 | tf_op jit(solution)/shard_map/ppermute | solution.py:166
  4.9 7.1 %collective-permute-start.1 = (bf16[64,512]{1,0:T(8,128)(2,1)S(1)}, bf16[64,512]{1,0:T(8,128)(2,1)S(1)}, u32[]{:S(2)}, u32[]{:S(2)}) collective-permute-start(bf16[64,512]{1,0:T(8,128)(2,1)S(1)} %pick.1.window_ref), channel_id=1, source_target_pairs={{132,0},{204,8},{128,4},{72,12},{196,64},{12,72},{192,68},{136,76}... | collective-permute-start | bytes 196616 | tf_op jit(solution)/shard_map/ppermute | solution.py:162
  8.9 5.9 %collective-permute-start.2 = (bf16[64,512]{1,0:T(8,128)(2,1)S(1)}, bf16[64,512]{1,0:T(8,128)(2,1)S(1)}, u32[]{:S(2)}, u32[]{:S(2)}) collective-permute-start(bf16[64,512]{1,0:T(8,128)(2,1)S(1)} %pick.1.window_ref), channel_id=1, source_target_pairs={{72,8},{204,12},{136,72},{12,76},{200,136},{76,140},{8,200},{140,2... | collective-permute-start | bytes 196616 | tf_op jit(solution)/shard_map/ppermute | solution.py:162
  14.8 6.4 %collective-permute-start.3 = (bf16[2,64,512]{2,1,0:T(8,128)(2,1)S(1)}, bf16[2,64,512]{2,1,0:T(8,128)(2,1)S(1)}, u32[]{:S(2)}, u32[]{:S(2)}) collective-permute-start(bf16[2,64,512]{2,1,0:T(8,128)(2,1)S(1)} %stack.1.refs_3_), channel_id=1, source_target_pairs={{32,0},{48,16},{0,32},{16,48},{33,1},{49,17},{1,33},{17,49},{34,2}... | collective-permute-start | bytes 393224 | tf_op jit(solution)/shard_map/ppermute | solution.py:147
  17.6 6.0 %collective-permute-start.6 = (bf16[2,64,512]{2,1,0:T(8,128)(2,1)S(1)}, bf16[2,64,512]{2,1,0:T(8,128)(2,1)S(1)}, u32[]{:S(2)}, u32[]{:S(2)}) collective-permute-start(bf16[2,64,512]{2,1,0:T(8,128)(2,1)S(1)} %stack.1.refs_3_), channel_id=1, source_target_pairs={{16,0},{32,16},{48,32},{0,48},{17,1},{33,17},{49,33},{1,49},{18,2}... | collective-permute-start | bytes 393224 | tf_op jit(solution)/shard_map/ppermute | solution.py:147
  18.5 5.9 %collective-permute-start.8 = (bf16[2,64,512]{2,1,0:T(8,128)(2,1)S(1)}, bf16[2,64,512]{2,1,0:T(8,128)(2,1)S(1)}, u32[]{:S(2)}, u32[]{:S(2)}) collective-permute-start(bf16[2,64,512]{2,1,0:T(8,128)(2,1)S(1)} %stack.1.refs_3_), channel_id=1, source_target_pairs={{48,0},{0,16},{16,32},{32,48},{49,1},{1,17},{17,33},{33,49},{50,2}... | collective-permute-start | bytes 393224 | tf_op jit(solution)/shard_map/ppermute | solution.py:147
  19.1 5.4 %collective-permute-start.4 = (bf16[2,64,512]{2,1,0:T(8,128)(2,1)S(1)}, bf16[2,64,512]{2,1,0:T(8,128)(2,1)S(1)}, u32[]{:S(2)}, u32[]{:S(2)}) collective-permute-start(bf16[2,64,512]{2,1,0:T(8,128)(2,1)S(1)} %stack.1.refs_3_), channel_id=1, source_target_pairs={{0,8},{8,0},{1,9},{9,1},{2,10},{10,2},{3,11},{11,3},{4,12},{12,4},... | collective-permute-start | bytes 393224 | tf_op jit(solution)/shard_map/ppermute | solution.py:166
  21.2 3.4 %collective-permute-start.5 = (bf16[2,64,512]{2,1,0:T(8,128)(2,1)S(1)}, bf16[2,64,512]{2,1,0:T(8,128)(2,1)S(1)}, u32[]{:S(2)}, u32[]{:S(2)}) collective-permute-start(bf16[2,64,512]{2,1,0:T(8,128)(2,1)S(1)} %collective-permute-done.3.refs_4_), channel_id=1, source_target_pairs={{0,8},{8,0},{1,9},{9,1},{2,10},{10,2},{3,11},{11,3},{4,12},{12,4},... | collective-permute-start | bytes 393224 | tf_op jit(solution)/shard_map/ppermute | solution.py:166
  23.7 1.6 %collective-permute-start.7 = (bf16[2,64,512]{2,1,0:T(8,128)(2,1)S(1)}, bf16[2,64,512]{2,1,0:T(8,128)(2,1)S(1)}, u32[]{:S(2)}, u32[]{:S(2)}) collective-permute-start(bf16[2,64,512]{2,1,0:T(8,128)(2,1)S(1)} %collective-permute-done.6.refs_3_), channel_id=1, source_target_pairs={{0,8},{8,0},{1,9},{9,1},{2,10},{10,2},{3,11},{11,3},{4,12},{12,4},... | collective-permute-start | bytes 393224 | tf_op jit(solution)/shard_map/ppermute | solution.py:166
  24.4 1.4 %collective-permute-start.9 = (bf16[2,64,512]{2,1,0:T(8,128)(2,1)S(1)}, bf16[2,64,512]{2,1,0:T(8,128)(2,1)S(1)}, u32[]{:S(2)}, u32[]{:S(2)}) collective-permute-start(bf16[2,64,512]{2,1,0:T(8,128)(2,1)S(1)} %collective-permute-done.8.refs_3_), channel_id=1, source_target_pairs={{0,8},{8,0},{1,9},{9,1},{2,10},{10,2},{3,11},{11,3},{4,12},{12,4},... | collective-permute-start | bytes 393224 | tf_op jit(solution)/shard_map/ppermute | solution.py:166
  26.3 5.3 %collective-permute-start.10 = (bf16[256,128]{1,0:T(8,128)(2,1)S(1)}, bf16[256,128]{1,0:T(8,128)(2,1)S(1)}, u32[]{:S(2)}, u32[]{:S(2)}) collective-permute-start(bf16[256,128]{1,0:T(8,128)(2,1)S(1)} %half.7.refs_0_), channel_id=1, source_target_pairs={{7,0},{0,1},{1,2},{2,3},{3,4},{4,5},{5,6},{6,7},{15,8},{8,9},{9,10... | collective-permute-start | bytes 196616 | tf_op jit(solution)/shard_map/ppermute | solution.py:147
  27.7 5.6 %collective-permute-start.11 = (bf16[256,128]{1,0:T(8,128)(2,1)S(1)}, bf16[256,128]{1,0:T(8,128)(2,1)S(1)}, u32[]{:S(2)}, u32[]{:S(2)}) collective-permute-start(bf16[256,128]{1,0:T(8,128)(2,1)S(1)} %half.7.refs_0_), channel_id=1, source_target_pairs={{6,0},{7,1},{0,2},{1,3},{2,4},{3,5},{4,6},{5,7},{14,8},{15,9},{8,1... | collective-permute-start | bytes 196616 | tf_op jit(solution)/shard_map/ppermute | solution.py:147
  33.5 2.7 %collective-permute-start.12 = (f32[64,384]{1,0:T(8,128)S(1)}, f32[64,384]{1,0:T(8,128)S(1)}, u32[]{:S(2)}, u32[]{:S(2)}) collective-permute-start(f32[64,384]{1,0:T(8,128)S(1)} %get-tuple-element.24), channel_id=1, source_target_pairs={{0,8},{8,0},{1,9},{9,1},{2,10},{10,2},{3,11},{11,3},{4,12},{12,4},... | collective-permute-start | bytes 294920 | tf_op jit(solution)/shard_map/ppermute | solution.py:166

commit v6 on v5

--- a/solution.py
+++ b/solution.py
@@ -60,9 +60,9 @@
     out_ref[1] = first_ref[...]
 
 
-def stage_kernel(integrals_ref, total_ref):
+def stage_kernel(integrals_ref, token_ref):
     del integrals_ref
-    total_ref[...] = jnp.zeros_like(total_ref)
+    token_ref[...] = jnp.zeros_like(token_ref)
 
 
 def half_kernel(parts, last, small_ref, integrals_ref, before_ref, *refs):
@@ -73,7 +73,10 @@
     layers, width = lax.axis_size(ZH), lax.axis_size(X)
     near = jnp.where(zl == 0, layers - 1, 1)
     pairs = p_local // 2
-    totals = [before_ref[pair] for pair in range(pairs)]
+    if before_ref.shape[0] == pairs:
+        totals = [before_ref[pair] for pair in range(pairs)]
+    else:
+        totals = [jnp.zeros((batch, 2 * rows), jnp.float32) + before_ref[0:1, 0:1]] * pairs
     masks = small_ref[...].astype(jnp.float32)
     entry = lax.broadcasted_iota(jnp.int32, masks.shape, 1)
     column = lax.broadcasted_iota(jnp.int32, (1, 2 * rows), 1) % rows
@@ -82,7 +85,7 @@
         holder = core if mine else 1 - core
         for slot in range(slots):
             even = 0 if slot == 0 else 2
-            odd = layers - near if slot == 0 else near
+            odd = near if slot == 0 else layers - near
             q = lax.rem(zh + jnp.where(holder == 0, even, odd), layers) * width + x
             offset = lax.rem(COL_BLK * q, ALIGN)
             chosen = jnp.sum(jnp.where(entry == q, masks, 0.0), axis=1, keepdims=True)
@@ -195,15 +198,15 @@
     running = jax.ShapeDtypeStruct((p_local // 2, batch, 2 * r_local), jnp.float32)
     total = pl.pallas_call(
         stage_kernel,
-        out_shape=running,
+        out_shape=jax.ShapeDtypeStruct((8, 128), jnp.float32),
         in_specs=[pl.BlockSpec(memory_space=pl.ANY)],
         out_specs=WHOLE,
         compiler_params=params(52),
         name="stage",
     )(by_column)
     window, total = lax.optimization_barrier((window, total))
-    second = along_z(window, {(1, 0): 2, (1, 1): -2})
-    first = along_z(window, {(0, 0): -3, (0, 1): 3, (1, 0): -1, (1, 1): 1})
+    second = along_z(window, {(1, 0): -1, (1, 1): 1})
+    first = along_z(window, {(0, 0): -3, (0, 1): 3, (1, 0): 2, (1, 1): -2})
     first, window = lax.optimization_barrier((first, window))
     stack = pl.pallas_call(
         stack_kernel,

time: 49.2 us -> 49 us (level); the launches traced: 49 us -> 48.3 us
  blocking collectives: 12.2 us -> 11.2 us
  waiting for transfers between devices: 11.6 us -> 12.6 us
  starting transfers between devices: 20.5 us -> 19.7 us
    ppermute x2, waiting for transfers between devices: 2.81 us -> 4.28 us  [along_z(): return lax.ppermute(block, (ZH, CORE, ZL), route)]
    all_to_all x1, blocking collectives: 12.2 us -> 11.2 us  [per_device(): lax.all_to_all(chip_sum.reshape(chips, rows_dev, BANDS * r_local), (ZH, X...]
    ppermute x2, starting transfers between devices: 7.09 us -> 6.35 us  [along_z(): return lax.ppermute(block, (ZH, CORE, ZL), route)]
    ppermute x5, waiting for transfers between devices: 7.6 us -> 7.02 us  [from_behind(): return lax.ppermute(block, axis, route)]
  transfers between devices with their start and end apart: 13 -> 13, of which waited for: 8 -> 9; matrix products, arithmetic and copies ran while one was open for 2% -> 2% of each run, Pallas kernels for 4% -> 4%
where the time goes in v6:
time: 49 us; the launch traced here: 48.3 us
  starting transfers between devices  19.7 us (40%)
  waiting for transfers between devices  12.6 us (26%)
  blocking collectives  11.2 us (23%)
  Pallas kernels  2.9 us (6%)
  local copies, waits for them, and re-layouts  0.95 us (2%)
  other arithmetic  0.65 us (1%)
    all_to_all x1, blocking collectives, per_device(): lax.all_to_all(chip_sum.reshape(chips, rows_dev, BANDS * r_local), (ZH, X...  11.2 us
    ppermute x5, starting transfers between devices, from_behind(): return lax.ppermute(block, axis, route)  8.32 us
    ppermute x5, waiting for transfers between devices, from_behind(): return lax.ppermute(block, axis, route)  7.02 us
    ppermute x2, starting transfers between devices, along_z(): return lax.ppermute(block, (ZH, CORE, ZL), route)  6.35 us
    ppermute x6, starting transfers between devices, other_core(): return lax.ppermute(block, CORE, [(0, 1), (1, 0)])  5.08 us
    ppermute x2, waiting for transfers between devices, along_z(): return lax.ppermute(block, (ZH, CORE, ZL), route)  4.28 us
    pallas_call x4, Pallas kernels, add_products(): pl.pallas_call(lambda *refs: half_kernel(parts, last, *refs), out_shape=o...  1.97 us
    ppermute x6, waiting for transfers between devices, other_core(): return lax.ppermute(block, CORE, [(0, 1), (1, 0)])  1.31 us
  transfers between devices with their start and end apart: 13, of which 9 were waited for; matrix products, arithmetic and copies ran while one was open for 2% of the time, Pallas kernels for 4%

profile of v6, /device:TPU:1, one launch (start us, length us, event | category | flops | bytes accessed | tf_op | source)
XLA Modules:
  0.0 48.3 jit_solution(9539801234121162142)
XLA Ops:
  0.0 3.2 %collective-permute-start = (bf16[250,256]{1,0:T(8,128)(2,1)}, bf16[250,256]{1,0:T(8,128)(2,1)S(1)}, u32[]{:S(2)}, u32[]{:S(2)}) collective-permute-start(bf16[250,256]{1,0:T(8,128)(2,1)} %param.6), channel_id=1, source_target_pairs={{0,8},{8,0},{1,9},{9,1},{2,10},{10,2},{3,11},{11,3},{4,12},{12,4},... | collective-permute-start | bytes 384008 | tf_op jit(solution)/shard_map/ppermute | solution.py:169
  3.2 0.9 %pad.9.refs_1_ = bf16[256,256]{1,0:T(8,128)(2,1)S(1)} pad(bf16[250,256]{1,0:T(8,128)(2,1)} %param.6, bf16[]{:T(256)} %constant.4.clone.1), padding=0_6x0_0 | pad | bytes 259074 | tf_op jit(solution)/shard_map/jit(_pad)/pad | solution.py:187
  4.4 0.4 pick.1.window_ref
  4.9 4.4 %collective-permute-start.1 = (bf16[64,512]{1,0:T(8,128)(2,1)S(1)}, bf16[64,512]{1,0:T(8,128)(2,1)S(1)}, u32[]{:S(2)}, u32[]{:S(2)}) collective-permute-start(bf16[64,512]{1,0:T(8,128)(2,1)S(1)} %pick.1.window_ref), channel_id=1, source_target_pairs={{132,0},{72,8},{128,4},{204,12},{196,64},{136,72},{192,68},{12,76}... | collective-permute-start | bytes 196616 | tf_op jit(solution)/shard_map/ppermute | solution.py:165
  9.3 1.9 %collective-permute-start.2 = (bf16[64,512]{1,0:T(8,128)(2,1)S(1)}, bf16[64,512]{1,0:T(8,128)(2,1)S(1)}, u32[]{:S(2)}, u32[]{:S(2)}) collective-permute-start(bf16[64,512]{1,0:T(8,128)(2,1)S(1)} %pick.1.window_ref), channel_id=1, source_target_pairs={{204,8},{72,12},{12,72},{136,76},{76,136},{200,140},{140,200},{8,2... | collective-permute-start | bytes 196616 | tf_op jit(solution)/shard_map/ppermute | solution.py:165
  11.3 4.3 %collective-permute-done.2.second_ref = bf16[64,512]{1,0:T(8,128)(2,1)S(1)} collective-permute-done((bf16[64,512]{1,0:T(8,128)(2,1)S(1)}, bf16[64,512]{1,0:T(8,128)(2,1)S(1)}, u32[]{:S(2)}, u32[]{:S(2)}) %collective-permute-start.2) | collective-permute-done | bytes 65568 | tf_op jit(solution)/shard_map/ppermute | solution.py:165
  15.6 2.8 %collective-permute-start.3 = (bf16[2,64,512]{2,1,0:T(8,128)(2,1)S(1)}, bf16[2,64,512]{2,1,0:T(8,128)(2,1)S(1)}, u32[]{:S(2)}, u32[]{:S(2)}) collective-permute-start(bf16[2,64,512]{2,1,0:T(8,128)(2,1)S(1)} %stack.1.refs_3_), channel_id=1, source_target_pairs={{32,0},{48,16},{0,32},{16,48},{33,1},{49,17},{1,33},{17,49},{34,2}... | collective-permute-start | bytes 393224 | tf_op jit(solution)/shard_map/ppermute | solution.py:150
  18.4 0.8 %collective-permute-start.6 = (bf16[2,64,512]{2,1,0:T(8,128)(2,1)S(1)}, bf16[2,64,512]{2,1,0:T(8,128)(2,1)S(1)}, u32[]{:S(2)}, u32[]{:S(2)}) collective-permute-start(bf16[2,64,512]{2,1,0:T(8,128)(2,1)S(1)} %stack.1.refs_3_), channel_id=1, source_target_pairs={{16,0},{32,16},{48,32},{0,48},{17,1},{33,17},{49,33},{1,49},{18,2}... | collective-permute-start | bytes 393224 | tf_op jit(solution)/shard_map/ppermute | solution.py:150
  19.2 0.6 %collective-permute-start.8 = (bf16[2,64,512]{2,1,0:T(8,128)(2,1)S(1)}, bf16[2,64,512]{2,1,0:T(8,128)(2,1)S(1)}, u32[]{:S(2)}, u32[]{:S(2)}) collective-permute-start(bf16[2,64,512]{2,1,0:T(8,128)(2,1)S(1)} %stack.1.refs_3_), channel_id=1, source_target_pairs={{48,0},{0,16},{16,32},{32,48},{49,1},{1,17},{17,33},{33,49},{50,2}... | collective-permute-start | bytes 393224 | tf_op jit(solution)/shard_map/ppermute | solution.py:150
  20.2 2.1 %collective-permute-done.3.refs_4_ = bf16[2,64,512]{2,1,0:T(8,128)(2,1)S(1)} collective-permute-done((bf16[2,64,512]{2,1,0:T(8,128)(2,1)S(1)}, bf16[2,64,512]{2,1,0:T(8,128)(2,1)S(1)}, u32[]{:S(2)}, u32[]{:S(2)}) %collective-permute-start.3) | collective-permute-done | bytes 131104 | tf_op jit(solution)/shard_map/ppermute | solution.py:150
  22.3 1.0 %collective-permute-done.6.refs_3_ = bf16[2,64,512]{2,1,0:T(8,128)(2,1)S(1)} collective-permute-done((bf16[2,64,512]{2,1,0:T(8,128)(2,1)S(1)}, bf16[2,64,512]{2,1,0:T(8,128)(2,1)S(1)}, u32[]{:S(2)}, u32[]{:S(2)}) %collective-permute-start.6) | collective-permute-done | bytes 131104 | tf_op jit(solution)/shard_map/ppermute | solution.py:150
  23.3 1.3 %collective-permute-done.8.refs_3_ = bf16[2,64,512]{2,1,0:T(8,128)(2,1)S(1)} collective-permute-done((bf16[2,64,512]{2,1,0:T(8,128)(2,1)S(1)}, bf16[2,64,512]{2,1,0:T(8,128)(2,1)S(1)}, u32[]{:S(2)}, u32[]{:S(2)}) %collective-permute-start.8) | collective-permute-done | bytes 131104 | tf_op jit(solution)/shard_map/ppermute | solution.py:150
  24.6 0.7 %half.5.refs_2_ = f32[2,64,256]{2,1,0:T(8,128)S(1)} custom-call(s32[3,64]{1,0:T(4,128)S(1)} %pad_add_fusion.refs_0_, bf16[4,8000,128]{2,1,0:T(8,128)(2,1)S(1)} %bitcast.5, f32[2,64,256]{2,1,0:T(8,128)S(1)} %half.4.refs_2_, bf16[2,64,512]{2,1,0:T(8,128)(2,1)S(1)} %collective-permute-done.4.refs_3_, bf16[2,64,512]{2,1,0:T(8,128)(2,1)S(1)} %collective-permute-done.3.refs_4_, ...), custom_call_target="tpu_custom_call" | custom-call | flops 201326592 | bytes 3072000 | tf_op jit(solution)/shard_map/half/pallas_call | solution.py:222
  25.3 0.5 %half.6.refs_2_ = f32[2,64,256]{2,1,0:T(8,128)S(1)} custom-call(s32[3,64]{1,0:T(4,128)S(1)} %pad_add_fusion.refs_0_, bf16[4,8000,128]{2,1,0:T(8,128)(2,1)S(1)} %bitcast.6, f32[2,64,256]{2,1,0:T(8,128)S(1)} %half.5.refs_2_, bf16[2,64,512]{2,1,0:T(8,128)(2,1)S(1)} %collective-permute-done.6.refs_3_, bf16[2,64,512]{2,1,0:T(8,128)(2,1)S(1)} %collective-permute-done.7.refs_4_), custom_call_target="tpu_custom_call" | custom-call | flops 134217728 | bytes 2048000 | tf_op jit(solution)/shard_map/half/pallas_call | solution.py:222
  25.9 0.5 half.7.refs_0_
  26.4 1.4 %collective-permute-start.10 = (bf16[256,128]{1,0:T(8,128)(2,1)S(1)}, bf16[256,128]{1,0:T(8,128)(2,1)S(1)}, u32[]{:S(2)}, u32[]{:S(2)}) collective-permute-start(bf16[256,128]{1,0:T(8,128)(2,1)S(1)} %half.7.refs_0_), channel_id=1, source_target_pairs={{7,0},{0,1},{1,2},{2,3},{3,4},{4,5},{5,6},{6,7},{15,8},{8,9},{9,10... | collective-permute-start | bytes 196616 | tf_op jit(solution)/shard_map/ppermute | solution.py:150
  27.8 2.6 %collective-permute-start.11 = (bf16[256,128]{1,0:T(8,128)(2,1)S(1)}, bf16[256,128]{1,0:T(8,128)(2,1)S(1)}, u32[]{:S(2)}, u32[]{:S(2)}) collective-permute-start(bf16[256,128]{1,0:T(8,128)(2,1)S(1)} %half.7.refs_0_), channel_id=1, source_target_pairs={{6,0},{7,1},{0,2},{1,3},{2,4},{3,5},{4,6},{5,7},{14,8},{15,9},{8,1... | collective-permute-start | bytes 196616 | tf_op jit(solution)/shard_map/ppermute | solution.py:150
  30.4 1.3 %collective-permute-done.10.refs_1_ = bf16[256,128]{1,0:T(8,128)(2,1)S(1)} collective-permute-done((bf16[256,128]{1,0:T(8,128)(2,1)S(1)}, bf16[256,128]{1,0:T(8,128)(2,1)S(1)}, u32[]{:S(2)}, u32[]{:S(2)}) %collective-permute-start.10) | collective-permute-done | bytes 65568 | tf_op jit(solution)/shard_map/ppermute | solution.py:150
  31.7 0.3 near.1
  32.1 1.3 %collective-permute-done.11.farther_ref = bf16[256,128]{1,0:T(8,128)(2,1)S(1)} collective-permute-done((bf16[256,128]{1,0:T(8,128)(2,1)S(1)}, bf16[256,128]{1,0:T(8,128)(2,1)S(1)}, u32[]{:S(2)}, u32[]{:S(2)}) %collective-permute-start.11) | collective-permute-done | bytes 65568 | tf_op jit(solution)/shard_map/ppermute | solution.py:150
  33.6 1.8 %collective-permute-start.12 = (f32[64,384]{1,0:T(8,128)S(1)}, f32[64,384]{1,0:T(8,128)S(1)}, u32[]{:S(2)}, u32[]{:S(2)}) collective-permute-start(f32[64,384]{1,0:T(8,128)S(1)} %get-tuple-element.24), channel_id=1, source_target_pairs={{0,8},{8,0},{1,9},{9,1},{2,10},{10,2},{3,11},{11,3},{4,12},{12,4},... | collective-permute-start | bytes 294920 | tf_op jit(solution)/shard_map/ppermute | solution.py:169
  35.4 0.9 %collective-permute-done.12 = f32[64,384]{1,0:T(8,128)S(1)} collective-permute-done((f32[64,384]{1,0:T(8,128)S(1)}, f32[64,384]{1,0:T(8,128)S(1)}, u32[]{:S(2)}, u32[]{:S(2)}) %collective-permute-start.12) | collective-permute-done | bytes 98336 | tf_op jit(solution)/shard_map/ppermute | solution.py:169
  36.4 11.2 %all_to_all.5 = f32[16,4,384]{2,1,0:T(4,128)S(1)} all-to-all(f32[16,4,384]{2,1,0:T(4,128)S(1)} %reshape.3), channel_id=1, replica_groups={{160,176,128,144,224,240,192,208,32,48,0,16,96,112,64,80},{161,177,129,..., dimensions={0} | all-to-all | bytes 196608 | tf_op jit(solution)/shard_map/all_to_all | solution.py:279
  47.6 0.6 %reduce_sum.9 = f32[4,384]{1,0:T(4,128)} reduce(f32[16,4,384]{2,1,0:T(4,128)S(1)} %all_to_all.5, f32[]{:T(128)} %constant.5.clone.1), dimensions={0}, to_apply=%region_0.1 | reduce | flops 23040 | bytes 104452 | tf_op jit(solution)/shard_map/reduce_sum | solution.py:286
  (23 shorter events, 0.9 us)
Async XLA Ops:
  0.0 19.9 %copy-start = (bf16[4,128,8000]{1,2,0:T(8,128)(2,1)S(1)}, bf16[4,128,8000]{1,2,0:T(8,128)(2,1)}, u32[]{:S(2)}) copy-start(bf16[4,128,8000]{1,2,0:T(8,128)(2,1)} %param.4) | copy-start | bytes 24576004
  0.0 4.2 %copy-start.2 = (s32[64]{0:T(128)S(1)}, s32[64]{0:T(128)}, u32[]{:S(2)}) copy-start(s32[64]{0:T(128)} %param.7) | copy-start | bytes 772
  0.0 4.2 %copy-start.1 = (s32[1,2,16]{2,1,0:T(2,128)S(1)}, s32[1,2,16]{2,1,0:T(2,128)}, u32[]{:S(2)}) copy-start(s32[1,2,16]{2,1,0:T(2,128)} %param.5) | copy-start | bytes 388
  0.0 4.4 %collective-permute-start = (bf16[250,256]{1,0:T(8,128)(2,1)}, bf16[250,256]{1,0:T(8,128)(2,1)S(1)}, u32[]{:S(2)}, u32[]{:S(2)}) collective-permute-start(bf16[250,256]{1,0:T(8,128)(2,1)} %param.6), channel_id=1, source_target_pairs={{0,8},{8,0},{1,9},{9,1},{2,10},{10,2},{3,11},{11,3},{4,12},{12,4},... | collective-permute-start | bytes 384008 | tf_op jit(solution)/shard_map/ppermute | solution.py:169
  4.9 6.4 %collective-permute-start.1 = (bf16[64,512]{1,0:T(8,128)(2,1)S(1)}, bf16[64,512]{1,0:T(8,128)(2,1)S(1)}, u32[]{:S(2)}, u32[]{:S(2)}) collective-permute-start(bf16[64,512]{1,0:T(8,128)(2,1)S(1)} %pick.1.window_ref), channel_id=1, source_target_pairs={{132,0},{72,8},{128,4},{204,12},{196,64},{136,72},{192,68},{12,76}... | collective-permute-start | bytes 196616 | tf_op jit(solution)/shard_map/ppermute | solution.py:165
  9.3 6.2 %collective-permute-start.2 = (bf16[64,512]{1,0:T(8,128)(2,1)S(1)}, bf16[64,512]{1,0:T(8,128)(2,1)S(1)}, u32[]{:S(2)}, u32[]{:S(2)}) collective-permute-start(bf16[64,512]{1,0:T(8,128)(2,1)S(1)} %pick.1.window_ref), channel_id=1, source_target_pairs={{204,8},{72,12},{12,72},{136,76},{76,136},{200,140},{140,200},{8,2... | collective-permute-start | bytes 196616 | tf_op jit(solution)/shard_map/ppermute | solution.py:165
  15.6 6.8 %collective-permute-start.3 = (bf16[2,64,512]{2,1,0:T(8,128)(2,1)S(1)}, bf16[2,64,512]{2,1,0:T(8,128)(2,1)S(1)}, u32[]{:S(2)}, u32[]{:S(2)}) collective-permute-start(bf16[2,64,512]{2,1,0:T(8,128)(2,1)S(1)} %stack.1.refs_3_), channel_id=1, source_target_pairs={{32,0},{48,16},{0,32},{16,48},{33,1},{49,17},{1,33},{17,49},{34,2}... | collective-permute-start | bytes 393224 | tf_op jit(solution)/shard_map/ppermute | solution.py:150
  18.4 4.9 %collective-permute-start.6 = (bf16[2,64,512]{2,1,0:T(8,128)(2,1)S(1)}, bf16[2,64,512]{2,1,0:T(8,128)(2,1)S(1)}, u32[]{:S(2)}, u32[]{:S(2)}) collective-permute-start(bf16[2,64,512]{2,1,0:T(8,128)(2,1)S(1)} %stack.1.refs_3_), channel_id=1, source_target_pairs={{16,0},{32,16},{48,32},{0,48},{17,1},{33,17},{49,33},{1,49},{18,2}... | collective-permute-start | bytes 393224 | tf_op jit(solution)/shard_map/ppermute | solution.py:150
  19.2 5.3 %collective-permute-start.8 = (bf16[2,64,512]{2,1,0:T(8,128)(2,1)S(1)}, bf16[2,64,512]{2,1,0:T(8,128)(2,1)S(1)}, u32[]{:S(2)}, u32[]{:S(2)}) collective-permute-start(bf16[2,64,512]{2,1,0:T(8,128)(2,1)S(1)} %stack.1.refs_3_), channel_id=1, source_target_pairs={{48,0},{0,16},{16,32},{32,48},{49,1},{1,17},{17,33},{33,49},{50,2}... | collective-permute-start | bytes 393224 | tf_op jit(solution)/shard_map/ppermute | solution.py:150
  19.9 4.7 %collective-permute-start.4 = (bf16[2,64,512]{2,1,0:T(8,128)(2,1)S(1)}, bf16[2,64,512]{2,1,0:T(8,128)(2,1)S(1)}, u32[]{:S(2)}, u32[]{:S(2)}) collective-permute-start(bf16[2,64,512]{2,1,0:T(8,128)(2,1)S(1)} %stack.1.refs_3_), channel_id=1, source_target_pairs={{0,8},{8,0},{1,9},{9,1},{2,10},{10,2},{3,11},{11,3},{4,12},{12,4},... | collective-permute-start | bytes 393224 | tf_op jit(solution)/shard_map/ppermute | solution.py:169
  22.3 2.3 %collective-permute-start.5 = (bf16[2,64,512]{2,1,0:T(8,128)(2,1)S(1)}, bf16[2,64,512]{2,1,0:T(8,128)(2,1)S(1)}, u32[]{:S(2)}, u32[]{:S(2)}) collective-permute-start(bf16[2,64,512]{2,1,0:T(8,128)(2,1)S(1)} %collective-permute-done.3.refs_4_), channel_id=1, source_target_pairs={{0,8},{8,0},{1,9},{9,1},{2,10},{10,2},{3,11},{11,3},{4,12},{12,4},... | collective-permute-start | bytes 393224 | tf_op jit(solution)/shard_map/ppermute | solution.py:169
  23.3 2.0 %collective-permute-start.7 = (bf16[2,64,512]{2,1,0:T(8,128)(2,1)S(1)}, bf16[2,64,512]{2,1,0:T(8,128)(2,1)S(1)}, u32[]{:S(2)}, u32[]{:S(2)}) collective-permute-start(bf16[2,64,512]{2,1,0:T(8,128)(2,1)S(1)} %collective-permute-done.6.refs_3_), channel_id=1, source_target_pairs={{0,8},{8,0},{1,9},{9,1},{2,10},{10,2},{3,11},{11,3},{4,12},{12,4},... | collective-permute-start | bytes 393224 | tf_op jit(solution)/shard_map/ppermute | solution.py:169
  24.6 1.3 %collective-permute-start.9 = (bf16[2,64,512]{2,1,0:T(8,128)(2,1)S(1)}, bf16[2,64,512]{2,1,0:T(8,128)(2,1)S(1)}, u32[]{:S(2)}, u32[]{:S(2)}) collective-permute-start(bf16[2,64,512]{2,1,0:T(8,128)(2,1)S(1)} %collective-permute-done.8.refs_3_), channel_id=1, source_target_pairs={{0,8},{8,0},{1,9},{9,1},{2,10},{10,2},{3,11},{11,3},{4,12},{12,4},... | collective-permute-start | bytes 393224 | tf_op jit(solution)/shard_map/ppermute | solution.py:169
  26.4 5.3 %collective-permute-start.10 = (bf16[256,128]{1,0:T(8,128)(2,1)S(1)}, bf16[256,128]{1,0:T(8,128)(2,1)S(1)}, u32[]{:S(2)}, u32[]{:S(2)}) collective-permute-start(bf16[256,128]{1,0:T(8,128)(2,1)S(1)} %half.7.refs_0_), channel_id=1, source_target_pairs={{7,0},{0,1},{1,2},{2,3},{3,4},{4,5},{5,6},{6,7},{15,8},{8,9},{9,10... | collective-permute-start | bytes 196616 | tf_op jit(solution)/shard_map/ppermute | solution.py:150
  27.8 5.6 %collective-permute-start.11 = (bf16[256,128]{1,0:T(8,128)(2,1)S(1)}, bf16[256,128]{1,0:T(8,128)(2,1)S(1)}, u32[]{:S(2)}, u32[]{:S(2)}) collective-permute-start(bf16[256,128]{1,0:T(8,128)(2,1)S(1)} %half.7.refs_0_), channel_id=1, source_target_pairs={{6,0},{7,1},{0,2},{1,3},{2,4},{3,5},{4,6},{5,7},{14,8},{15,9},{8,1... | collective-permute-start | bytes 196616 | tf_op jit(solution)/shard_map/ppermute | solution.py:150
  33.6 2.8 %collective-permute-start.12 = (f32[64,384]{1,0:T(8,128)S(1)}, f32[64,384]{1,0:T(8,128)S(1)}, u32[]{:S(2)}, u32[]{:S(2)}) collective-permute-start(f32[64,384]{1,0:T(8,128)S(1)} %get-tuple-element.24), channel_id=1, source_target_pairs={{0,8},{8,0},{1,9},{9,1},{2,10},{10,2},{3,11},{11,3},{4,12},{12,4},... | collective-permute-start | bytes 294920 | tf_op jit(solution)/shard_map/ppermute | solution.py:169

commit v7 on v6

--- a/solution.py
+++ b/solution.py
@@ -241,9 +241,13 @@
         own = from_behind(stack, X, -distance)
         if distance == 2:
             own, total = lax.optimization_barrier((own, total))
-        parts += [(distance, True), (distance, False)]
-        stacks += [own, other_core(own)]
-        total = add_products(total, parts, stacks, last=distance == 3)
+        if distance == 3:
+            total = add_products(total, [(distance, True)], [own])
+            total = add_products(total, [(distance, False)], [other_core(own)], last=True)
+        else:
+            parts += [(distance, True), (distance, False)]
+            stacks += [own, other_core(own)]
+            total = add_products(total, parts, stacks)
         parts, stacks = [], []
     half = total
 

time: 49 us -> 49.2 us (level)
    pallas_call x4 -> x5, Pallas kernels: 1.97 us -> 2.14 us  [add_products(): pl.pallas_call(lambda *refs: half_kernel(parts, last, *refs), out_shape=o...]
  transfers between devices with their start and end apart: 13 -> 13, of which waited for: 9 -> 8; matrix products, arithmetic and copies ran while one was open for 2% -> 2% of each run, Pallas kernels for 4% -> 4%
where the time goes in v7:
time: 49.2 us; the launch traced here: 48.4 us
  starting transfers between devices  19.8 us (40%)
  waiting for transfers between devices  12.5 us (25%)
  blocking collectives  11.2 us (23%)
  Pallas kernels  3.08 us (6%)
  local copies, waits for them, and re-layouts  0.95 us (2%)
  other arithmetic  0.65 us (1%)
    all_to_all x1, blocking collectives, per_device(): lax.all_to_all(chip_sum.reshape(chips, rows_dev, BANDS * r_local), (ZH, X...  11.2 us
    ppermute x5, starting transfers between devices, from_behind(): return lax.ppermute(block, axis, route)  8.32 us
    ppermute x5, waiting for transfers between devices, from_behind(): return lax.ppermute(block, axis, route)  7.02 us
    ppermute x2, starting transfers between devices, along_z(): return lax.ppermute(block, (ZH, CORE, ZL), route)  6.35 us
    ppermute x6, starting transfers between devices, other_core(): return lax.ppermute(block, CORE, [(0, 1), (1, 0)])  5.16 us
    ppermute x2, waiting for transfers between devices, along_z(): return lax.ppermute(block, (ZH, CORE, ZL), route)  4.28 us
    pallas_call x5, Pallas kernels, add_products(): pl.pallas_call(lambda *refs: half_kernel(parts, last, *refs), out_shape=o...  2.14 us
    ppermute x6, waiting for transfers between devices, other_core(): return lax.ppermute(block, CORE, [(0, 1), (1, 0)])  1.19 us
  transfers between devices with their start and end apart: 13, of which 8 were waited for; matrix products, arithmetic and copies ran while one was open for 2% of the time, Pallas kernels for 4%

profile of v7, /device:TPU:1, one launch (start us, length us, event | category | flops | bytes accessed | tf_op | source)
XLA Modules:
  0.0 48.4 jit_solution(13316670163716756410)
XLA Ops:
  0.0 3.2 %collective-permute-start = (bf16[250,256]{1,0:T(8,128)(2,1)}, bf16[250,256]{1,0:T(8,128)(2,1)S(1)}, u32[]{:S(2)}, u32[]{:S(2)}) collective-permute-start(bf16[250,256]{1,0:T(8,128)(2,1)} %param.6), channel_id=1, source_target_pairs={{0,8},{8,0},{1,9},{9,1},{2,10},{10,2},{3,11},{11,3},{4,12},{12,4},... | collective-permute-start | bytes 384008 | tf_op jit(solution)/shard_map/ppermute | solution.py:169
  3.2 0.9 %pad.9.refs_1_ = bf16[256,256]{1,0:T(8,128)(2,1)S(1)} pad(bf16[250,256]{1,0:T(8,128)(2,1)} %param.6, bf16[]{:T(256)} %constant.4.clone.1), padding=0_6x0_0 | pad | bytes 259074 | tf_op jit(solution)/shard_map/jit(_pad)/pad | solution.py:187
  4.4 0.4 pick.1.window_ref
  4.9 4.4 %collective-permute-start.1 = (bf16[64,512]{1,0:T(8,128)(2,1)S(1)}, bf16[64,512]{1,0:T(8,128)(2,1)S(1)}, u32[]{:S(2)}, u32[]{:S(2)}) collective-permute-start(bf16[64,512]{1,0:T(8,128)(2,1)S(1)} %pick.1.window_ref), channel_id=1, source_target_pairs={{132,0},{72,8},{128,4},{204,12},{196,64},{136,72},{192,68},{12,76}... | collective-permute-start | bytes 196616 | tf_op jit(solution)/shard_map/ppermute | solution.py:165
  9.3 1.9 %collective-permute-start.2 = (bf16[64,512]{1,0:T(8,128)(2,1)S(1)}, bf16[64,512]{1,0:T(8,128)(2,1)S(1)}, u32[]{:S(2)}, u32[]{:S(2)}) collective-permute-start(bf16[64,512]{1,0:T(8,128)(2,1)S(1)} %pick.1.window_ref), channel_id=1, source_target_pairs={{204,8},{72,12},{12,72},{136,76},{76,136},{200,140},{140,200},{8,2... | collective-permute-start | bytes 196616 | tf_op jit(solution)/shard_map/ppermute | solution.py:165
  11.3 4.3 %collective-permute-done.2.second_ref = bf16[64,512]{1,0:T(8,128)(2,1)S(1)} collective-permute-done((bf16[64,512]{1,0:T(8,128)(2,1)S(1)}, bf16[64,512]{1,0:T(8,128)(2,1)S(1)}, u32[]{:S(2)}, u32[]{:S(2)}) %collective-permute-start.2) | collective-permute-done | bytes 65568 | tf_op jit(solution)/shard_map/ppermute | solution.py:165
  15.6 2.8 %collective-permute-start.3 = (bf16[2,64,512]{2,1,0:T(8,128)(2,1)S(1)}, bf16[2,64,512]{2,1,0:T(8,128)(2,1)S(1)}, u32[]{:S(2)}, u32[]{:S(2)}) collective-permute-start(bf16[2,64,512]{2,1,0:T(8,128)(2,1)S(1)} %stack.1.refs_3_), channel_id=1, source_target_pairs={{32,0},{48,16},{0,32},{16,48},{33,1},{49,17},{1,33},{17,49},{34,2}... | collective-permute-start | bytes 393224 | tf_op jit(solution)/shard_map/ppermute | solution.py:150
  18.4 0.8 %collective-permute-start.6 = (bf16[2,64,512]{2,1,0:T(8,128)(2,1)S(1)}, bf16[2,64,512]{2,1,0:T(8,128)(2,1)S(1)}, u32[]{:S(2)}, u32[]{:S(2)}) collective-permute-start(bf16[2,64,512]{2,1,0:T(8,128)(2,1)S(1)} %stack.1.refs_3_), channel_id=1, source_target_pairs={{16,0},{32,16},{48,32},{0,48},{17,1},{33,17},{49,33},{1,49},{18,2}... | collective-permute-start | bytes 393224 | tf_op jit(solution)/shard_map/ppermute | solution.py:150
  19.2 0.6 %collective-permute-start.8 = (bf16[2,64,512]{2,1,0:T(8,128)(2,1)S(1)}, bf16[2,64,512]{2,1,0:T(8,128)(2,1)S(1)}, u32[]{:S(2)}, u32[]{:S(2)}) collective-permute-start(bf16[2,64,512]{2,1,0:T(8,128)(2,1)S(1)} %stack.1.refs_3_), channel_id=1, source_target_pairs={{48,0},{0,16},{16,32},{32,48},{49,1},{1,17},{17,33},{33,49},{50,2}... | collective-permute-start | bytes 393224 | tf_op jit(solution)/shard_map/ppermute | solution.py:150
  20.2 2.1 %collective-permute-done.3.refs_4_ = bf16[2,64,512]{2,1,0:T(8,128)(2,1)S(1)} collective-permute-done((bf16[2,64,512]{2,1,0:T(8,128)(2,1)S(1)}, bf16[2,64,512]{2,1,0:T(8,128)(2,1)S(1)}, u32[]{:S(2)}, u32[]{:S(2)}) %collective-permute-start.3) | collective-permute-done | bytes 131104 | tf_op jit(solution)/shard_map/ppermute | solution.py:150
  22.3 1.0 %collective-permute-done.6.refs_3_ = bf16[2,64,512]{2,1,0:T(8,128)(2,1)S(1)} collective-permute-done((bf16[2,64,512]{2,1,0:T(8,128)(2,1)S(1)}, bf16[2,64,512]{2,1,0:T(8,128)(2,1)S(1)}, u32[]{:S(2)}, u32[]{:S(2)}) %collective-permute-start.6) | collective-permute-done | bytes 131104 | tf_op jit(solution)/shard_map/ppermute | solution.py:150
  23.3 1.3 %collective-permute-done.8.refs_3_ = bf16[2,64,512]{2,1,0:T(8,128)(2,1)S(1)} collective-permute-done((bf16[2,64,512]{2,1,0:T(8,128)(2,1)S(1)}, bf16[2,64,512]{2,1,0:T(8,128)(2,1)S(1)}, u32[]{:S(2)}, u32[]{:S(2)}) %collective-permute-start.8) | collective-permute-done | bytes 131104 | tf_op jit(solution)/shard_map/ppermute | solution.py:150
  24.6 0.7 %half.6.refs_2_ = f32[2,64,256]{2,1,0:T(8,128)S(1)} custom-call(s32[3,64]{1,0:T(4,128)S(1)} %pad_add_fusion.refs_0_, bf16[4,8000,128]{2,1,0:T(8,128)(2,1)S(1)} %bitcast.5, f32[2,64,256]{2,1,0:T(8,128)S(1)} %half.5.refs_2_, bf16[2,64,512]{2,1,0:T(8,128)(2,1)S(1)} %collective-permute-done.4.refs_3_, bf16[2,64,512]{2,1,0:T(8,128)(2,1)S(1)} %collective-permute-done.3.refs_4_, ...), custom_call_target="tpu_custom_call" | custom-call | flops 201326592 | bytes 3072000 | tf_op jit(solution)/shard_map/half/pallas_call | solution.py:222
  25.3 0.5 %half.7.refs_2_ = f32[2,64,256]{2,1,0:T(8,128)S(1)} custom-call(s32[3,64]{1,0:T(4,128)S(1)} %pad_add_fusion.refs_0_, bf16[4,8000,128]{2,1,0:T(8,128)(2,1)S(1)} %bitcast.6, f32[2,64,256]{2,1,0:T(8,128)S(1)} %half.6.refs_2_, bf16[2,64,512]{2,1,0:T(8,128)(2,1)S(1)} %collective-permute-done.6.refs_3_, bf16[2,64,512]{2,1,0:T(8,128)(2,1)S(1)} %collective-permute-done.7.refs_4_), custom_call_target="tpu_custom_call" | custom-call | flops 134217728 | bytes 2048000 | tf_op jit(solution)/shard_map/half/pallas_call | solution.py:222
  25.8 0.3 half.8.refs_2_
  26.5 1.4 %collective-permute-start.10 = (bf16[256,128]{1,0:T(8,128)(2,1)S(1)}, bf16[256,128]{1,0:T(8,128)(2,1)S(1)}, u32[]{:S(2)}, u32[]{:S(2)}) collective-permute-start(bf16[256,128]{1,0:T(8,128)(2,1)S(1)} %half.9.refs_0_), channel_id=1, source_target_pairs={{7,0},{0,1},{1,2},{2,3},{3,4},{4,5},{5,6},{6,7},{15,8},{8,9},{9,10... | collective-permute-start | bytes 196616 | tf_op jit(solution)/shard_map/ppermute | solution.py:150
  27.9 2.6 %collective-permute-start.11 = (bf16[256,128]{1,0:T(8,128)(2,1)S(1)}, bf16[256,128]{1,0:T(8,128)(2,1)S(1)}, u32[]{:S(2)}, u32[]{:S(2)}) collective-permute-start(bf16[256,128]{1,0:T(8,128)(2,1)S(1)} %half.9.refs_0_), channel_id=1, source_target_pairs={{6,0},{7,1},{0,2},{1,3},{2,4},{3,5},{4,6},{5,7},{14,8},{15,9},{8,1... | collective-permute-start | bytes 196616 | tf_op jit(solution)/shard_map/ppermute | solution.py:150
  30.5 1.3 %collective-permute-done.10.refs_1_ = bf16[256,128]{1,0:T(8,128)(2,1)S(1)} collective-permute-done((bf16[256,128]{1,0:T(8,128)(2,1)S(1)}, bf16[256,128]{1,0:T(8,128)(2,1)S(1)}, u32[]{:S(2)}, u32[]{:S(2)}) %collective-permute-start.10) | collective-permute-done | bytes 65568 | tf_op jit(solution)/shard_map/ppermute | solution.py:150
  31.8 0.3 near.1
  32.1 1.3 %collective-permute-done.11.farther_ref = bf16[256,128]{1,0:T(8,128)(2,1)S(1)} collective-permute-done((bf16[256,128]{1,0:T(8,128)(2,1)S(1)}, bf16[256,128]{1,0:T(8,128)(2,1)S(1)}, u32[]{:S(2)}, u32[]{:S(2)}) %collective-permute-start.11) | collective-permute-done | bytes 65568 | tf_op jit(solution)/shard_map/ppermute | solution.py:150
  33.6 1.9 %collective-permute-start.12 = (f32[64,384]{1,0:T(8,128)S(1)}, f32[64,384]{1,0:T(8,128)S(1)}, u32[]{:S(2)}, u32[]{:S(2)}) collective-permute-start(f32[64,384]{1,0:T(8,128)S(1)} %get-tuple-element.24), channel_id=1, source_target_pairs={{0,8},{8,0},{1,9},{9,1},{2,10},{10,2},{3,11},{11,3},{4,12},{12,4},... | collective-permute-start | bytes 294920 | tf_op jit(solution)/shard_map/ppermute | solution.py:169
  35.5 0.9 %collective-permute-done.12 = f32[64,384]{1,0:T(8,128)S(1)} collective-permute-done((f32[64,384]{1,0:T(8,128)S(1)}, f32[64,384]{1,0:T(8,128)S(1)}, u32[]{:S(2)}, u32[]{:S(2)}) %collective-permute-start.12) | collective-permute-done | bytes 98336 | tf_op jit(solution)/shard_map/ppermute | solution.py:169
  36.5 11.2 %all_to_all.5 = f32[16,4,384]{2,1,0:T(4,128)S(1)} all-to-all(f32[16,4,384]{2,1,0:T(4,128)S(1)} %reshape.3), channel_id=1, replica_groups={{160,176,128,144,224,240,192,208,32,48,0,16,96,112,64,80},{161,177,129,..., dimensions={0} | all-to-all | bytes 196608 | tf_op jit(solution)/shard_map/all_to_all | solution.py:283
  47.8 0.6 %reduce_sum.9 = f32[4,384]{1,0:T(4,128)} reduce(f32[16,4,384]{2,1,0:T(4,128)S(1)} %all_to_all.5, f32[]{:T(128)} %constant.5.clone.1), dimensions={0}, to_apply=%region_0.1 | reduce | flops 23040 | bytes 104452 | tf_op jit(solution)/shard_map/reduce_sum | solution.py:290
  (24 shorter events, 1.1 us)
Async XLA Ops:
  0.0 19.9 %copy-start = (bf16[4,128,8000]{1,2,0:T(8,128)(2,1)S(1)}, bf16[4,128,8000]{1,2,0:T(8,128)(2,1)}, u32[]{:S(2)}) copy-start(bf16[4,128,8000]{1,2,0:T(8,128)(2,1)} %param.4) | copy-start | bytes 24576004
  0.0 4.2 %copy-start.2 = (s32[64]{0:T(128)S(1)}, s32[64]{0:T(128)}, u32[]{:S(2)}) copy-start(s32[64]{0:T(128)} %param.7) | copy-start | bytes 772
  0.0 4.2 %copy-start.1 = (s32[1,2,16]{2,1,0:T(2,128)S(1)}, s32[1,2,16]{2,1,0:T(2,128)}, u32[]{:S(2)}) copy-start(s32[1,2,16]{2,1,0:T(2,128)} %param.5) | copy-start | bytes 388
  0.0 4.4 %collective-permute-start = (bf16[250,256]{1,0:T(8,128)(2,1)}, bf16[250,256]{1,0:T(8,128)(2,1)S(1)}, u32[]{:S(2)}, u32[]{:S(2)}) collective-permute-start(bf16[250,256]{1,0:T(8,128)(2,1)} %param.6), channel_id=1, source_target_pairs={{0,8},{8,0},{1,9},{9,1},{2,10},{10,2},{3,11},{11,3},{4,12},{12,4},... | collective-permute-start | bytes 384008 | tf_op jit(solution)/shard_map/ppermute | solution.py:169
  4.9 6.4 %collective-permute-start.1 = (bf16[64,512]{1,0:T(8,128)(2,1)S(1)}, bf16[64,512]{1,0:T(8,128)(2,1)S(1)}, u32[]{:S(2)}, u32[]{:S(2)}) collective-permute-start(bf16[64,512]{1,0:T(8,128)(2,1)S(1)} %pick.1.window_ref), channel_id=1, source_target_pairs={{132,0},{72,8},{128,4},{204,12},{196,64},{136,72},{192,68},{12,76}... | collective-permute-start | bytes 196616 | tf_op jit(solution)/shard_map/ppermute | solution.py:165
  9.3 6.2 %collective-permute-start.2 = (bf16[64,512]{1,0:T(8,128)(2,1)S(1)}, bf16[64,512]{1,0:T(8,128)(2,1)S(1)}, u32[]{:S(2)}, u32[]{:S(2)}) collective-permute-start(bf16[64,512]{1,0:T(8,128)(2,1)S(1)} %pick.1.window_ref), channel_id=1, source_target_pairs={{204,8},{72,12},{12,72},{136,76},{76,136},{200,140},{140,200},{8,2... | collective-permute-start | bytes 196616 | tf_op jit(solution)/shard_map/ppermute | solution.py:165
  15.6 6.8 %collective-permute-start.3 = (bf16[2,64,512]{2,1,0:T(8,128)(2,1)S(1)}, bf16[2,64,512]{2,1,0:T(8,128)(2,1)S(1)}, u32[]{:S(2)}, u32[]{:S(2)}) collective-permute-start(bf16[2,64,512]{2,1,0:T(8,128)(2,1)S(1)} %stack.1.refs_3_), channel_id=1, source_target_pairs={{32,0},{48,16},{0,32},{16,48},{33,1},{49,17},{1,33},{17,49},{34,2}... | collective-permute-start | bytes 393224 | tf_op jit(solution)/shard_map/ppermute | solution.py:150
  18.4 4.9 %collective-permute-start.6 = (bf16[2,64,512]{2,1,0:T(8,128)(2,1)S(1)}, bf16[2,64,512]{2,1,0:T(8,128)(2,1)S(1)}, u32[]{:S(2)}, u32[]{:S(2)}) collective-permute-start(bf16[2,64,512]{2,1,0:T(8,128)(2,1)S(1)} %stack.1.refs_3_), channel_id=1, source_target_pairs={{16,0},{32,16},{48,32},{0,48},{17,1},{33,17},{49,33},{1,49},{18,2}... | collective-permute-start | bytes 393224 | tf_op jit(solution)/shard_map/ppermute | solution.py:150
  19.2 5.3 %collective-permute-start.8 = (bf16[2,64,512]{2,1,0:T(8,128)(2,1)S(1)}, bf16[2,64,512]{2,1,0:T(8,128)(2,1)S(1)}, u32[]{:S(2)}, u32[]{:S(2)}) collective-permute-start(bf16[2,64,512]{2,1,0:T(8,128)(2,1)S(1)} %stack.1.refs_3_), channel_id=1, source_target_pairs={{48,0},{0,16},{16,32},{32,48},{49,1},{1,17},{17,33},{33,49},{50,2}... | collective-permute-start | bytes 393224 | tf_op jit(solution)/shard_map/ppermute | solution.py:150
  19.9 4.7 %collective-permute-start.4 = (bf16[2,64,512]{2,1,0:T(8,128)(2,1)S(1)}, bf16[2,64,512]{2,1,0:T(8,128)(2,1)S(1)}, u32[]{:S(2)}, u32[]{:S(2)}) collective-permute-start(bf16[2,64,512]{2,1,0:T(8,128)(2,1)S(1)} %stack.1.refs_3_), channel_id=1, source_target_pairs={{0,8},{8,0},{1,9},{9,1},{2,10},{10,2},{3,11},{11,3},{4,12},{12,4},... | collective-permute-start | bytes 393224 | tf_op jit(solution)/shard_map/ppermute | solution.py:169
  22.3 2.3 %collective-permute-start.5 = (bf16[2,64,512]{2,1,0:T(8,128)(2,1)S(1)}, bf16[2,64,512]{2,1,0:T(8,128)(2,1)S(1)}, u32[]{:S(2)}, u32[]{:S(2)}) collective-permute-start(bf16[2,64,512]{2,1,0:T(8,128)(2,1)S(1)} %collective-permute-done.3.refs_4_), channel_id=1, source_target_pairs={{0,8},{8,0},{1,9},{9,1},{2,10},{10,2},{3,11},{11,3},{4,12},{12,4},... | collective-permute-start | bytes 393224 | tf_op jit(solution)/shard_map/ppermute | solution.py:169
  23.3 2.0 %collective-permute-start.7 = (bf16[2,64,512]{2,1,0:T(8,128)(2,1)S(1)}, bf16[2,64,512]{2,1,0:T(8,128)(2,1)S(1)}, u32[]{:S(2)}, u32[]{:S(2)}) collective-permute-start(bf16[2,64,512]{2,1,0:T(8,128)(2,1)S(1)} %collective-permute-done.6.refs_3_), channel_id=1, source_target_pairs={{0,8},{8,0},{1,9},{9,1},{2,10},{10,2},{3,11},{11,3},{4,12},{12,4},... | collective-permute-start | bytes 393224 | tf_op jit(solution)/shard_map/ppermute | solution.py:169
  24.6 1.6 %collective-permute-start.9 = (bf16[2,64,512]{2,1,0:T(8,128)(2,1)S(1)}, bf16[2,64,512]{2,1,0:T(8,128)(2,1)S(1)}, u32[]{:S(2)}, u32[]{:S(2)}) collective-permute-start(bf16[2,64,512]{2,1,0:T(8,128)(2,1)S(1)} %collective-permute-done.8.refs_3_), channel_id=1, source_target_pairs={{0,8},{8,0},{1,9},{9,1},{2,10},{10,2},{3,11},{11,3},{4,12},{12,4},... | collective-permute-start | bytes 393224 | tf_op jit(solution)/shard_map/ppermute | solution.py:169
  26.5 5.3 %collective-permute-start.10 = (bf16[256,128]{1,0:T(8,128)(2,1)S(1)}, bf16[256,128]{1,0:T(8,128)(2,1)S(1)}, u32[]{:S(2)}, u32[]{:S(2)}) collective-permute-start(bf16[256,128]{1,0:T(8,128)(2,1)S(1)} %half.9.refs_0_), channel_id=1, source_target_pairs={{7,0},{0,1},{1,2},{2,3},{3,4},{4,5},{5,6},{6,7},{15,8},{8,9},{9,10... | collective-permute-start | bytes 196616 | tf_op jit(solution)/shard_map/ppermute | solution.py:150
  27.9 5.6 %collective-permute-start.11 = (bf16[256,128]{1,0:T(8,128)(2,1)S(1)}, bf16[256,128]{1,0:T(8,128)(2,1)S(1)}, u32[]{:S(2)}, u32[]{:S(2)}) collective-permute-start(bf16[256,128]{1,0:T(8,128)(2,1)S(1)} %half.9.refs_0_), channel_id=1, source_target_pairs={{6,0},{7,1},{0,2},{1,3},{2,4},{3,5},{4,6},{5,7},{14,8},{15,9},{8,1... | collective-permute-start | bytes 196616 | tf_op jit(solution)/shard_map/ppermute | solution.py:150
  33.6 2.9 %collective-permute-start.12 = (f32[64,384]{1,0:T(8,128)S(1)}, f32[64,384]{1,0:T(8,128)S(1)}, u32[]{:S(2)}, u32[]{:S(2)}) collective-permute-start(f32[64,384]{1,0:T(8,128)S(1)} %get-tuple-element.24), channel_id=1, source_target_pairs={{0,8},{8,0},{1,9},{9,1},{2,10},{10,2},{3,11},{11,3},{4,12},{12,4},... | collective-permute-start | bytes 294920 | tf_op jit(solution)/shard_map/ppermute | solution.py:169
